TPU v7x, 32 devices: a whole 2x2x4 slice. The times are simulated.
32 devices in a mesh: depth: 8 (over y, x, core), tile: 4 (over z).
Axes of the slice: x: 2, y: 2, z: 4, core: 2. Of those that a mesh axis runs over, the one named last changes fastest.
Arguments:
- volume: float32 [16, 512, 384], P('depth', 'tile'), may hold values from -6 to 6
- point_spread: float32 [16, 255, 255], P('depth'), may hold values from -0.005859375 to 0.005859375
- measured: float32 [512, 384], P('tile'), may hold values from -6 to 6
Outputs:
- volume_next: float32 [16, 512, 384], P('depth', 'tile')
- residual: float32 [512, 384], P('tile')
All inputs are finite; a program needn't handle non-finite values.
Results may differ from a plain program's by a relative error of at most 0.0003.
Values sent between devices are 32-bit elements; how exact they have to be, the bound alone decides.
No kernel may reach another device: no remote copies, remote signals or barrier semaphores. Data moves between devices by JAX's collectives and lax.ppermute only.
A program may use at most 64 MiB of HBM per device.

v0:
```python
import functools

import jax
import jax.numpy as jnp
import ml_dtypes
import numpy as np
from jax import lax
from jax.experimental import pallas as pl
from jax.experimental.pallas import tpu as pltpu
from jax.sharding import PartitionSpec as P

step_size = 2.0
threshold = 0.5
VMEM = pl.BlockSpec(memory_space=pltpu.VMEM)
PARAMS = pltpu.CompilerParams(vmem_limit_bytes=48 * 1024 * 1024)


def pair(table):
    high = table.astype(ml_dtypes.bfloat16)
    low = (table - high.astype(np.float64)).astype(ml_dtypes.bfloat16)
    return np.stack([high, low])


def tables(row_count, width_count, half_width):
    freq_rows = 3 * row_count
    freq_cols = -(-(width_count + half_width) // 256) * 256
    row_angle = 2.0 * np.pi / freq_rows * (np.arange(freq_rows // 2) + 0.5)
    col_angle = 2.0 * np.pi / freq_cols * (np.arange(freq_cols // 2) + 0.5)

    def rows_at(position):
        phase = row_angle[:, None] * position[None, :]
        return np.concatenate([np.cos(phase), np.sin(phase)], axis=0)

    def cols_at(position):
        phase = position[:, None] * col_angle[None, :]
        return np.concatenate([np.cos(phase), -np.sin(phase)], axis=1)

    scale = 2.0 / (freq_rows * freq_cols)
    cols = np.arange(width_count)
    frame = np.arange(freq_rows)
    row_forward = pair(rows_at(frame))
    col_forward = pair(cols_at(cols))
    row_project = pair(rows_at(frame - row_count + half_width).T * scale)
    col_project = pair(cols_at(cols + half_width).T)
    row_back = pair(rows_at(np.arange(row_count) + row_count - half_width).T * scale)
    col_back = pair(cols_at(cols - half_width).T)
    return row_forward, col_forward, row_project, col_project, row_back, col_back


def split(x):
    high = x.astype(jnp.bfloat16)
    low = (x - high.astype(jnp.float32)).astype(jnp.bfloat16)
    return high, low


def times_table(x, high, low):
    x_high, x_low = split(x)
    return jnp.dot(
        jnp.concatenate([x_high, x_low, x_high], axis=1),
        jnp.concatenate([high, high, low], axis=0),
        preferred_element_type=jnp.float32,
    )


def table_times(high, low, x):
    x_high, x_low = split(x)
    return jnp.dot(
        jnp.concatenate([high, high, low], axis=1),
        jnp.concatenate([x_high, x_low, x_high], axis=0),
        preferred_element_type=jnp.float32,
    )


def row_spectrum(high, low, x):
    q = table_times(high, low, x)
    u, v = q.shape[0] // 2, q.shape[1] // 2
    cr, ci, sr, si = q[:u, :v], q[:u, v:], q[u:, :v], q[u:, v:]
    return cr + si, ci - sr, cr - si, ci + sr


def inverse(high, low, col_high, col_low, spectrum):
    pr, pi, mr, mi = spectrum
    top = jnp.concatenate([pr + mr, pi + mi], axis=1)
    bottom = jnp.concatenate([mi - pi, pr - mr], axis=1)
    mixed = table_times(high, low, jnp.concatenate([top, bottom], axis=0))
    return times_table(mixed, col_high, col_low)


def project_kernel(
    share, volume, point_spread, measured, rf, cf, ri, ci, keep, send, optic, frame, pad
):
    planes, rows, width = volume.shape
    k = point_spread.shape[1]
    kp = pad.shape[0]
    d, t = lax.axis_index("depth"), lax.axis_index("tile")
    tiles = lax.axis_size("tile")
    total = None
    for i in range(planes):
        pad[...] = jnp.zeros_like(pad)
        pad[:k, :k] = point_spread[i]
        h = times_table(pad[...], cf[0, :kp], cf[1, :kp])
        h = row_spectrum(rf[0, :, :kp], rf[1, :, :kp], h)
        for j in range(4):
            optic[i, j] = h[j]
        f = times_table(volume[i], cf[0], cf[1])
        f = row_spectrum(rf[0, :, :rows], rf[1, :, :rows], f)
        term = (
            h[0] * f[0] - h[1] * f[1],
            h[0] * f[1] + h[1] * f[0],
            h[2] * f[2] - h[3] * f[3],
            h[2] * f[3] + h[3] * f[2],
        )
        total = term if total is None else [a + b for a, b in zip(total, term)]
    frame[...] = inverse(ri[0], ri[1], ci[0], ci[1], total)
    up = frame[:rows] * jnp.where(t == 0, 0.0, 1.0)
    own = frame[rows : 2 * rows] - measured[...] * jnp.where(d == 0, 1.0, 0.0)
    down = frame[2 * rows :] * jnp.where(t == tiles - 1, 0.0, 1.0)
    even = d % 2 == 0
    for s, strip in enumerate((up, own, down)):
        for c in range(keep.shape[0]):
            a = strip[2 * c * share : (2 * c + 1) * share]
            b = strip[(2 * c + 1) * share : (2 * c + 2) * share]
            keep[c, s] = jnp.where(even, a, b)
            send[c, s] = jnp.where(even, b, a)


def back_kernel(volume, mine, other, optic, rf, cf, ri, ci, volume_next, residual, frame):
    planes, rows, width = volume.shape
    chips, _, share, _ = mine.shape
    d = lax.axis_index("depth")
    chip, core = d // 2, d % 2
    for m in range(chips):
        c = chip ^ m
        for s in range(3):
            at = s * rows + (2 * c + core) * share
            frame[pl.ds(pl.multiple_of(at, share), share)] = mine[m, s]
            at = s * rows + (2 * c + 1 - core) * share
            frame[pl.ds(pl.multiple_of(at, share), share)] = other[m, s]
    residual[...] = frame[rows : 2 * rows]
    r = times_table(frame[...], cf[0], cf[1])
    r = row_spectrum(rf[0], rf[1], r)
    for i in range(planes):
        h = [optic[i, j] for j in range(4)]
        g = (
            h[0] * r[0] + h[1] * r[1],
            h[0] * r[1] - h[1] * r[0],
            h[2] * r[2] + h[3] * r[3],
            h[2] * r[3] - h[3] * r[2],
        )
        shifted = volume[i] - step_size * inverse(ri[0], ri[1], ci[0], ci[1], g)
        volume_next[i] = jnp.maximum(shifted - threshold, 0.0) + jnp.minimum(
            shifted + threshold, 0.0
        )


def swap(x, axis, mask):
    return lax.ppermute(x, axis, [(i, i ^ mask) for i in range(lax.axis_size(axis))])


def both_ways(pairs):
    return [(a, b) for a, b in pairs] + [(b, a) for a, b in pairs]


def neighbours(parts):
    up, own, down = parts[0], parts[1], parts[2]
    t, n = lax.axis_index("tile"), lax.axis_size("tile")
    for_above, for_below = parts[1:], parts[:2]
    even = t % 2 == 0
    first = both_ways([(i, i + 1) for i in range(0, n - 1, 2)])
    second = both_ways([(i, i + 1) for i in range(1, n - 1, 2)])
    a = lax.ppermute(jnp.where(even, for_above, for_below), "tile", first)
    b = lax.ppermute(jnp.where(even, for_below, for_above), "tile", second)
    lower = t % 4 < 2
    third = both_ways([(i, i + 2) for i in range(n - 2) if i % 4 < 2])
    fourth = both_ways([(i, i + 2) for i in range(n - 2) if i % 4 >= 2])
    c = lax.ppermute(jnp.where(lower, down, up), "tile", third)
    e = jnp.zeros_like(c)
    if fourth:
        e = lax.ppermute(jnp.where(lower, up, down), "tile", fourth)
    from_above = jnp.where(even, a, b)
    from_below = jnp.where(even, b, a)
    far_above = jnp.where(lower, c, e)
    far_below = jnp.where(lower, e, c)
    return jnp.stack(
        [
            from_below[0] + up + far_below,
            own + from_below[1] + from_above[0],
            from_above[1] + down + far_above,
        ]
    )


def per_device(volume, point_spread, measured):
    planes, rows, width = volume.shape
    half_width = (point_spread.shape[1] - 1) // 2
    n = lax.axis_size("depth")
    chips = n // 2
    share = rows // n
    f32 = jnp.float32
    rf, cf, rp, cp, rb, cb = (
        jnp.asarray(x) for x in tables(rows, width, half_width)
    )
    half = (chips, 3, share, width)
    padded = -(-point_spread.shape[1] // 128) * 128
    keep, send, optic = pl.pallas_call(
        functools.partial(project_kernel, share),
        out_shape=[
            jax.ShapeDtypeStruct(half, f32),
            jax.ShapeDtypeStruct(half, f32),
            jax.ShapeDtypeStruct((planes, 4, rf.shape[1] // 2, cf.shape[2] // 2), f32),
        ],
        in_specs=[VMEM] * 7,
        out_specs=[VMEM] * 3,
        scratch_shapes=[
            pltpu.VMEM((3 * rows, width), f32),
            pltpu.VMEM((padded, padded), f32),
        ],
        compiler_params=PARAMS,
        name="project",
    )(volume, point_spread, measured, rf, cf, rp, cp)
    halves = keep + swap(send, "depth", 1)
    chip = lax.axis_index("depth") // 2
    mine = [lax.dynamic_index_in_dim(halves, chip ^ m, 0, False) for m in range(chips)]
    parts = mine[0]
    arrived = [swap(mine[m], "depth", 2 * m) for m in range(1, chips)]
    for x in arrived:
        parts = parts + x
    strips = neighbours(parts)
    gathered = jnp.stack([strips] + [swap(strips, "depth", 2 * m) for m in range(1, chips)])
    other = swap(gathered, "depth", 1)
    volume_next, residual = pl.pallas_call(
        back_kernel,
        out_shape=[
            jax.ShapeDtypeStruct(volume.shape, f32),
            jax.ShapeDtypeStruct(measured.shape, f32),
        ],
        in_specs=[VMEM] * 8,
        out_specs=[VMEM] * 2,
        scratch_shapes=[pltpu.VMEM((3 * rows, width), f32)],
        compiler_params=PARAMS,
        name="back",
    )(volume, gathered, other, optic, rf, cf, rb, cb)
    return volume_next, residual


def solution(mesh):
    placed = (P("depth", "tile", None), P("depth", None, None), P("tile", None))
    return jax.shard_map(
        per_device,
        mesh=mesh,
        in_specs=placed,
        out_specs=(P("depth", "tile", None), P("tile", None)),
        check_vma=False,
    )
```

profile of v0, /device:TPU:0, one launch (start us, length us, event | category | flops | bytes accessed | tf_op | source)
XLA Modules:
  0.0 57.1 jit_solution(11862341887116078869)
XLA Ops:
  0.6 0.0 copy-start
  0.6 1.1 %copy.11.point_spread = f32[2,255,255]{2,1,0:T(8,128)S(1)} copy(f32[2,255,255]{2,0,1:T(2,128)} %param.10) | data formatting | bytes 1040400 | tf_op args[1]
  1.8 0.1 copy-done
  1.9 0.0 copy-start.1
  1.9 1.1 %copy-done.1 = bf16[2,384,384]{2,1,0:T(8,128)(2,1)S(1)} copy-done((bf16[2,384,384]{2,1,0:T(8,128)(2,1)S(1)}, bf16[2,384,384]{2,1,0:T(8,128)(2,1)}, u32[]{:S(2)}) %copy-start.1) | copy-done | bytes 589848
  3.0 0.0 copy-start.3
  3.0 1.0 %copy-done.3 = f32[2,128,384]{2,1,0:T(8,128)S(1)} copy-done((f32[2,128,384]{2,1,0:T(8,128)S(1)}, f32[2,128,384]{2,1,0:T(8,128)}, u32[]{:S(2)}) %copy-start.3) | copy-done | bytes 393240
  4.0 0.0 copy-start.6
  4.0 1.1 %copy-done.6 = bf16[2,512,384]{2,1,0:T(8,128)(2,1)S(1)} copy-done((bf16[2,512,384]{2,1,0:T(8,128)(2,1)S(1)}, bf16[2,512,384]{2,1,0:T(8,128)(2,1)}, u32[]{:S(2)}) %copy-start.6) | copy-done | bytes 786456
  5.1 0.0 copy-start.7
  5.1 1.1 %copy-done.7 = bf16[2,384,384]{2,1,0:T(8,128)(2,1)S(1)} copy-done((bf16[2,384,384]{2,1,0:T(8,128)(2,1)S(1)}, bf16[2,384,384]{2,1,0:T(8,128)(2,1)}, u32[]{:S(2)}) %copy-start.7) | copy-done | bytes 589848
  6.2 0.0 copy-start.10
  6.2 0.9 %copy-done.10 = f32[128,384]{1,0:T(8,128)S(1)} copy-done((f32[128,384]{1,0:T(8,128)S(1)}, f32[128,384]{1,0:T(8,128)}, u32[]{:S(2)}) %copy-start.10) | copy-done | bytes 196632
  7.1 4.8 %project.1 = (f32[4,3,16,384]{3,2,1,0:T(8,128)S(1)}, f32[4,3,16,384]{3,2,1,0:T(8,128)}, f32[2,4,192,256]{3,2,1,0:T(8,128)S(1)}) custom-call(f32[2,128,384]{2,1,0:T(8,128)S(1)} %copy-done.3, f32[2,255,255]{2,1,0:T(8,128)S(1)} %copy.11.point_spread, f32[128,384]{1,0:T(8,128)S(1)} %copy-done.10, bf16[2,384,384]{2,1,0:T(8,128)(2,1)S(1)} %copy-done.1, ...), custom_call_target="tpu_custom_call" | custom-call | tf_op jit(solution)/shard_map/project/pallas_call | solution.py:205
  11.9 0.0 copy-start.8
  11.9 0.7 %copy-done.8 = f32[4,3,16,384]{3,2,1,0:T(8,128)} copy-done((f32[4,3,16,384]{3,2,1,0:T(8,128)}, f32[4,3,16,384]{3,2,1,0:T(8,128)S(1)}, u32[]{:S(2)}) %copy-start.8) | copy-done | bytes 294936
  12.6 0.4 collective-permute-start
  13.1 1.4 %collective-permute-done = f32[4,3,16,384]{3,2,1,0:T(8,128)S(1)} collective-permute-done((f32[4,3,16,384]{3,2,1,0:T(8,128)}, f32[4,3,16,384]{3,2,1,0:T(8,128)S(1)}, u32[]{:S(2)}, u32[]{:S(2)}) %collective-permute-start) | collective-permute-done | bytes 294944 | tf_op jit(solution)/shard_map/ppermute | solution.py:157
  14.5 0.0 copy-start.13
  14.5 0.7 %copy-done.13 = f32[4,3,16,384]{3,2,1,0:T(8,128)} copy-done((f32[4,3,16,384]{3,2,1,0:T(8,128)}, f32[4,3,16,384]{3,2,1,0:T(8,128)S(1)}, u32[]{:S(2)}) %copy-start.13) | copy-done | bytes 294936
  15.2 0.0 copy-start.2
  15.2 0.0 copy-start.4
  15.2 0.0 copy-start.9
  15.2 1.2 %add.60 = f32[4,3,16,384]{3,2,1,0:T(8,128)S(1)} add(f32[4,3,16,384]{3,2,1,0:T(8,128)} %copy-done.8, f32[4,3,16,384]{3,2,1,0:T(8,128)} %copy-done.13) | non-fusion elementwise | flops 73728 | bytes 884736 | tf_op jit(solution)/shard_map/add | solution.py:221
  16.4 0.0 copy-start.11
  16.4 0.7 %copy-done.11 = f32[4,3,16,384]{3,2,1,0:T(8,128)} copy-done((f32[4,3,16,384]{3,2,1,0:T(8,128)}, f32[4,3,16,384]{3,2,1,0:T(8,128)S(1)}, u32[]{:S(2)}) %copy-start.11) | copy-done | bytes 294936
  17.1 0.7 %dynamic-slice_bitcast_fusion.2 = (f32[3,16,384]{2,1,0:T(8,128)}, f32[3,16,384]{2,1,0:T(8,128)}, f32[3,16,384]{2,1,0:T(8,128)}) fusion(f32[4,3,16,384]{3,2,1,0:T(8,128)S(1)} %add.60, s32[]{:T(128)S(6)} %select_n.73, s32[]{:T(128)S(6)} %select_n.75, s32[]{:T(128)S(6)} %select_n.74), kind=kLoop, calls=%fused_computation.7 | loop fusion | bytes 442380 | tf_op jit(solution)/shard_map/jit(dynamic_index_in_dim)/squeeze | solution.py:223
  17.8 2.9 %collective-permute-start.1 = (f32[3,16,384]{2,1,0:T(8,128)}, f32[3,16,384]{2,1,0:T(8,128)}, u32[]{:S(2)}, u32[]{:S(2)}) collective-permute-start(f32[3,16,384]{2,1,0:T(8,128)} %get-tuple-element.8), channel_id=1, source_target_pairs={{0,8},{4,12},{8,0},{12,4},{16,24},{20,28},{24,16},{28,20},{1,9},{5... | collective-permute-start | bytes 221192 | tf_op jit(solution)/shard_map/ppermute | solution.py:157
  20.7 1.5 %collective-permute-start.3 = (f32[3,16,384]{2,1,0:T(8,128)}, f32[3,16,384]{2,1,0:T(8,128)}, u32[]{:S(2)}, u32[]{:S(2)}) collective-permute-start(f32[3,16,384]{2,1,0:T(8,128)} %get-tuple-element.9), channel_id=1, source_target_pairs={{0,24},{4,28},{8,16},{12,20},{16,8},{20,12},{24,0},{28,4},{1,25},{... | collective-permute-start | bytes 221192 | tf_op jit(solution)/shard_map/ppermute | solution.py:157
  22.2 0.0 collective-permute-start.2
  22.2 1.4 %collective-permute-done.1 = f32[3,16,384]{2,1,0:T(8,128)} collective-permute-done((f32[3,16,384]{2,1,0:T(8,128)}, f32[3,16,384]{2,1,0:T(8,128)}, u32[]{:S(2)}, u32[]{:S(2)}) %collective-permute-start.1) | collective-permute-done | bytes 73760 | tf_op jit(solution)/shard_map/ppermute | solution.py:157
  23.5 2.9 %collective-permute-done.3 = f32[3,16,384]{2,1,0:T(8,128)} collective-permute-done((f32[3,16,384]{2,1,0:T(8,128)}, f32[3,16,384]{2,1,0:T(8,128)}, u32[]{:S(2)}, u32[]{:S(2)}) %collective-permute-start.3) | collective-permute-done | bytes 73760 | tf_op jit(solution)/shard_map/ppermute | solution.py:157
  26.5 1.2 %collective-permute-done.2 = f32[3,16,384]{2,1,0:T(8,128)} collective-permute-done((f32[3,16,384]{2,1,0:T(8,128)}, f32[3,16,384]{2,1,0:T(8,128)}, u32[]{:S(2)}, u32[]{:S(2)}) %collective-permute-start.2) | collective-permute-done | bytes 73760 | tf_op jit(solution)/shard_map/ppermute | solution.py:157
  27.6 1.0 %fusion.1 = f32[3,16,384]{2,1,0:T(8,128)S(1)} fusion(f32[3,16,384]{2,1,0:T(8,128)} %collective-permute-done.3, f32[3,16,384]{2,1,0:T(8,128)} %collective-permute-done.2, f32[3,16,384]{2,1,0:T(8,128)} %collective-permute-done.1, f32[4,3,16,384]{3,2,1,0:T(8,128)} %copy-done.11, s32[]{:T(128)S(6)} %select_n.72), kind=kLoop, calls=%fused_computation.4 | loop fusion | flops 55296 | bytes 368644 | tf_op jit(solution)/shard_map/add | solution.py:227
  28.7 0.0 copy-start.12
  28.7 0.6 %copy-done.12 = f32[3,16,384]{2,1,0:T(8,128)} copy-done((f32[3,16,384]{2,1,0:T(8,128)}, f32[3,16,384]{2,1,0:T(8,128)S(1)}, u32[]{:S(2)}) %copy-start.12) | copy-done | bytes 73752
  29.3 0.6 %slice_select_fusion.1 = (f32[2,16,384]{2,1,0:T(8,128)}, f32[2,16,384]{2,1,0:T(8,128)}) fusion(f32[3,16,384]{2,1,0:T(8,128)S(1)} %fusion.1, pred[]{:T(512)S(6)} %eq.6), kind=kLoop, calls=%fused_computation.9 | loop fusion | flops 24576 | bytes 196609 | tf_op jit(solution)/shard_map/jit(_where)/select_n | solution.py:172
  29.9 1.3 %collective-permute-start.4 = (f32[2,16,384]{2,1,0:T(8,128)}, f32[2,16,384]{2,1,0:T(8,128)}, u32[]{:S(2)}, u32[]{:S(2)}) collective-permute-start(f32[2,16,384]{2,1,0:T(8,128)} %get-tuple-element.19), channel_id=1, source_target_pairs={{1,2},{2,1},{5,6},{6,5},{9,10},{10,9},{13,14},{14,13},{17,18},{18,... | collective-permute-start | bytes 147464 | tf_op jit(solution)/shard_map/ppermute | solution.py:172
  31.2 3.9 %collective-permute-start.5 = (f32[2,16,384]{2,1,0:T(8,128)}, f32[2,16,384]{2,1,0:T(8,128)}, u32[]{:S(2)}, u32[]{:S(2)}) collective-permute-start(f32[2,16,384]{2,1,0:T(8,128)} %get-tuple-element.20), channel_id=1, source_target_pairs={{0,1},{2,3},{1,0},{3,2},{4,5},{6,7},{5,4},{7,6},{8,9},{10,11},{9,8... | collective-permute-start | bytes 147464 | tf_op jit(solution)/shard_map/ppermute | solution.py:171
  35.1 0.0 copy-start.5
  35.1 0.0 collective-permute-done.4
  35.1 2.4 %collective-permute-done.5 = f32[2,16,384]{2,1,0:T(8,128)} collective-permute-done((f32[2,16,384]{2,1,0:T(8,128)}, f32[2,16,384]{2,1,0:T(8,128)}, u32[]{:S(2)}, u32[]{:S(2)}) %collective-permute-start.5) | collective-permute-done | bytes 49184 | tf_op jit(solution)/shard_map/ppermute | solution.py:171
  37.4 0.8 %broadcast_select_fusion.1 = (f32[2,16,384]{2,1,0:T(8,128)S(1)}, f32[2,16,384]{2,1,0:T(8,128)S(1)}) fusion(f32[2,16,384]{2,1,0:T(8,128)} %collective-permute-done.4, f32[2,16,384]{2,1,0:T(8,128)} %collective-permute-done.5, pred[]{:T(512)S(6)} %eq.6), kind=kLoop, calls=%fused_computation.22 | loop fusion | flops 24576 | bytes 196609 | tf_op jit(solution)/shard_map/jit(_where)/select_n | solution.py:181
  38.3 0.8 %slice_add_fusion.1 = (f32[1,16,384]{2,1,0:T(8,128)S(1)}, f32[16,384]{1,0:T(8,128)S(1)}) fusion(f32[2,16,384]{2,1,0:T(8,128)S(1)} %get-tuple-element.14, f32[2,16,384]{2,1,0:T(8,128)S(1)} %get-tuple-element.13, f32[3,16,384]{2,1,0:T(8,128)} %copy-done.12, pred[]{:T(512)S(6)} %lt.32), kind=kLoop, calls=%fused_computation.14 | loop fusion | flops 18432 | bytes 172033 | tf_op jit(solution)/shard_map/add | solution.py:187
  39.1 2.0 %collective-permute-start.6 = (f32[16,384]{1,0:T(8,128)S(1)}, f32[16,384]{1,0:T(8,128)S(1)}, u32[]{:S(2)}, u32[]{:S(2)}) collective-permute-start(f32[16,384]{1,0:T(8,128)S(1)} %get-tuple-element.18), channel_id=1, source_target_pairs={{0,2},{1,3},{2,0},{3,1},{4,6},{5,7},{6,4},{7,5},{8,10},{9,11},{10,... | collective-permute-start | bytes 73736 | tf_op jit(solution)/shard_map/ppermute | solution.py:176
  41.0 2.8 %collective-permute-done.6 = f32[16,384]{1,0:T(8,128)S(1)} collective-permute-done((f32[16,384]{1,0:T(8,128)S(1)}, f32[16,384]{1,0:T(8,128)S(1)}, u32[]{:S(2)}, u32[]{:S(2)}) %collective-permute-start.6) | collective-permute-done | bytes 24608 | tf_op jit(solution)/shard_map/ppermute | solution.py:176
  43.8 0.8 %fusion.7 = (f32[1,16,384]{2,1,0:T(8,128)S(1)}, f32[1,16,384]{2,1,0:T(8,128)S(1)}) fusion(f32[2,16,384]{2,1,0:T(8,128)S(1)} %get-tuple-element.13, f32[16,384]{1,0:T(8,128)S(1)} %collective-permute-done.6, f32[3,16,384]{2,1,0:T(8,128)} %copy-done.12, pred[]{:T(512)S(6)} %lt.32, f32[2,16,384]{2,1,0:T(8,128)S(1)} %get-tuple-element.14), kind=kLoop, calls=%fused_computation.19 | loop fusion | flops 36864 | bytes 172033 | tf_op jit(solution)/shard_map/stack | solution.py:184
  44.6 0.7 %collective-permute-start.8 = (f32[3,16,384]{2,1,0:T(8,128)S(1)}, f32[3,16,384]{2,1,0:T(8,128)S(1)}, u32[]{:S(2)}, u32[]{:S(2)}) collective-permute-start(f32[3,16,384]{2,1,0:T(8,128)S(1)} %get-tuple-element.16), channel_id=1, source_target_pairs={{0,16},{4,20},{8,24},{12,28},{16,0},{20,4},{24,8},{28,12},{1,17},{... | collective-permute-start | bytes 221192 | tf_op jit(solution)/shard_map/ppermute | solution.py:157
  45.4 1.3 %collective-permute-start.7 = (f32[3,16,384]{2,1,0:T(8,128)S(1)}, f32[3,16,384]{2,1,0:T(8,128)S(1)}, u32[]{:S(2)}, u32[]{:S(2)}) collective-permute-start(f32[3,16,384]{2,1,0:T(8,128)S(1)} %get-tuple-element.16), channel_id=1, source_target_pairs={{0,8},{4,12},{8,0},{12,4},{16,24},{20,28},{24,16},{28,20},{1,9},{5... | collective-permute-start | bytes 221192 | tf_op jit(solution)/shard_map/ppermute | solution.py:157
  46.7 1.5 %collective-permute-start.9 = (f32[3,16,384]{2,1,0:T(8,128)S(1)}, f32[3,16,384]{2,1,0:T(8,128)S(1)}, u32[]{:S(2)}, u32[]{:S(2)}) collective-permute-start(f32[3,16,384]{2,1,0:T(8,128)S(1)} %get-tuple-element.16), channel_id=1, source_target_pairs={{0,24},{4,28},{8,16},{12,20},{16,8},{20,12},{24,0},{28,4},{1,25},{... | collective-permute-start | bytes 221192 | tf_op jit(solution)/shard_map/ppermute | solution.py:157
  48.2 0.9 %collective-permute-done.8 = f32[3,16,384]{2,1,0:T(8,128)S(1)} collective-permute-done((f32[3,16,384]{2,1,0:T(8,128)S(1)}, f32[3,16,384]{2,1,0:T(8,128)S(1)}, u32[]{:S(2)}, u32[]{:S(2)}) %collective-permute-start.8) | collective-permute-done | bytes 73760 | tf_op jit(solution)/shard_map/ppermute | solution.py:157
  49.1 0.7 %collective-permute-done.7 = f32[3,16,384]{2,1,0:T(8,128)S(1)} collective-permute-done((f32[3,16,384]{2,1,0:T(8,128)S(1)}, f32[3,16,384]{2,1,0:T(8,128)S(1)}, u32[]{:S(2)}, u32[]{:S(2)}) %collective-permute-start.7) | collective-permute-done | bytes 73760 | tf_op jit(solution)/shard_map/ppermute | solution.py:157
  49.7 2.2 %collective-permute-done.9 = f32[3,16,384]{2,1,0:T(8,128)S(1)} collective-permute-done((f32[3,16,384]{2,1,0:T(8,128)S(1)}, f32[3,16,384]{2,1,0:T(8,128)S(1)}, u32[]{:S(2)}, u32[]{:S(2)}) %collective-permute-start.9) | collective-permute-done | bytes 73760 | tf_op jit(solution)/shard_map/ppermute | solution.py:157
  52.0 0.1 collective-permute-start.10
  52.0 1.6 %collective-permute-done.10.other = f32[4,3,16,384]{3,2,1,0:T(8,128)S(1)} collective-permute-done((f32[4,3,16,384]{3,2,1,0:T(8,128)S(1)}, f32[4,3,16,384]{3,2,1,0:T(8,128)S(1)}, u32[]{:S(2)}, u32[]{:S(2)}) %collective-permute-start.10) | collective-permute-done | bytes 294944 | tf_op jit(solution)/shard_map/ppermute | solution.py:157
  53.6 0.0 copy-done.2
  53.6 0.0 copy-done.4
  53.6 0.0 copy-done.9
  53.6 0.0 copy-done.5
  53.6 3.5 %back.1 = (f32[2,128,384]{2,1,0:T(8,128)}, f32[128,384]{1,0:T(8,128)}) custom-call(f32[2,128,384]{2,1,0:T(8,128)S(1)} %copy-done.4, f32[4,3,16,384]{3,2,1,0:T(8,128)S(1)} %pad_maximum_fusion.mine, f32[4,3,16,384]{3,2,1,0:T(8,128)S(1)} %collective-permute-done.10.other, f32[2,4,192,256]{3,2,1,0:T(8,128)S(1)} %get-tuple-element.7.optic, ...), custom_call_target="tpu_custom_call" | custom-call | tf_op jit(solution)/shard_map/back/pallas_call | solution.py:231
  (2 shorter events, 0.0 us)
Async XLA Ops:
  0.6 1.3 %copy-start = (bf16[2,384,512]{2,1,0:T(8,128)(2,1)S(1)}, bf16[2,384,512]{2,1,0:T(8,128)(2,1)}, u32[]{:S(2)}) copy-start(bf16[2,384,512]{2,1,0:T(8,128)(2,1)} %constant.71.clone.cf) | copy-start | bytes 2359300
  1.9 1.1 %copy-start.1 = (bf16[2,384,384]{2,1,0:T(8,128)(2,1)S(1)}, bf16[2,384,384]{2,1,0:T(8,128)(2,1)}, u32[]{:S(2)}) copy-start(bf16[2,384,384]{2,1,0:T(8,128)(2,1)} %constant.70.clone.rf) | copy-start | bytes 1769476
  3.0 1.0 %copy-start.3 = (f32[2,128,384]{2,1,0:T(8,128)S(1)}, f32[2,128,384]{2,1,0:T(8,128)}, u32[]{:S(2)}) copy-start(f32[2,128,384]{2,1,0:T(8,128)} %volume.3) | copy-start | bytes 1179652
  4.0 1.1 %copy-start.6 = (bf16[2,512,384]{2,1,0:T(8,128)(2,1)S(1)}, bf16[2,512,384]{2,1,0:T(8,128)(2,1)}, u32[]{:S(2)}) copy-start(bf16[2,512,384]{2,1,0:T(8,128)(2,1)} %constant.73.clone.ci) | copy-start | bytes 2359300
  5.1 1.1 %copy-start.7 = (bf16[2,384,384]{2,1,0:T(8,128)(2,1)S(1)}, bf16[2,384,384]{2,1,0:T(8,128)(2,1)}, u32[]{:S(2)}) copy-start(bf16[2,384,384]{2,1,0:T(8,128)(2,1)} %constant.72.clone.ri) | copy-start | bytes 1769476
  6.2 0.9 %copy-start.10 = (f32[128,384]{1,0:T(8,128)S(1)}, f32[128,384]{1,0:T(8,128)}, u32[]{:S(2)}) copy-start(f32[128,384]{1,0:T(8,128)} %measured.1) | copy-start | bytes 589828
  11.9 0.7 %copy-start.8 = (f32[4,3,16,384]{3,2,1,0:T(8,128)}, f32[4,3,16,384]{3,2,1,0:T(8,128)S(1)}, u32[]{:S(2)}) copy-start(f32[4,3,16,384]{3,2,1,0:T(8,128)S(1)} %get-tuple-element.5) | copy-start | bytes 884740
  12.6 1.9 %collective-permute-start = (f32[4,3,16,384]{3,2,1,0:T(8,128)}, f32[4,3,16,384]{3,2,1,0:T(8,128)S(1)}, u32[]{:S(2)}, u32[]{:S(2)}) collective-permute-start(f32[4,3,16,384]{3,2,1,0:T(8,128)} %get-tuple-element.6), channel_id=1, source_target_pairs={{0,4},{4,0},{8,12},{12,8},{16,20},{20,16},{24,28},{28,24},{1,5},{5... | collective-permute-start | bytes 884744 | tf_op jit(solution)/shard_map/ppermute | solution.py:157
  14.5 0.7 %copy-start.13 = (f32[4,3,16,384]{3,2,1,0:T(8,128)}, f32[4,3,16,384]{3,2,1,0:T(8,128)S(1)}, u32[]{:S(2)}) copy-start(f32[4,3,16,384]{3,2,1,0:T(8,128)S(1)} %collective-permute-done) | copy-start | bytes 884740
  15.2 38.4 %copy-start.2 = (bf16[2,384,384]{2,1,0:T(8,128)(2,1)S(1)}, bf16[2,384,384]{2,1,0:T(8,128)(2,1)}, u32[]{:S(2)}) copy-start(bf16[2,384,384]{2,1,0:T(8,128)(2,1)} %constant.70.clone.rf) | copy-start | bytes 1769476
  15.2 38.4 %copy-start.4 = (f32[2,128,384]{2,1,0:T(8,128)S(1)}, f32[2,128,384]{2,1,0:T(8,128)}, u32[]{:S(2)}) copy-start(f32[2,128,384]{2,1,0:T(8,128)} %volume.3) | copy-start | bytes 1179652
  15.2 38.4 %copy-start.9 = (bf16[2,128,384]{2,1,0:T(8,128)(2,1)S(1)}, bf16[2,128,384]{2,1,0:T(8,128)(2,1)}, u32[]{:S(2)}) copy-start(bf16[2,128,384]{2,1,0:T(8,128)(2,1)} %constant.74.clone.ri) | copy-start | bytes 589828
  16.4 0.7 %copy-start.11 = (f32[4,3,16,384]{3,2,1,0:T(8,128)}, f32[4,3,16,384]{3,2,1,0:T(8,128)S(1)}, u32[]{:S(2)}) copy-start(f32[4,3,16,384]{3,2,1,0:T(8,128)S(1)} %add.60) | copy-start | bytes 884740
  17.8 5.7 %collective-permute-start.1 = (f32[3,16,384]{2,1,0:T(8,128)}, f32[3,16,384]{2,1,0:T(8,128)}, u32[]{:S(2)}, u32[]{:S(2)}) collective-permute-start(f32[3,16,384]{2,1,0:T(8,128)} %get-tuple-element.8), channel_id=1, source_target_pairs={{0,8},{4,12},{8,0},{12,4},{16,24},{20,28},{24,16},{28,20},{1,9},{5... | collective-permute-start | bytes 221192 | tf_op jit(solution)/shard_map/ppermute | solution.py:157
  20.7 5.8 %collective-permute-start.3 = (f32[3,16,384]{2,1,0:T(8,128)}, f32[3,16,384]{2,1,0:T(8,128)}, u32[]{:S(2)}, u32[]{:S(2)}) collective-permute-start(f32[3,16,384]{2,1,0:T(8,128)} %get-tuple-element.9), channel_id=1, source_target_pairs={{0,24},{4,28},{8,16},{12,20},{16,8},{20,12},{24,0},{28,4},{1,25},{... | collective-permute-start | bytes 221192 | tf_op jit(solution)/shard_map/ppermute | solution.py:157
  22.2 5.5 %collective-permute-start.2 = (f32[3,16,384]{2,1,0:T(8,128)}, f32[3,16,384]{2,1,0:T(8,128)}, u32[]{:S(2)}, u32[]{:S(2)}) collective-permute-start(f32[3,16,384]{2,1,0:T(8,128)} %get-tuple-element.10), channel_id=1, source_target_pairs={{0,16},{4,20},{8,24},{12,28},{16,0},{20,4},{24,8},{28,12},{1,17},{... | collective-permute-start | bytes 221192 | tf_op jit(solution)/shard_map/ppermute | solution.py:157
  28.7 0.6 %copy-start.12 = (f32[3,16,384]{2,1,0:T(8,128)}, f32[3,16,384]{2,1,0:T(8,128)S(1)}, u32[]{:S(2)}) copy-start(f32[3,16,384]{2,1,0:T(8,128)S(1)} %fusion.1) | copy-start | bytes 221188
  29.9 5.1 %collective-permute-start.4 = (f32[2,16,384]{2,1,0:T(8,128)}, f32[2,16,384]{2,1,0:T(8,128)}, u32[]{:S(2)}, u32[]{:S(2)}) collective-permute-start(f32[2,16,384]{2,1,0:T(8,128)} %get-tuple-element.19), channel_id=1, source_target_pairs={{1,2},{2,1},{5,6},{6,5},{9,10},{10,9},{13,14},{14,13},{17,18},{18,... | collective-permute-start | bytes 147464 | tf_op jit(solution)/shard_map/ppermute | solution.py:172
  31.2 6.2 %collective-permute-start.5 = (f32[2,16,384]{2,1,0:T(8,128)}, f32[2,16,384]{2,1,0:T(8,128)}, u32[]{:S(2)}, u32[]{:S(2)}) collective-permute-start(f32[2,16,384]{2,1,0:T(8,128)} %get-tuple-element.20), channel_id=1, source_target_pairs={{0,1},{2,3},{1,0},{3,2},{4,5},{6,7},{5,4},{7,6},{8,9},{10,11},{9,8... | collective-permute-start | bytes 147464 | tf_op jit(solution)/shard_map/ppermute | solution.py:171
  35.1 18.6 %copy-start.5 = (bf16[2,512,384]{2,1,0:T(8,128)(2,1)S(1)}, bf16[2,512,384]{2,1,0:T(8,128)(2,1)}, u32[]{:S(2)}) copy-start(bf16[2,512,384]{2,1,0:T(8,128)(2,1)} %constant.75.clone.ci) | copy-start | bytes 2359300
  39.1 4.8 %collective-permute-start.6 = (f32[16,384]{1,0:T(8,128)S(1)}, f32[16,384]{1,0:T(8,128)S(1)}, u32[]{:S(2)}, u32[]{:S(2)}) collective-permute-start(f32[16,384]{1,0:T(8,128)S(1)} %get-tuple-element.18), channel_id=1, source_target_pairs={{0,2},{1,3},{2,0},{3,1},{4,6},{5,7},{6,4},{7,5},{8,10},{9,11},{10,... | collective-permute-start | bytes 73736 | tf_op jit(solution)/shard_map/ppermute | solution.py:176
  44.6 4.4 %collective-permute-start.8 = (f32[3,16,384]{2,1,0:T(8,128)S(1)}, f32[3,16,384]{2,1,0:T(8,128)S(1)}, u32[]{:S(2)}, u32[]{:S(2)}) collective-permute-start(f32[3,16,384]{2,1,0:T(8,128)S(1)} %get-tuple-element.16), channel_id=1, source_target_pairs={{0,16},{4,20},{8,24},{12,28},{16,0},{20,4},{24,8},{28,12},{1,17},{... | collective-permute-start | bytes 221192 | tf_op jit(solution)/shard_map/ppermute | solution.py:157
  45.4 4.4 %collective-permute-start.7 = (f32[3,16,384]{2,1,0:T(8,128)S(1)}, f32[3,16,384]{2,1,0:T(8,128)S(1)}, u32[]{:S(2)}, u32[]{:S(2)}) collective-permute-start(f32[3,16,384]{2,1,0:T(8,128)S(1)} %get-tuple-element.16), channel_id=1, source_target_pairs={{0,8},{4,12},{8,0},{12,4},{16,24},{20,28},{24,16},{28,20},{1,9},{5... | collective-permute-start | bytes 221192 | tf_op jit(solution)/shard_map/ppermute | solution.py:157
  46.7 5.3 %collective-permute-start.9 = (f32[3,16,384]{2,1,0:T(8,128)S(1)}, f32[3,16,384]{2,1,0:T(8,128)S(1)}, u32[]{:S(2)}, u32[]{:S(2)}) collective-permute-start(f32[3,16,384]{2,1,0:T(8,128)S(1)} %get-tuple-element.16), channel_id=1, source_target_pairs={{0,24},{4,28},{8,16},{12,20},{16,8},{20,12},{24,0},{28,4},{1,25},{... | collective-permute-start | bytes 221192 | tf_op jit(solution)/shard_map/ppermute | solution.py:157
  52.0 1.6 %collective-permute-start.10 = (f32[4,3,16,384]{3,2,1,0:T(8,128)S(1)}, f32[4,3,16,384]{3,2,1,0:T(8,128)S(1)}, u32[]{:S(2)}, u32[]{:S(2)}) collective-permute-start(f32[4,3,16,384]{3,2,1,0:T(8,128)S(1)} %pad_maximum_fusion.mine), channel_id=1, source_target_pairs={{0,4},{4,0},{8,12},{12,8},{16,20},{20,16},{24,28},{28,24},{1,5},{5... | collective-permute-start | bytes 884744 | tf_op jit(solution)/shard_map/ppermute | solution.py:157
where the time goes:
time: 57.7 us; the launch traced here: 57.1 us
  waiting for transfers between devices  17.4 us (30%)
  starting transfers between devices  15.5 us (27%)
  local copies, waits for them, and re-layouts  9.92 us (17%)
  Pallas kernels  8.29 us (14%)
  other arithmetic  5.25 us (9%)
  between operations  0.72 us (1%)
    ppermute x8, waiting for transfers between devices, swap(): lax.ppermute(x, axis, [(i, i ^ mask) for i in range(lax.axis_size(axis))])  12.2 us
    unnamed x29, local copies, waits for them, and re-layouts  9.23 us
    ppermute x8, starting transfers between devices, swap(): lax.ppermute(x, axis, [(i, i ^ mask) for i in range(lax.axis_size(axis))])  8.45 us
    pallas_call x1, Pallas kernels, per_device(): pl.pallas_call(functools.partial(project_kernel, share), out_shape=[jax.S...  4.81 us
    ppermute x1, starting transfers between devices, neighbours(): a = lax.ppermute(jnp.where(even, for_above, for_below), 'tile', first)  3.86 us
    pallas_call x1, Pallas kernels, per_device(): pl.pallas_call(back_kernel, out_shape=[jax.ShapeDtypeStruct(volume.shape,...  3.48 us
    ppermute x1, waiting for transfers between devices, neighbours(): c = lax.ppermute(jnp.where(lower, down, up), 'tile', third)  2.82 us
    ppermute x1, waiting for transfers between devices, neighbours(): a = lax.ppermute(jnp.where(even, for_above, for_below), 'tile', first)  2.38 us
  transfers between devices with their start and end apart: 11, of which 10 were waited for; matrix products, arithmetic and copies ran while one was open for 0% of the time, Pallas kernels for 0%

commit v1 on v0

--- a/solution.py
+++ b/solution.py
@@ -12,7 +12,8 @@
 step_size = 2.0
 threshold = 0.5
 VMEM = pl.BlockSpec(memory_space=pltpu.VMEM)
-PARAMS = pltpu.CompilerParams(vmem_limit_bytes=48 * 1024 * 1024)
+PARAMS = pltpu.CompilerParams(vmem_limit_bytes=24 * 1024 * 1024)
+SMALL = pltpu.CompilerParams(vmem_limit_bytes=4 * 1024 * 1024)
 
 
 def pair(table):
@@ -87,23 +88,61 @@
 
 
 def project_kernel(
-    share, volume, point_spread, measured, rf, cf, ri, ci, keep, send, optic, frame, pad
+    share,
+    volume_h,
+    point_spread_h,
+    measured_h,
+    rf_h,
+    cf_h,
+    ri_h,
+    ci_h,
+    keep,
+    send,
+    optic,
+    volume,
+    point_spread,
+    measured,
+    rf,
+    cf,
+    ri,
+    ci,
+    frame,
+    pad,
+    arrived,
 ):
+    moves = {}
+    order = (
+        ("spread", point_spread_h, point_spread),
+        ("cf", cf_h, cf),
+        ("rf", rf_h, rf),
+        ("volume", volume_h, volume),
+        ("ri", ri_h, ri),
+        ("ci", ci_h, ci),
+        ("measured", measured_h, measured),
+    )
+    for i, (name, source, target) in enumerate(order):
+        moves[name] = pltpu.make_async_copy(source, target, arrived.at[i])
+        moves[name].start()
     planes, rows, width = volume.shape
-    k = point_spread.shape[1]
-    kp = pad.shape[0]
+    k = point_spread.shape[0]
+    kp = pad.shape[1]
     d, t = lax.axis_index("depth"), lax.axis_index("tile")
     tiles = lax.axis_size("tile")
+    pad[...] = jnp.zeros_like(pad)
+    moves["spread"].wait()
+    for i in range(planes):
+        pad[i, :k, :k] = point_spread[:, i, :]
+    moves["cf"].wait()
+    spread = [times_table(pad[i], cf[0, :kp], cf[1, :kp]) for i in range(planes)]
+    moves["volume"].wait()
+    image = [times_table(volume[i], cf[0], cf[1]) for i in range(planes)]
+    moves["rf"].wait()
     total = None
     for i in range(planes):
-        pad[...] = jnp.zeros_like(pad)
-        pad[:k, :k] = point_spread[i]
-        h = times_table(pad[...], cf[0, :kp], cf[1, :kp])
-        h = row_spectrum(rf[0, :, :kp], rf[1, :, :kp], h)
+        h = row_spectrum(rf[0, :, :kp], rf[1, :, :kp], spread[i])
         for j in range(4):
             optic[i, j] = h[j]
-        f = times_table(volume[i], cf[0], cf[1])
-        f = row_spectrum(rf[0, :, :rows], rf[1, :, :rows], f)
+        f = row_spectrum(rf[0, :, :rows], rf[1, :, :rows], image[i])
         term = (
             h[0] * f[0] - h[1] * f[1],
             h[0] * f[1] + h[1] * f[0],
@@ -111,7 +150,10 @@
             h[2] * f[3] + h[3] * f[2],
         )
         total = term if total is None else [a + b for a, b in zip(total, term)]
+    moves["ri"].wait()
+    moves["ci"].wait()
     frame[...] = inverse(ri[0], ri[1], ci[0], ci[1], total)
+    moves["measured"].wait()
     up = frame[:rows] * jnp.where(t == 0, 0.0, 1.0)
     own = frame[rows : 2 * rows] - measured[...] * jnp.where(d == 0, 1.0, 0.0)
     down = frame[2 * rows :] * jnp.where(t == tiles - 1, 0.0, 1.0)
@@ -122,6 +164,44 @@
             b = strip[(2 * c + 1) * share : (2 * c + 2) * share]
             keep[c, s] = jnp.where(even, a, b)
             send[c, s] = jnp.where(even, b, a)
+
+
+def first_sum_kernel(keep, received, *outs):
+    chip = lax.axis_index("depth") // 2
+    for m, out in enumerate(outs):
+        out[...] = keep[chip ^ m] + received[chip ^ m]
+
+
+def second_sum_kernel(fourth, own, *refs):
+    ins, outs = refs[: len(refs) - (4 + fourth)], refs[len(refs) - (4 + fourth) :]
+    t = lax.axis_index("tile")
+    even, lower = t % 2 == 0, t % 4 < 2
+    parts = own[...]
+    for x in ins:
+        parts = parts + x[...]
+    outs[0][...] = parts
+    outs[1][...] = jnp.where(even, parts[1:], parts[:2])
+    outs[2][...] = jnp.where(even, parts[:2], parts[1:])
+    outs[3][...] = jnp.where(lower, parts[2], parts[0])
+    if fourth:
+        outs[4][...] = jnp.where(lower, parts[0], parts[2])
+
+
+def third_sum_kernel(parts, a, b, c, *refs):
+    strips = refs[-1]
+    t = lax.axis_index("tile")
+    even, lower = t % 2 == 0, t % 4 < 2
+    e = refs[0][...] if len(refs) > 1 else jnp.zeros_like(c)
+    from_above = jnp.where(even, a[...], b[...])
+    from_below = jnp.where(even, b[...], a[...])
+    strips[0] = from_below[0] + parts[0] + jnp.where(lower, e, c[...])
+    strips[1] = parts[1] + from_below[1] + from_above[0]
+    strips[2] = from_above[1] + parts[2] + jnp.where(lower, c[...], e)
+
+
+def stack_kernel(*refs):
+    for m, x in enumerate(refs[:-1]):
+        refs[-1][m] = x[...]
 
 
 def back_kernel(volume, mine, other, optic, rf, cf, ri, ci, volume_next, residual, frame):
@@ -161,39 +241,22 @@
     return [(a, b) for a, b in pairs] + [(b, a) for a, b in pairs]
 
 
-def neighbours(parts):
-    up, own, down = parts[0], parts[1], parts[2]
-    t, n = lax.axis_index("tile"), lax.axis_size("tile")
-    for_above, for_below = parts[1:], parts[:2]
-    even = t % 2 == 0
-    first = both_ways([(i, i + 1) for i in range(0, n - 1, 2)])
-    second = both_ways([(i, i + 1) for i in range(1, n - 1, 2)])
-    a = lax.ppermute(jnp.where(even, for_above, for_below), "tile", first)
-    b = lax.ppermute(jnp.where(even, for_below, for_above), "tile", second)
-    lower = t % 4 < 2
-    third = both_ways([(i, i + 2) for i in range(n - 2) if i % 4 < 2])
-    fourth = both_ways([(i, i + 2) for i in range(n - 2) if i % 4 >= 2])
-    c = lax.ppermute(jnp.where(lower, down, up), "tile", third)
-    e = jnp.zeros_like(c)
-    if fourth:
-        e = lax.ppermute(jnp.where(lower, up, down), "tile", fourth)
-    from_above = jnp.where(even, a, b)
-    from_below = jnp.where(even, b, a)
-    far_above = jnp.where(lower, c, e)
-    far_below = jnp.where(lower, e, c)
-    return jnp.stack(
-        [
-            from_below[0] + up + far_below,
-            own + from_below[1] + from_above[0],
-            from_above[1] + down + far_above,
-        ]
-    )
+def local(kernel, name, outs, *args):
+    return pl.pallas_call(
+        kernel,
+        out_shape=[pltpu.VMEM(x, jnp.float32) for x in outs],
+        in_specs=[VMEM] * len(args),
+        out_specs=[VMEM] * len(outs),
+        compiler_params=SMALL,
+        name=name,
+    )(*args)
 
 
 def per_device(volume, point_spread, measured):
     planes, rows, width = volume.shape
     half_width = (point_spread.shape[1] - 1) // 2
     n = lax.axis_size("depth")
+    tiles = lax.axis_size("tile")
     chips = n // 2
     share = rows // n
     f32 = jnp.float32
@@ -201,32 +264,50 @@
         jnp.asarray(x) for x in tables(rows, width, half_width)
     )
     half = (chips, 3, share, width)
-    padded = -(-point_spread.shape[1] // 128) * 128
+    piece = (3, share, width)
+    kp = -(-point_spread.shape[1] // 128) * 128
+    spread = jnp.transpose(point_spread, (1, 0, 2))
+    operands = (volume, spread, measured, rf, cf, rp, cp)
     keep, send, optic = pl.pallas_call(
         functools.partial(project_kernel, share),
         out_shape=[
-            jax.ShapeDtypeStruct(half, f32),
-            jax.ShapeDtypeStruct(half, f32),
-            jax.ShapeDtypeStruct((planes, 4, rf.shape[1] // 2, cf.shape[2] // 2), f32),
+            pltpu.VMEM(half, f32),
+            pltpu.VMEM(half, f32),
+            pltpu.VMEM((planes, 4, rf.shape[1] // 2, cf.shape[2] // 2), f32),
         ],
-        in_specs=[VMEM] * 7,
+        in_specs=[pl.BlockSpec(memory_space=pltpu.HBM)] * 7,
         out_specs=[VMEM] * 3,
-        scratch_shapes=[
+        scratch_shapes=[pltpu.VMEM(x.shape, x.dtype) for x in operands]
+        + [
             pltpu.VMEM((3 * rows, width), f32),
-            pltpu.VMEM((padded, padded), f32),
+            pltpu.VMEM((planes, kp, kp), f32),
+            pltpu.SemaphoreType.DMA((7,)),
         ],
         compiler_params=PARAMS,
         name="project",
-    )(volume, point_spread, measured, rf, cf, rp, cp)
-    halves = keep + swap(send, "depth", 1)
-    chip = lax.axis_index("depth") // 2
-    mine = [lax.dynamic_index_in_dim(halves, chip ^ m, 0, False) for m in range(chips)]
-    parts = mine[0]
+    )(*[pltpu.with_memory_space_constraint(x, pltpu.HBM) for x in operands])
+    received = swap(send, "depth", 1)
+    mine = local(first_sum_kernel, "first_sum", [piece] * chips, keep, received)
     arrived = [swap(mine[m], "depth", 2 * m) for m in range(1, chips)]
-    for x in arrived:
-        parts = parts + x
-    strips = neighbours(parts)
-    gathered = jnp.stack([strips] + [swap(strips, "depth", 2 * m) for m in range(1, chips)])
+    pairs = [
+        [(i, i + 1) for i in range(0, tiles - 1, 2)],
+        [(i, i + 1) for i in range(1, tiles - 1, 2)],
+        [(i, i + 2) for i in range(tiles - 2) if i % 4 < 2],
+        [(i, i + 2) for i in range(tiles - 2) if i % 4 >= 2],
+    ]
+    fourth = int(bool(pairs[3]))
+    edge = (2, share, width)
+    parts, *sends = local(
+        functools.partial(second_sum_kernel, fourth),
+        "second_sum",
+        [piece, edge, edge] + [piece[1:]] * (1 + fourth),
+        mine[0],
+        *arrived,
+    )
+    arrived = [lax.ppermute(x, "tile", both_ways(p)) for x, p in zip(sends, pairs)]
+    (strips,) = local(third_sum_kernel, "third_sum", [piece], parts, *arrived)
+    arrived = [swap(strips, "depth", 2 * m) for m in range(1, chips)]
+    (gathered,) = local(stack_kernel, "stack", [half], strips, *arrived)
     other = swap(gathered, "depth", 1)
     volume_next, residual = pl.pallas_call(
         back_kernel,

time: 57.7 us -> 38.1 us (0.66)
  local copies, waits for them, and re-layouts: 9.92 us -> 0.03 us
  other arithmetic: 5.25 us -> 0 us
  waiting for transfers between devices: 17.4 us -> 13.4 us
  starting transfers between devices: 15.5 us -> 14.8 us
  Pallas kernels: 8.29 us -> 8.94 us
    unnamed x29 -> x10, local copies, waits for them, and re-layouts: 9.23 us -> 0.03 us
    add x3 -> x0, other arithmetic: 2.97 us -> none  [the longest x1 1.18 us: per_device(): halves = keep + swap(send, 'depth', 1)]
    ppermute x3, waiting for transfers between devices: 5.2 us -> 2.41 us  [per_device(): lax.ppermute(x, 'tile', both_ways(p))]
    select_n x2 -> x0, other arithmetic: 1.47 us -> none  [the longest x1 0.83 us: neighbours(): from_below = jnp.where(even, b, a)]
    ppermute x8, waiting for transfers between devices: 12.2 us -> 11 us  [swap(): lax.ppermute(x, axis, [(i, i ^ mask) for i in range(lax.axis_size(axis))])]
    ppermute x3, starting transfers between devices: 7.09 us -> 6.21 us  [per_device(): lax.ppermute(x, 'tile', both_ways(p))]
    another operation x3 -> x0, other arithmetic: 0.81 us -> none  [the longest x1 0.77 us: neighbours(): jnp.stack([from_below[0] + up + far_below, own + from_below[1] + from_abo...]
    squeeze x1 -> x0, local copies, waits for them, and re-layouts: 0.69 us -> none  [per_device(): lax.dynamic_index_in_dim(halves, chip ^ m, 0, False)]
  transfers between devices with their start and end apart: 11 -> 11, of which waited for: 10 -> 9; matrix products, arithmetic and copies ran while one was open for 0% -> 0% of each run, Pallas kernels for 0% -> 0%
where the time goes in v1:
time: 38.1 us; the launch traced here: 37.9 us
  starting transfers between devices  14.8 us (39%)
  waiting for transfers between devices  13.4 us (35%)
  Pallas kernels  8.94 us (23%)
  between operations  0.74 us (2%)
    ppermute x8, waiting for transfers between devices, swap(): lax.ppermute(x, axis, [(i, i ^ mask) for i in range(lax.axis_size(axis))])  11 us
    ppermute x8, starting transfers between devices, swap(): lax.ppermute(x, axis, [(i, i ^ mask) for i in range(lax.axis_size(axis))])  8.6 us
    ppermute x3, starting transfers between devices, per_device(): lax.ppermute(x, 'tile', both_ways(p))  6.21 us
    pallas_call x1, Pallas kernels, per_device(): pl.pallas_call(functools.partial(project_kernel, share), out_shape=[pltpu...  5.35 us
    pallas_call x1, Pallas kernels, per_device(): pl.pallas_call(back_kernel, out_shape=[jax.ShapeDtypeStruct(volume.shape,...  3.48 us
    ppermute x3, waiting for transfers between devices, per_device(): lax.ppermute(x, 'tile', both_ways(p))  2.41 us
  transfers between devices with their start and end apart: 11, of which 9 were waited for; matrix products, arithmetic and copies ran while one was open for 0% of the time, Pallas kernels for 0%

profile of v1, /device:TPU:0, one launch (start us, length us, event | category | flops | bytes accessed | tf_op | source)
XLA Modules:
  0.0 37.9 jit_solution(12303369599004978337)
XLA Ops:
  0.6 0.0 copy-start.2
  0.6 0.0 copy-start.3
  0.7 5.4 %project.1 = (f32[4,3,16,384]{3,2,1,0:T(8,128)S(1)}, f32[4,3,16,384]{3,2,1,0:T(8,128)S(1)}, f32[2,4,192,256]{3,2,1,0:T(8,128)S(1)}) custom-call(f32[2,128,384]{2,1,0:T(8,128)} %volume.1, f32[255,2,255]{2,1,0:T(2,128)} %bitcast.1, f32[128,384]{1,0:T(8,128)} %measured_h.1, bf16[2,384,384]{2,1,0:T(8,128)(2,1)} %constant.12.clone.rf_h.rf, ...), custom_call_target="tpu_custom_call" | custom-call | tf_op jit(solution)/shard_map/project/pallas_call | solution.py:271
  6.0 0.0 copy-start
  6.0 0.0 copy-start.1
  6.0 0.0 copy-start.4
  6.0 0.5 %collective-permute-start = (f32[4,3,16,384]{3,2,1,0:T(8,128)S(1)}, f32[4,3,16,384]{3,2,1,0:T(8,128)S(1)}, u32[]{:S(2)}, u32[]{:S(2)}) collective-permute-start(f32[4,3,16,384]{3,2,1,0:T(8,128)S(1)} %get-tuple-element.14), channel_id=1, source_target_pairs={{0,4},{4,0},{8,12},{12,8},{16,20},{20,16},{24,28},{28,24},{1,5},{5... | collective-permute-start | bytes 884744 | tf_op jit(solution)/shard_map/ppermute | solution.py:237
  6.6 1.2 %collective-permute-done.received = f32[4,3,16,384]{3,2,1,0:T(8,128)S(1)} collective-permute-done((f32[4,3,16,384]{3,2,1,0:T(8,128)S(1)}, f32[4,3,16,384]{3,2,1,0:T(8,128)S(1)}, u32[]{:S(2)}, u32[]{:S(2)}) %collective-permute-start) | collective-permute-done | bytes 294944 | tf_op jit(solution)/shard_map/ppermute | solution.py:237
  7.8 2.9 %collective-permute-start.1 = (f32[3,16,384]{2,1,0:T(8,128)S(1)}, f32[3,16,384]{2,1,0:T(8,128)S(1)}, u32[]{:S(2)}, u32[]{:S(2)}) collective-permute-start(f32[3,16,384]{2,1,0:T(8,128)S(1)} %get-tuple-element.16), channel_id=1, source_target_pairs={{0,8},{4,12},{8,0},{12,4},{16,24},{20,28},{24,16},{28,20},{1,9},{5... | collective-permute-start | bytes 221192 | tf_op jit(solution)/shard_map/ppermute | solution.py:237
  10.7 1.5 %collective-permute-start.2 = (f32[3,16,384]{2,1,0:T(8,128)S(1)}, f32[3,16,384]{2,1,0:T(8,128)S(1)}, u32[]{:S(2)}, u32[]{:S(2)}) collective-permute-start(f32[3,16,384]{2,1,0:T(8,128)S(1)} %get-tuple-element.17), channel_id=1, source_target_pairs={{0,16},{4,20},{8,24},{12,28},{16,0},{20,4},{24,8},{28,12},{1,17},{... | collective-permute-start | bytes 221192 | tf_op jit(solution)/shard_map/ppermute | solution.py:237
  12.3 0.0 collective-permute-start.3
  12.3 1.0 %collective-permute-done.1.refs_0_ = f32[3,16,384]{2,1,0:T(8,128)S(1)} collective-permute-done((f32[3,16,384]{2,1,0:T(8,128)S(1)}, f32[3,16,384]{2,1,0:T(8,128)S(1)}, u32[]{:S(2)}, u32[]{:S(2)}) %collective-permute-start.1) | collective-permute-done | bytes 73760 | tf_op jit(solution)/shard_map/ppermute | solution.py:237
  13.3 1.8 %collective-permute-done.2.refs_1_ = f32[3,16,384]{2,1,0:T(8,128)S(1)} collective-permute-done((f32[3,16,384]{2,1,0:T(8,128)S(1)}, f32[3,16,384]{2,1,0:T(8,128)S(1)}, u32[]{:S(2)}, u32[]{:S(2)}) %collective-permute-start.2) | collective-permute-done | bytes 73760 | tf_op jit(solution)/shard_map/ppermute | solution.py:237
  15.1 2.4 %collective-permute-done.3.refs_2_ = f32[3,16,384]{2,1,0:T(8,128)S(1)} collective-permute-done((f32[3,16,384]{2,1,0:T(8,128)S(1)}, f32[3,16,384]{2,1,0:T(8,128)S(1)}, u32[]{:S(2)}, u32[]{:S(2)}) %collective-permute-start.3) | collective-permute-done | bytes 73760 | tf_op jit(solution)/shard_map/ppermute | solution.py:237
  17.5 1.6 %collective-permute-start.4 = (f32[2,16,384]{2,1,0:T(8,128)S(1)}, f32[2,16,384]{2,1,0:T(8,128)S(1)}, u32[]{:S(2)}, u32[]{:S(2)}) collective-permute-start(f32[2,16,384]{2,1,0:T(8,128)S(1)} %get-tuple-element.20), channel_id=1, source_target_pairs={{0,1},{2,3},{1,0},{3,2},{4,5},{6,7},{5,4},{7,6},{8,9},{10,11},{9,8... | collective-permute-start | bytes 147464 | tf_op jit(solution)/shard_map/ppermute | solution.py:307
  19.2 0.7 %collective-permute-start.5 = (f32[2,16,384]{2,1,0:T(8,128)S(1)}, f32[2,16,384]{2,1,0:T(8,128)S(1)}, u32[]{:S(2)}, u32[]{:S(2)}) collective-permute-start(f32[2,16,384]{2,1,0:T(8,128)S(1)} %get-tuple-element.21), channel_id=1, source_target_pairs={{1,2},{2,1},{5,6},{6,5},{9,10},{10,9},{13,14},{14,13},{17,18},{18,... | collective-permute-start | bytes 147464 | tf_op jit(solution)/shard_map/ppermute | solution.py:307
  19.8 3.9 %collective-permute-start.6 = (f32[16,384]{1,0:T(8,128)S(1)}, f32[16,384]{1,0:T(8,128)S(1)}, u32[]{:S(2)}, u32[]{:S(2)}) collective-permute-start(f32[16,384]{1,0:T(8,128)S(1)} %get-tuple-element.22), channel_id=1, source_target_pairs={{0,2},{1,3},{2,0},{3,1},{4,6},{5,7},{6,4},{7,5},{8,10},{9,11},{10,... | collective-permute-start | bytes 73736 | tf_op jit(solution)/shard_map/ppermute | solution.py:307
  23.8 2.4 %collective-permute-done.6.c = f32[16,384]{1,0:T(8,128)S(1)} collective-permute-done((f32[16,384]{1,0:T(8,128)S(1)}, f32[16,384]{1,0:T(8,128)S(1)}, u32[]{:S(2)}, u32[]{:S(2)}) %collective-permute-start.6) | collective-permute-done | bytes 24608 | tf_op jit(solution)/shard_map/ppermute | solution.py:307
  26.2 0.0 collective-permute-done.4.a
  26.2 0.0 collective-permute-done.5.b
  26.2 0.8 %collective-permute-start.9 = (f32[3,16,384]{2,1,0:T(8,128)S(1)}, f32[3,16,384]{2,1,0:T(8,128)S(1)}, u32[]{:S(2)}, u32[]{:S(2)}) collective-permute-start(f32[3,16,384]{2,1,0:T(8,128)S(1)} %third_sum.1.refs_0_), channel_id=1, source_target_pairs={{0,24},{4,28},{8,16},{12,20},{16,8},{20,12},{24,0},{28,4},{1,25},{... | collective-permute-start | bytes 221192 | tf_op jit(solution)/shard_map/ppermute | solution.py:237
  27.0 1.4 %collective-permute-start.8 = (f32[3,16,384]{2,1,0:T(8,128)S(1)}, f32[3,16,384]{2,1,0:T(8,128)S(1)}, u32[]{:S(2)}, u32[]{:S(2)}) collective-permute-start(f32[3,16,384]{2,1,0:T(8,128)S(1)} %third_sum.1.refs_0_), channel_id=1, source_target_pairs={{0,16},{4,20},{8,24},{12,28},{16,0},{20,4},{24,8},{28,12},{1,17},{... | collective-permute-start | bytes 221192 | tf_op jit(solution)/shard_map/ppermute | solution.py:237
  28.3 1.4 %collective-permute-start.7 = (f32[3,16,384]{2,1,0:T(8,128)S(1)}, f32[3,16,384]{2,1,0:T(8,128)S(1)}, u32[]{:S(2)}, u32[]{:S(2)}) collective-permute-start(f32[3,16,384]{2,1,0:T(8,128)S(1)} %third_sum.1.refs_0_), channel_id=1, source_target_pairs={{0,8},{4,12},{8,0},{12,4},{16,24},{20,28},{24,16},{28,20},{1,9},{5... | collective-permute-start | bytes 221192 | tf_op jit(solution)/shard_map/ppermute | solution.py:237
  29.8 1.9 %collective-permute-done.9.refs_3_ = f32[3,16,384]{2,1,0:T(8,128)S(1)} collective-permute-done((f32[3,16,384]{2,1,0:T(8,128)S(1)}, f32[3,16,384]{2,1,0:T(8,128)S(1)}, u32[]{:S(2)}, u32[]{:S(2)}) %collective-permute-start.9) | collective-permute-done | bytes 73760 | tf_op jit(solution)/shard_map/ppermute | solution.py:237
  31.6 0.5 %collective-permute-done.8.refs_2_ = f32[3,16,384]{2,1,0:T(8,128)S(1)} collective-permute-done((f32[3,16,384]{2,1,0:T(8,128)S(1)}, f32[3,16,384]{2,1,0:T(8,128)S(1)}, u32[]{:S(2)}, u32[]{:S(2)}) %collective-permute-start.8) | collective-permute-done | bytes 73760 | tf_op jit(solution)/shard_map/ppermute | solution.py:237
  32.1 0.6 %collective-permute-done.7.refs_1_ = f32[3,16,384]{2,1,0:T(8,128)S(1)} collective-permute-done((f32[3,16,384]{2,1,0:T(8,128)S(1)}, f32[3,16,384]{2,1,0:T(8,128)S(1)}, u32[]{:S(2)}, u32[]{:S(2)}) %collective-permute-start.7) | collective-permute-done | bytes 73760 | tf_op jit(solution)/shard_map/ppermute | solution.py:237
  32.7 0.1 collective-permute-start.10
  32.8 1.6 %collective-permute-done.10.other = f32[4,3,16,384]{3,2,1,0:T(8,128)S(1)} collective-permute-done((f32[4,3,16,384]{3,2,1,0:T(8,128)S(1)}, f32[4,3,16,384]{3,2,1,0:T(8,128)S(1)}, u32[]{:S(2)}, u32[]{:S(2)}) %collective-permute-start.10) | collective-permute-done | bytes 294944 | tf_op jit(solution)/shard_map/ppermute | solution.py:237
  34.4 0.0 copy-done.2
  34.4 0.0 copy-done.3
  34.4 0.0 copy-done
  34.4 0.0 copy-done.1
  34.4 0.0 copy-done.4
  34.4 3.5 %back.1 = (f32[2,128,384]{2,1,0:T(8,128)}, f32[128,384]{1,0:T(8,128)}) custom-call(f32[2,128,384]{2,1,0:T(8,128)S(1)} %copy-done.2, f32[4,3,16,384]{3,2,1,0:T(8,128)S(1)} %stack.1.mine, f32[4,3,16,384]{3,2,1,0:T(8,128)S(1)} %collective-permute-done.10.other, f32[2,4,192,256]{3,2,1,0:T(8,128)S(1)} %get-tuple-element.23.optic, ...), custom_call_target="tpu_custom_call" | custom-call | tf_op jit(solution)/shard_map/back/pallas_call | solution.py:312
  (4 shorter events, 0.1 us)
Async XLA Ops:
  0.6 33.7 %copy-start.2 = (f32[2,128,384]{2,1,0:T(8,128)S(1)}, f32[2,128,384]{2,1,0:T(8,128)}, u32[]{:S(2)}) copy-start(f32[2,128,384]{2,1,0:T(8,128)} %volume.1) | copy-start | bytes 1179652
  0.6 33.7 %copy-start.3 = (bf16[2,512,384]{2,1,0:T(8,128)(2,1)S(1)}, bf16[2,512,384]{2,1,0:T(8,128)(2,1)}, u32[]{:S(2)}) copy-start(bf16[2,512,384]{2,1,0:T(8,128)(2,1)} %constant.17.clone.ci) | copy-start | bytes 2359300
  6.0 28.4 %copy-start = (bf16[2,384,512]{2,1,0:T(8,128)(2,1)S(1)}, bf16[2,384,512]{2,1,0:T(8,128)(2,1)}, u32[]{:S(2)}) copy-start(bf16[2,384,512]{2,1,0:T(8,128)(2,1)} %constant.13.clone.cf_h.cf) | copy-start | bytes 2359300
  6.0 28.4 %copy-start.1 = (bf16[2,384,384]{2,1,0:T(8,128)(2,1)S(1)}, bf16[2,384,384]{2,1,0:T(8,128)(2,1)}, u32[]{:S(2)}) copy-start(bf16[2,384,384]{2,1,0:T(8,128)(2,1)} %constant.12.clone.rf_h.rf) | copy-start | bytes 1769476
  6.0 28.4 %copy-start.4 = (bf16[2,128,384]{2,1,0:T(8,128)(2,1)S(1)}, bf16[2,128,384]{2,1,0:T(8,128)(2,1)}, u32[]{:S(2)}) copy-start(bf16[2,128,384]{2,1,0:T(8,128)(2,1)} %constant.16.clone.ri) | copy-start | bytes 589828
  6.0 1.7 %collective-permute-start = (f32[4,3,16,384]{3,2,1,0:T(8,128)S(1)}, f32[4,3,16,384]{3,2,1,0:T(8,128)S(1)}, u32[]{:S(2)}, u32[]{:S(2)}) collective-permute-start(f32[4,3,16,384]{3,2,1,0:T(8,128)S(1)} %get-tuple-element.14), channel_id=1, source_target_pairs={{0,4},{4,0},{8,12},{12,8},{16,20},{20,16},{24,28},{28,24},{1,5},{5... | collective-permute-start | bytes 884744 | tf_op jit(solution)/shard_map/ppermute | solution.py:237
  7.8 5.5 %collective-permute-start.1 = (f32[3,16,384]{2,1,0:T(8,128)S(1)}, f32[3,16,384]{2,1,0:T(8,128)S(1)}, u32[]{:S(2)}, u32[]{:S(2)}) collective-permute-start(f32[3,16,384]{2,1,0:T(8,128)S(1)} %get-tuple-element.16), channel_id=1, source_target_pairs={{0,8},{4,12},{8,0},{12,4},{16,24},{20,28},{24,16},{28,20},{1,9},{5... | collective-permute-start | bytes 221192 | tf_op jit(solution)/shard_map/ppermute | solution.py:237
  10.7 4.4 %collective-permute-start.2 = (f32[3,16,384]{2,1,0:T(8,128)S(1)}, f32[3,16,384]{2,1,0:T(8,128)S(1)}, u32[]{:S(2)}, u32[]{:S(2)}) collective-permute-start(f32[3,16,384]{2,1,0:T(8,128)S(1)} %get-tuple-element.17), channel_id=1, source_target_pairs={{0,16},{4,20},{8,24},{12,28},{16,0},{20,4},{24,8},{28,12},{1,17},{... | collective-permute-start | bytes 221192 | tf_op jit(solution)/shard_map/ppermute | solution.py:237
  12.3 5.3 %collective-permute-start.3 = (f32[3,16,384]{2,1,0:T(8,128)S(1)}, f32[3,16,384]{2,1,0:T(8,128)S(1)}, u32[]{:S(2)}, u32[]{:S(2)}) collective-permute-start(f32[3,16,384]{2,1,0:T(8,128)S(1)} %get-tuple-element.18), channel_id=1, source_target_pairs={{0,24},{4,28},{8,16},{12,20},{16,8},{20,12},{24,0},{28,4},{1,25},{... | collective-permute-start | bytes 221192 | tf_op jit(solution)/shard_map/ppermute | solution.py:237
  17.5 8.6 %collective-permute-start.4 = (f32[2,16,384]{2,1,0:T(8,128)S(1)}, f32[2,16,384]{2,1,0:T(8,128)S(1)}, u32[]{:S(2)}, u32[]{:S(2)}) collective-permute-start(f32[2,16,384]{2,1,0:T(8,128)S(1)} %get-tuple-element.20), channel_id=1, source_target_pairs={{0,1},{2,3},{1,0},{3,2},{4,5},{6,7},{5,4},{7,6},{8,9},{10,11},{9,8... | collective-permute-start | bytes 147464 | tf_op jit(solution)/shard_map/ppermute | solution.py:307
  19.2 7.0 %collective-permute-start.5 = (f32[2,16,384]{2,1,0:T(8,128)S(1)}, f32[2,16,384]{2,1,0:T(8,128)S(1)}, u32[]{:S(2)}, u32[]{:S(2)}) collective-permute-start(f32[2,16,384]{2,1,0:T(8,128)S(1)} %get-tuple-element.21), channel_id=1, source_target_pairs={{1,2},{2,1},{5,6},{6,5},{9,10},{10,9},{13,14},{14,13},{17,18},{18,... | collective-permute-start | bytes 147464 | tf_op jit(solution)/shard_map/ppermute | solution.py:307
  19.8 6.3 %collective-permute-start.6 = (f32[16,384]{1,0:T(8,128)S(1)}, f32[16,384]{1,0:T(8,128)S(1)}, u32[]{:S(2)}, u32[]{:S(2)}) collective-permute-start(f32[16,384]{1,0:T(8,128)S(1)} %get-tuple-element.22), channel_id=1, source_target_pairs={{0,2},{1,3},{2,0},{3,1},{4,6},{5,7},{6,4},{7,5},{8,10},{9,11},{10,... | collective-permute-start | bytes 73736 | tf_op jit(solution)/shard_map/ppermute | solution.py:307
  26.2 5.4 %collective-permute-start.9 = (f32[3,16,384]{2,1,0:T(8,128)S(1)}, f32[3,16,384]{2,1,0:T(8,128)S(1)}, u32[]{:S(2)}, u32[]{:S(2)}) collective-permute-start(f32[3,16,384]{2,1,0:T(8,128)S(1)} %third_sum.1.refs_0_), channel_id=1, source_target_pairs={{0,24},{4,28},{8,16},{12,20},{16,8},{20,12},{24,0},{28,4},{1,25},{... | collective-permute-start | bytes 221192 | tf_op jit(solution)/shard_map/ppermute | solution.py:237
  27.0 5.1 %collective-permute-start.8 = (f32[3,16,384]{2,1,0:T(8,128)S(1)}, f32[3,16,384]{2,1,0:T(8,128)S(1)}, u32[]{:S(2)}, u32[]{:S(2)}) collective-permute-start(f32[3,16,384]{2,1,0:T(8,128)S(1)} %third_sum.1.refs_0_), channel_id=1, source_target_pairs={{0,16},{4,20},{8,24},{12,28},{16,0},{20,4},{24,8},{28,12},{1,17},{... | collective-permute-start | bytes 221192 | tf_op jit(solution)/shard_map/ppermute | solution.py:237
  28.3 4.4 %collective-permute-start.7 = (f32[3,16,384]{2,1,0:T(8,128)S(1)}, f32[3,16,384]{2,1,0:T(8,128)S(1)}, u32[]{:S(2)}, u32[]{:S(2)}) collective-permute-start(f32[3,16,384]{2,1,0:T(8,128)S(1)} %third_sum.1.refs_0_), channel_id=1, source_target_pairs={{0,8},{4,12},{8,0},{12,4},{16,24},{20,28},{24,16},{28,20},{1,9},{5... | collective-permute-start | bytes 221192 | tf_op jit(solution)/shard_map/ppermute | solution.py:237
  32.7 1.6 %collective-permute-start.10 = (f32[4,3,16,384]{3,2,1,0:T(8,128)S(1)}, f32[4,3,16,384]{3,2,1,0:T(8,128)S(1)}, u32[]{:S(2)}, u32[]{:S(2)}) collective-permute-start(f32[4,3,16,384]{3,2,1,0:T(8,128)S(1)} %stack.1.mine), channel_id=1, source_target_pairs={{0,4},{4,0},{8,12},{12,8},{16,20},{20,16},{24,28},{28,24},{1,5},{5... | collective-permute-start | bytes 884744 | tf_op jit(solution)/shard_map/ppermute | solution.py:237

commit v2 on v1

--- a/solution.py
+++ b/solution.py
@@ -1,5 +1,3 @@
-import functools
-
 import jax
 import jax.numpy as jnp
 import ml_dtypes
@@ -88,7 +86,6 @@
 
 
 def project_kernel(
-    share,
     volume_h,
     point_spread_h,
     measured_h,
@@ -158,45 +155,42 @@
     own = frame[rows : 2 * rows] - measured[...] * jnp.where(d == 0, 1.0, 0.0)
     down = frame[2 * rows :] * jnp.where(t == tiles - 1, 0.0, 1.0)
     even = d % 2 == 0
+    half = rows // 2
     for s, strip in enumerate((up, own, down)):
-        for c in range(keep.shape[0]):
-            a = strip[2 * c * share : (2 * c + 1) * share]
-            b = strip[(2 * c + 1) * share : (2 * c + 2) * share]
-            keep[c, s] = jnp.where(even, a, b)
-            send[c, s] = jnp.where(even, b, a)
-
-
-def first_sum_kernel(keep, received, *outs):
-    chip = lax.axis_index("depth") // 2
-    for m, out in enumerate(outs):
-        out[...] = keep[chip ^ m] + received[chip ^ m]
-
-
-def second_sum_kernel(fourth, own, *refs):
-    ins, outs = refs[: len(refs) - (4 + fourth)], refs[len(refs) - (4 + fourth) :]
-    t = lax.axis_index("tile")
-    even, lower = t % 2 == 0, t % 4 < 2
-    parts = own[...]
-    for x in ins:
-        parts = parts + x[...]
-    outs[0][...] = parts
-    outs[1][...] = jnp.where(even, parts[1:], parts[:2])
-    outs[2][...] = jnp.where(even, parts[:2], parts[1:])
-    outs[3][...] = jnp.where(lower, parts[2], parts[0])
-    if fourth:
-        outs[4][...] = jnp.where(lower, parts[0], parts[2])
-
-
-def third_sum_kernel(parts, a, b, c, *refs):
-    strips = refs[-1]
-    t = lax.axis_index("tile")
-    even, lower = t % 2 == 0, t % 4 < 2
-    e = refs[0][...] if len(refs) > 1 else jnp.zeros_like(c)
-    from_above = jnp.where(even, a[...], b[...])
-    from_below = jnp.where(even, b[...], a[...])
-    strips[0] = from_below[0] + parts[0] + jnp.where(lower, e, c[...])
-    strips[1] = parts[1] + from_below[1] + from_above[0]
-    strips[2] = from_above[1] + parts[2] + jnp.where(lower, c[...], e)
+        keep[s] = jnp.where(even, strip[:half], strip[half:])
+        send[s] = jnp.where(even, strip[half:], strip[:half])
+
+
+def split_kernel(keep, received, own, first, second):
+    even = lax.axis_index("tile") % 2 == 0
+    up, down = keep[0] + received[0], keep[2] + received[2]
+    own[...] = keep[1] + received[1]
+    first[...] = jnp.where(even, down, up)
+    second[...] = jnp.where(even, up, down)
+
+
+def tree(terms):
+    if len(terms) == 1:
+        return terms[0]
+    middle = len(terms) // 2
+    return tree(terms[:middle]) + tree(terms[middle:])
+
+
+def paired():
+    t, n = lax.axis_index("tile"), lax.axis_size("tile")
+    even = t % 2 == 0
+    first = jnp.where(even, t + 1, t - 1)
+    second = jnp.where(even, t - 1, t + 1)
+    return first < n, jnp.logical_and(second >= 0, second < n)
+
+
+def tile_sum_kernel(own, a, b, out):
+    first, second = paired()
+    out[...] = own[...] + jnp.where(first, a[...], 0.0) + jnp.where(second, b[...], 0.0)
+
+
+def sum_kernel(*refs):
+    refs[-1][...] = tree([x[...] for x in refs[:-1]])
 
 
 def stack_kernel(*refs):
@@ -206,16 +200,15 @@
 
 def back_kernel(volume, mine, other, optic, rf, cf, ri, ci, volume_next, residual, frame):
     planes, rows, width = volume.shape
-    chips, _, share, _ = mine.shape
-    d = lax.axis_index("depth")
-    chip, core = d // 2, d % 2
-    for m in range(chips):
-        c = chip ^ m
-        for s in range(3):
-            at = s * rows + (2 * c + core) * share
-            frame[pl.ds(pl.multiple_of(at, share), share)] = mine[m, s]
-            at = s * rows + (2 * c + 1 - core) * share
-            frame[pl.ds(pl.multiple_of(at, share), share)] = other[m, s]
+    half = rows // 2
+    core = lax.axis_index("depth") % 2
+    even = lax.axis_index("tile") % 2 == 0
+    strips = (1, jnp.where(even, 2, 0), jnp.where(even, 0, 2))
+    for m, (strip, valid) in enumerate(zip(strips, (True,) + paired())):
+        at = strip * rows + core * half
+        frame[pl.ds(pl.multiple_of(at, half), half)] = jnp.where(valid, mine[m], 0.0)
+        at = strip * rows + (1 - core) * half
+        frame[pl.ds(pl.multiple_of(at, half), half)] = jnp.where(valid, other[m], 0.0)
     residual[...] = frame[rows : 2 * rows]
     r = times_table(frame[...], cf[0], cf[1])
     r = row_spectrum(rf[0], rf[1], r)
@@ -237,8 +230,14 @@
     return lax.ppermute(x, axis, [(i, i ^ mask) for i in range(lax.axis_size(axis))])
 
 
-def both_ways(pairs):
-    return [(a, b) for a, b in pairs] + [(b, a) for a, b in pairs]
+def pairing(depths, tiles, start):
+    partner = {}
+    for t in range(tiles):
+        other = t + 1 if (t - start) % 2 == 0 else t - 1
+        for d in range(depths):
+            inside = 0 <= other < tiles
+            partner[d * tiles + t] = d * tiles + other if inside else (d ^ 1) * tiles + t
+    return sorted(partner.items())
 
 
 def local(kernel, name, outs, *args):
@@ -258,18 +257,17 @@
     n = lax.axis_size("depth")
     tiles = lax.axis_size("tile")
     chips = n // 2
-    share = rows // n
     f32 = jnp.float32
     rf, cf, rp, cp, rb, cb = (
         jnp.asarray(x) for x in tables(rows, width, half_width)
     )
-    half = (chips, 3, share, width)
-    piece = (3, share, width)
+    half = (3, rows // 2, width)
+    piece = (rows // 2, width)
     kp = -(-point_spread.shape[1] // 128) * 128
     spread = jnp.transpose(point_spread, (1, 0, 2))
     operands = (volume, spread, measured, rf, cf, rp, cp)
     keep, send, optic = pl.pallas_call(
-        functools.partial(project_kernel, share),
+        project_kernel,
         out_shape=[
             pltpu.VMEM(half, f32),
             pltpu.VMEM(half, f32),
@@ -287,27 +285,14 @@
         name="project",
     )(*[pltpu.with_memory_space_constraint(x, pltpu.HBM) for x in operands])
     received = swap(send, "depth", 1)
-    mine = local(first_sum_kernel, "first_sum", [piece] * chips, keep, received)
-    arrived = [swap(mine[m], "depth", 2 * m) for m in range(1, chips)]
-    pairs = [
-        [(i, i + 1) for i in range(0, tiles - 1, 2)],
-        [(i, i + 1) for i in range(1, tiles - 1, 2)],
-        [(i, i + 2) for i in range(tiles - 2) if i % 4 < 2],
-        [(i, i + 2) for i in range(tiles - 2) if i % 4 >= 2],
-    ]
-    fourth = int(bool(pairs[3]))
-    edge = (2, share, width)
-    parts, *sends = local(
-        functools.partial(second_sum_kernel, fourth),
-        "second_sum",
-        [piece, edge, edge] + [piece[1:]] * (1 + fourth),
-        mine[0],
-        *arrived,
-    )
-    arrived = [lax.ppermute(x, "tile", both_ways(p)) for x, p in zip(sends, pairs)]
-    (strips,) = local(third_sum_kernel, "third_sum", [piece], parts, *arrived)
-    arrived = [swap(strips, "depth", 2 * m) for m in range(1, chips)]
-    (gathered,) = local(stack_kernel, "stack", [half], strips, *arrived)
+    pairs = [pairing(n, tiles, start) for start in (0, 1)]
+    own, *sends = local(split_kernel, "split", [piece] * 3, keep, received)
+    beside = [lax.ppermute(x, ("depth", "tile"), p) for x, p in zip(sends, pairs)]
+    (part,) = local(tile_sum_kernel, "sum_tiles", [piece], own, *beside)
+    others = [swap(part, "depth", 2 * m) for m in range(1, chips)]
+    (whole,) = local(sum_kernel, "sum_chips", [piece], part, *others)
+    beside = [lax.ppermute(whole, ("depth", "tile"), p) for p in pairs]
+    (gathered,) = local(stack_kernel, "stack", [half], whole, *beside)
     other = swap(gathered, "depth", 1)
     volume_next, residual = pl.pallas_call(
         back_kernel,

time: 38.1 us -> 34.3 us (0.900)
  starting transfers between devices: 14.8 us -> 11.7 us
  waiting for transfers between devices: 13.4 us -> 12.7 us
    ppermute x8 -> x5, starting transfers between devices: 8.6 us -> 4.14 us  [swap(): lax.ppermute(x, axis, [(i, i ^ mask) for i in range(lax.axis_size(axis))])]
    ppermute x8 -> x5, waiting for transfers between devices: 11 us -> 7.01 us  [swap(): lax.ppermute(x, axis, [(i, i ^ mask) for i in range(lax.axis_size(axis))])]
    ppermute x3 -> x4, waiting for transfers between devices: 2.41 us -> 5.69 us  [the longest x2 3.1 us: per_device(): lax.ppermute(x, ('depth', 'tile'), p)]
    ppermute x3 -> x4, starting transfers between devices: 6.21 us -> 7.6 us  [the longest x2 4.57 us: per_device(): beside = [lax.ppermute(whole, ('depth', 'tile'), p) for p in pairs]]
  transfers between devices with their start and end apart: 11 -> 9, of which waited for: 9 -> 7; matrix products, arithmetic and copies ran while one was open for 0% -> 0% of each run, Pallas kernels for 0% -> 0%
where the time goes in v2:
time: 34.3 us; the launch traced here: 34.1 us
  waiting for transfers between devices  12.7 us (37%)
  starting transfers between devices  11.7 us (34%)
  Pallas kernels  8.91 us (26%)
  between operations  0.74 us (2%)
    ppermute x5, waiting for transfers between devices, swap(): lax.ppermute(x, axis, [(i, i ^ mask) for i in range(lax.axis_size(axis))])  7.01 us
    pallas_call x1, Pallas kernels, per_device(): pl.pallas_call(project_kernel, out_shape=[pltpu.VMEM(half, f32), pltpu.VM...  5.32 us
    ppermute x2, starting transfers between devices, per_device(): beside = [lax.ppermute(whole, ('depth', 'tile'), p) for p in pairs]  4.57 us
    ppermute x5, starting transfers between devices, swap(): lax.ppermute(x, axis, [(i, i ^ mask) for i in range(lax.axis_size(axis))])  4.14 us
    pallas_call x1, Pallas kernels, per_device(): pl.pallas_call(back_kernel, out_shape=[jax.ShapeDtypeStruct(volume.shape,...  3.49 us
    ppermute x2, waiting for transfers between devices, per_device(): lax.ppermute(x, ('depth', 'tile'), p)  3.1 us
    ppermute x2, starting transfers between devices, per_device(): lax.ppermute(x, ('depth', 'tile'), p)  3.02 us
    ppermute x2, waiting for transfers between devices, per_device(): beside = [lax.ppermute(whole, ('depth', 'tile'), p) for p in pairs]  2.59 us
  transfers between devices with their start and end apart: 9, of which 7 were waited for; matrix products, arithmetic and copies ran while one was open for 0% of the time, Pallas kernels for 0%

profile of v2, /device:TPU:0, one launch (start us, length us, event | category | flops | bytes accessed | tf_op | source)
XLA Modules:
  0.0 34.1 jit_solution(793281811433557397)
XLA Ops:
  0.6 0.0 copy-start.3
  0.6 5.3 %project.1 = (f32[3,64,384]{2,1,0:T(8,128)S(1)}, f32[3,64,384]{2,1,0:T(8,128)S(1)}, f32[2,4,192,256]{3,2,1,0:T(8,128)S(1)}) custom-call(f32[2,128,384]{2,1,0:T(8,128)} %volume.1, f32[255,2,255]{2,1,0:T(2,128)} %bitcast.1, f32[128,384]{1,0:T(8,128)} %measured_h.1, bf16[2,384,384]{2,1,0:T(8,128)(2,1)} %constant.12.clone.rf_h.rf, ...), custom_call_target="tpu_custom_call" | custom-call | tf_op jit(solution)/shard_map/project/pallas_call | solution.py:269
  6.0 0.0 copy-start
  6.0 0.0 copy-start.1
  6.0 0.0 copy-start.2
  6.0 0.0 copy-start.4
  6.0 0.5 %collective-permute-start = (f32[3,64,384]{2,1,0:T(8,128)S(1)}, f32[3,64,384]{2,1,0:T(8,128)S(1)}, u32[]{:S(2)}, u32[]{:S(2)}) collective-permute-start(f32[3,64,384]{2,1,0:T(8,128)S(1)} %get-tuple-element.9), channel_id=1, source_target_pairs={{0,4},{4,0},{8,12},{12,8},{16,20},{20,16},{24,28},{28,24},{1,5},{5... | collective-permute-start | bytes 884744 | tf_op jit(solution)/shard_map/ppermute | solution.py:230
  6.5 1.2 %collective-permute-done.received = f32[3,64,384]{2,1,0:T(8,128)S(1)} collective-permute-done((f32[3,64,384]{2,1,0:T(8,128)S(1)}, f32[3,64,384]{2,1,0:T(8,128)S(1)}, u32[]{:S(2)}, u32[]{:S(2)}) %collective-permute-start) | collective-permute-done | bytes 294944 | tf_op jit(solution)/shard_map/ppermute | solution.py:230
  7.8 3.0 %collective-permute-start.1 = (f32[64,384]{1,0:T(8,128)S(1)}, f32[64,384]{1,0:T(8,128)S(1)}, u32[]{:S(2)}, u32[]{:S(2)}) collective-permute-start(f32[64,384]{1,0:T(8,128)S(1)} %get-tuple-element.11), channel_id=1, source_target_pairs={{0,1},{1,0},{2,3},{3,2},{4,5},{5,4},{6,7},{7,6},{8,9},{9,8},{10,11... | collective-permute-start | bytes 294920 | tf_op jit(solution)/shard_map/ppermute | solution.py:290
  10.8 0.0 collective-permute-start.2
  10.8 3.1 %collective-permute-done.1.a = f32[64,384]{1,0:T(8,128)S(1)} collective-permute-done((f32[64,384]{1,0:T(8,128)S(1)}, f32[64,384]{1,0:T(8,128)S(1)}, u32[]{:S(2)}, u32[]{:S(2)}) %collective-permute-start.1) | collective-permute-done | bytes 98336 | tf_op jit(solution)/shard_map/ppermute | solution.py:290
  13.9 0.0 collective-permute-done.2.b
  13.9 2.7 %collective-permute-start.5 = (f32[64,384]{1,0:T(8,128)S(1)}, f32[64,384]{1,0:T(8,128)S(1)}, u32[]{:S(2)}, u32[]{:S(2)}) collective-permute-start(f32[64,384]{1,0:T(8,128)S(1)} %sum_tiles.1.refs_0_), channel_id=1, source_target_pairs={{0,24},{4,28},{8,16},{12,20},{16,8},{20,12},{24,0},{28,4},{1,25},{... | collective-permute-start | bytes 294920 | tf_op jit(solution)/shard_map/ppermute | solution.py:230
  16.6 0.5 %collective-permute-start.4 = (f32[64,384]{1,0:T(8,128)S(1)}, f32[64,384]{1,0:T(8,128)S(1)}, u32[]{:S(2)}, u32[]{:S(2)}) collective-permute-start(f32[64,384]{1,0:T(8,128)S(1)} %sum_tiles.1.refs_0_), channel_id=1, source_target_pairs={{0,16},{4,20},{8,24},{12,28},{16,0},{20,4},{24,8},{28,12},{1,17},{... | collective-permute-start | bytes 294920 | tf_op jit(solution)/shard_map/ppermute | solution.py:230
  17.1 0.4 %collective-permute-start.3 = (f32[64,384]{1,0:T(8,128)S(1)}, f32[64,384]{1,0:T(8,128)S(1)}, u32[]{:S(2)}, u32[]{:S(2)}) collective-permute-start(f32[64,384]{1,0:T(8,128)S(1)} %sum_tiles.1.refs_0_), channel_id=1, source_target_pairs={{0,8},{4,12},{8,0},{12,4},{16,24},{20,28},{24,16},{28,20},{1,9},{5... | collective-permute-start | bytes 294920 | tf_op jit(solution)/shard_map/ppermute | solution.py:230
  17.5 2.2 %collective-permute-done.5.refs_3_ = f32[64,384]{1,0:T(8,128)S(1)} collective-permute-done((f32[64,384]{1,0:T(8,128)S(1)}, f32[64,384]{1,0:T(8,128)S(1)}, u32[]{:S(2)}, u32[]{:S(2)}) %collective-permute-start.5) | collective-permute-done | bytes 98336 | tf_op jit(solution)/shard_map/ppermute | solution.py:230
  19.6 1.7 %collective-permute-done.4.refs_2_ = f32[64,384]{1,0:T(8,128)S(1)} collective-permute-done((f32[64,384]{1,0:T(8,128)S(1)}, f32[64,384]{1,0:T(8,128)S(1)}, u32[]{:S(2)}, u32[]{:S(2)}) %collective-permute-start.4) | collective-permute-done | bytes 98336 | tf_op jit(solution)/shard_map/ppermute | solution.py:230
  21.4 0.3 %collective-permute-done.3.refs_1_ = f32[64,384]{1,0:T(8,128)S(1)} collective-permute-done((f32[64,384]{1,0:T(8,128)S(1)}, f32[64,384]{1,0:T(8,128)S(1)}, u32[]{:S(2)}, u32[]{:S(2)}) %collective-permute-start.3) | collective-permute-done | bytes 98336 | tf_op jit(solution)/shard_map/ppermute | solution.py:230
  21.7 0.1 collective-permute-start.7
  21.8 4.5 %collective-permute-start.6 = (f32[64,384]{1,0:T(8,128)S(1)}, f32[64,384]{1,0:T(8,128)S(1)}, u32[]{:S(2)}, u32[]{:S(2)}) collective-permute-start(f32[64,384]{1,0:T(8,128)S(1)} %sum_chips.1.refs_0_), channel_id=1, source_target_pairs={{0,1},{1,0},{2,3},{3,2},{4,5},{5,4},{6,7},{7,6},{8,9},{9,8},{10,11... | collective-permute-start | bytes 294920 | tf_op jit(solution)/shard_map/ppermute | solution.py:294
  26.3 0.0 collective-permute-done.7.refs_2_
  26.3 2.6 %collective-permute-done.6.refs_1_ = f32[64,384]{1,0:T(8,128)S(1)} collective-permute-done((f32[64,384]{1,0:T(8,128)S(1)}, f32[64,384]{1,0:T(8,128)S(1)}, u32[]{:S(2)}, u32[]{:S(2)}) %collective-permute-start.6) | collective-permute-done | bytes 98336 | tf_op jit(solution)/shard_map/ppermute | solution.py:294
  28.9 0.1 collective-permute-start.8
  29.0 1.6 %collective-permute-done.8.other = f32[3,64,384]{2,1,0:T(8,128)S(1)} collective-permute-done((f32[3,64,384]{2,1,0:T(8,128)S(1)}, f32[3,64,384]{2,1,0:T(8,128)S(1)}, u32[]{:S(2)}, u32[]{:S(2)}) %collective-permute-start.8) | collective-permute-done | bytes 294944 | tf_op jit(solution)/shard_map/ppermute | solution.py:230
  30.6 0.0 copy-done.3
  30.6 0.0 copy-done
  30.6 0.0 copy-done.1
  30.6 0.0 copy-done.2
  30.6 0.0 copy-done.4
  30.6 3.5 %back.1 = (f32[2,128,384]{2,1,0:T(8,128)}, f32[128,384]{1,0:T(8,128)}) custom-call(f32[2,128,384]{2,1,0:T(8,128)S(1)} %copy-done.2, f32[3,64,384]{2,1,0:T(8,128)S(1)} %stack.1.mine, f32[3,64,384]{2,1,0:T(8,128)S(1)} %collective-permute-done.8.other, f32[2,4,192,256]{3,2,1,0:T(8,128)S(1)} %get-tuple-element.13.optic, bf16[2,384,384]{2,1,0:T(8,128)(2,1)S(1)} %copy-done.1, ...), custom_call_target="tpu_custom_call" | custom-call | tf_op jit(solution)/shard_map/back/pallas_call | solution.py:297
  (4 shorter events, 0.1 us)
Async XLA Ops:
  0.6 30.0 %copy-start.3 = (bf16[2,512,384]{2,1,0:T(8,128)(2,1)S(1)}, bf16[2,512,384]{2,1,0:T(8,128)(2,1)}, u32[]{:S(2)}) copy-start(bf16[2,512,384]{2,1,0:T(8,128)(2,1)} %constant.17.clone.ci) | copy-start | bytes 2359300
  6.0 24.6 %copy-start = (bf16[2,384,512]{2,1,0:T(8,128)(2,1)S(1)}, bf16[2,384,512]{2,1,0:T(8,128)(2,1)}, u32[]{:S(2)}) copy-start(bf16[2,384,512]{2,1,0:T(8,128)(2,1)} %constant.13.clone.cf_h.cf) | copy-start | bytes 2359300
  6.0 24.6 %copy-start.1 = (bf16[2,384,384]{2,1,0:T(8,128)(2,1)S(1)}, bf16[2,384,384]{2,1,0:T(8,128)(2,1)}, u32[]{:S(2)}) copy-start(bf16[2,384,384]{2,1,0:T(8,128)(2,1)} %constant.12.clone.rf_h.rf) | copy-start | bytes 1769476
  6.0 24.6 %copy-start.2 = (f32[2,128,384]{2,1,0:T(8,128)S(1)}, f32[2,128,384]{2,1,0:T(8,128)}, u32[]{:S(2)}) copy-start(f32[2,128,384]{2,1,0:T(8,128)} %volume.1) | copy-start | bytes 1179652
  6.0 24.6 %copy-start.4 = (bf16[2,128,384]{2,1,0:T(8,128)(2,1)S(1)}, bf16[2,128,384]{2,1,0:T(8,128)(2,1)}, u32[]{:S(2)}) copy-start(bf16[2,128,384]{2,1,0:T(8,128)(2,1)} %constant.16.clone.ri) | copy-start | bytes 589828
  6.0 1.7 %collective-permute-start = (f32[3,64,384]{2,1,0:T(8,128)S(1)}, f32[3,64,384]{2,1,0:T(8,128)S(1)}, u32[]{:S(2)}, u32[]{:S(2)}) collective-permute-start(f32[3,64,384]{2,1,0:T(8,128)S(1)} %get-tuple-element.9), channel_id=1, source_target_pairs={{0,4},{4,0},{8,12},{12,8},{16,20},{20,16},{24,28},{28,24},{1,5},{5... | collective-permute-start | bytes 884744 | tf_op jit(solution)/shard_map/ppermute | solution.py:230
  7.8 6.1 %collective-permute-start.1 = (f32[64,384]{1,0:T(8,128)S(1)}, f32[64,384]{1,0:T(8,128)S(1)}, u32[]{:S(2)}, u32[]{:S(2)}) collective-permute-start(f32[64,384]{1,0:T(8,128)S(1)} %get-tuple-element.11), channel_id=1, source_target_pairs={{0,1},{1,0},{2,3},{3,2},{4,5},{5,4},{6,7},{7,6},{8,9},{9,8},{10,11... | collective-permute-start | bytes 294920 | tf_op jit(solution)/shard_map/ppermute | solution.py:290
  10.8 3.1 %collective-permute-start.2 = (f32[64,384]{1,0:T(8,128)S(1)}, f32[64,384]{1,0:T(8,128)S(1)}, u32[]{:S(2)}, u32[]{:S(2)}) collective-permute-start(f32[64,384]{1,0:T(8,128)S(1)} %get-tuple-element.12), channel_id=1, source_target_pairs={{0,4},{1,2},{2,1},{3,7},{4,0},{5,6},{6,5},{7,3},{8,12},{9,10},{10,... | collective-permute-start | bytes 294920 | tf_op jit(solution)/shard_map/ppermute | solution.py:290
  13.9 5.7 %collective-permute-start.5 = (f32[64,384]{1,0:T(8,128)S(1)}, f32[64,384]{1,0:T(8,128)S(1)}, u32[]{:S(2)}, u32[]{:S(2)}) collective-permute-start(f32[64,384]{1,0:T(8,128)S(1)} %sum_tiles.1.refs_0_), channel_id=1, source_target_pairs={{0,24},{4,28},{8,16},{12,20},{16,8},{20,12},{24,0},{28,4},{1,25},{... | collective-permute-start | bytes 294920 | tf_op jit(solution)/shard_map/ppermute | solution.py:230
  16.6 4.8 %collective-permute-start.4 = (f32[64,384]{1,0:T(8,128)S(1)}, f32[64,384]{1,0:T(8,128)S(1)}, u32[]{:S(2)}, u32[]{:S(2)}) collective-permute-start(f32[64,384]{1,0:T(8,128)S(1)} %sum_tiles.1.refs_0_), channel_id=1, source_target_pairs={{0,16},{4,20},{8,24},{12,28},{16,0},{20,4},{24,8},{28,12},{1,17},{... | collective-permute-start | bytes 294920 | tf_op jit(solution)/shard_map/ppermute | solution.py:230
  17.1 4.6 %collective-permute-start.3 = (f32[64,384]{1,0:T(8,128)S(1)}, f32[64,384]{1,0:T(8,128)S(1)}, u32[]{:S(2)}, u32[]{:S(2)}) collective-permute-start(f32[64,384]{1,0:T(8,128)S(1)} %sum_tiles.1.refs_0_), channel_id=1, source_target_pairs={{0,8},{4,12},{8,0},{12,4},{16,24},{20,28},{24,16},{28,20},{1,9},{5... | collective-permute-start | bytes 294920 | tf_op jit(solution)/shard_map/ppermute | solution.py:230
  21.7 4.6 %collective-permute-start.7 = (f32[64,384]{1,0:T(8,128)S(1)}, f32[64,384]{1,0:T(8,128)S(1)}, u32[]{:S(2)}, u32[]{:S(2)}) collective-permute-start(f32[64,384]{1,0:T(8,128)S(1)} %sum_chips.1.refs_0_), channel_id=1, source_target_pairs={{0,4},{1,2},{2,1},{3,7},{4,0},{5,6},{6,5},{7,3},{8,12},{9,10},{10,... | collective-permute-start | bytes 294920 | tf_op jit(solution)/shard_map/ppermute | solution.py:294
  21.8 7.1 %collective-permute-start.6 = (f32[64,384]{1,0:T(8,128)S(1)}, f32[64,384]{1,0:T(8,128)S(1)}, u32[]{:S(2)}, u32[]{:S(2)}) collective-permute-start(f32[64,384]{1,0:T(8,128)S(1)} %sum_chips.1.refs_0_), channel_id=1, source_target_pairs={{0,1},{1,0},{2,3},{3,2},{4,5},{5,4},{6,7},{7,6},{8,9},{9,8},{10,11... | collective-permute-start | bytes 294920 | tf_op jit(solution)/shard_map/ppermute | solution.py:294
  28.9 1.6 %collective-permute-start.8 = (f32[3,64,384]{2,1,0:T(8,128)S(1)}, f32[3,64,384]{2,1,0:T(8,128)S(1)}, u32[]{:S(2)}, u32[]{:S(2)}) collective-permute-start(f32[3,64,384]{2,1,0:T(8,128)S(1)} %stack.1.mine), channel_id=1, source_target_pairs={{0,4},{4,0},{8,12},{12,8},{16,20},{20,16},{24,28},{28,24},{1,5},{5... | collective-permute-start | bytes 884744 | tf_op jit(solution)/shard_map/ppermute | solution.py:230

commit v3 on v2

v3 whole, which is shorter than its diff:
```python
import jax
import jax.numpy as jnp
import ml_dtypes
import numpy as np
from jax import lax
from jax.experimental import pallas as pl
from jax.experimental.pallas import tpu as pltpu
from jax.sharding import PartitionSpec as P

step_size = 2.0
threshold = 0.5
VMEM = pl.BlockSpec(memory_space=pltpu.VMEM)
HBM = pl.BlockSpec(memory_space=pltpu.HBM)
PARAMS = pltpu.CompilerParams(vmem_limit_bytes=24 * 1024 * 1024)
SMALL = pltpu.CompilerParams(vmem_limit_bytes=4 * 1024 * 1024)


def pair(table):
    high = table.astype(ml_dtypes.bfloat16)
    low = (table - high.astype(np.float64)).astype(ml_dtypes.bfloat16)
    return np.stack([high, low])


def tables(row_count, width_count, half_width):
    freq_rows = 3 * row_count
    freq_cols = -(-(width_count + half_width) // 256) * 256
    row_angle = 2.0 * np.pi / freq_rows * (np.arange(freq_rows // 2) + 0.5)
    col_angle = 2.0 * np.pi / freq_cols * (np.arange(freq_cols // 2) + 0.5)
    row_phase = row_angle[:, None] * np.arange(freq_rows)[None, :]
    col_phase = np.arange(width_count)[:, None] * col_angle[None, :]
    row_table = np.concatenate([np.cos(row_phase), np.sin(row_phase)], axis=0)
    col_table = np.concatenate([np.cos(col_phase), -np.sin(col_phase)], axis=1)
    centre = np.stack([np.cos(half_width * col_angle), np.sin(half_width * col_angle)])
    shift = np.zeros((8, freq_cols // 2), np.float32)
    shift[:2] = centre * (2.0 / (freq_rows * freq_cols))
    return pair(row_table), pair(col_table), shift


def split(x):
    high = x.astype(jnp.bfloat16)
    low = (x - high.astype(jnp.float32)).astype(jnp.bfloat16)
    return high, low


def times_table(x, high, low):
    x_high, x_low = split(x)
    return jnp.dot(
        jnp.concatenate([x_high, x_low, x_high], axis=1),
        jnp.concatenate([high, high, low], axis=0),
        preferred_element_type=jnp.float32,
    )


def table_times(high, low, x):
    x_high, x_low = split(x)
    return jnp.dot(
        jnp.concatenate([high, high, low], axis=1),
        jnp.concatenate([x_high, x_low, x_high], axis=0),
        preferred_element_type=jnp.float32,
    )


def row_spectrum(high, low, x):
    q = table_times(high, low, x)
    u, v = q.shape[0] // 2, q.shape[1] // 2
    cr, ci, sr, si = q[:u, :v], q[:u, v:], q[u:, :v], q[u:, v:]
    return cr + si, ci - sr, cr - si, ci + sr


def folded(spectrum):
    pr, pi, mr, mi = spectrum
    top = jnp.concatenate([pr + mr, pi + mi], axis=1)
    bottom = jnp.concatenate([mi - pi, pr - mr], axis=1)
    return jnp.concatenate([top, bottom], axis=0)


def project_kernel(
    volume_h,
    point_spread_h,
    rf_h,
    cf_h,
    shift_h,
    measured_h,
    keep,
    send,
    optic,
    rf,
    rt,
    cf,
    ct,
    volume,
    point_spread,
    shift,
    measured,
    pad,
    arrived,
):
    kp = pad.shape[1]
    moves = {}
    order = (
        ("spread", point_spread_h, point_spread),
        ("cf", cf_h.at[:, :kp], cf.at[:, :kp]),
        ("shift", shift_h, shift),
        ("rf", rf_h, rf),
        ("volume", volume_h, volume),
        ("cf_rest", cf_h.at[:, kp:], cf.at[:, kp:]),
        ("measured", measured_h, measured),
    )
    for i, (name, source, target) in enumerate(order):
        moves[name] = pltpu.make_async_copy(source, target, arrived.at[i])
        moves[name].start()
    planes, rows, width = volume.shape
    k = point_spread.shape[0]
    d, t = lax.axis_index("depth"), lax.axis_index("tile")
    tiles = lax.axis_size("tile")
    above = rows - (k - 1) // 2
    pad[...] = jnp.zeros_like(pad)
    moves["spread"].wait()
    for i in range(planes):
        pad[i, above : above + k, :k] = point_spread[:, i, :]
    moves["cf"].wait()
    moves["shift"].wait()
    cos, sin = shift[0:1], shift[1:2]
    v = cos.shape[1]
    x = times_table(pad[...].reshape(planes * kp, kp), cf[0, :kp], cf[1, :kp])
    re, im = x[:, :v], x[:, v:]
    spread = jnp.concatenate([re * cos - im * sin, re * sin + im * cos], axis=1)
    moves["volume"].wait()
    moves["cf_rest"].wait()
    image = times_table(volume[...].reshape(planes * rows, width), cf[0], cf[1])
    for i in range(2):
        ct[i] = cf[i].T
    moves["rf"].wait()
    rt[0] = rf[0].T
    rt[1] = rf[1].T
    total = None
    for i in range(planes):
        h = row_spectrum(rf[0, :, :kp], rf[1, :, :kp], spread[i * kp : (i + 1) * kp])
        for j in range(4):
            optic[i, j] = h[j]
        f = row_spectrum(rf[0, :, :rows], rf[1, :, :rows], image[i * rows : (i + 1) * rows])
        term = (
            h[0] * f[0] - h[1] * f[1],
            h[0] * f[1] + h[1] * f[0],
            h[2] * f[2] - h[3] * f[3],
            h[2] * f[3] + h[3] * f[2],
        )
        total = term if total is None else [a + b for a, b in zip(total, term)]
    frame = times_table(table_times(rt[0], rt[1], folded(total)), ct[0], ct[1])
    moves["measured"].wait()
    strips = (
        frame[:rows] * jnp.where(t == 0, 0.0, 1.0),
        frame[rows : 2 * rows] - measured[...] * jnp.where(d == 0, 1.0, 0.0),
        frame[2 * rows :] * jnp.where(t == tiles - 1, 0.0, 1.0),
    )
    half = rows // 2
    for j, strip in enumerate(strips):
        keep[j] = jnp.where(d % 2 == 0, strip[:half], strip[half:])
        send[j] = jnp.where(d % 2 == 0, strip[half:], strip[:half])


def split_kernel(keep, received, own, first, second):
    even = lax.axis_index("tile") % 2 == 0
    up, down = keep[0] + received[0], keep[2] + received[2]
    own[...] = keep[1] + received[1]
    first[...] = jnp.where(even, down, up)
    second[...] = jnp.where(even, up, down)


def tree(terms):
    if len(terms) == 1:
        return terms[0]
    middle = len(terms) // 2
    return tree(terms[:middle]) + tree(terms[middle:])


def paired():
    t, n = lax.axis_index("tile"), lax.axis_size("tile")
    even = t % 2 == 0
    first = jnp.where(even, t + 1, t - 1)
    second = jnp.where(even, t - 1, t + 1)
    return first < n, jnp.logical_and(second >= 0, second < n)


def tile_sum_kernel(own, a, b, out):
    first, second = paired()
    out[...] = own[...] + jnp.where(first, a[...], 0.0) + jnp.where(second, b[...], 0.0)


def sum_kernel(*refs):
    refs[-1][...] = tree([x[...] for x in refs[:-1]])


def stack_kernel(*refs):
    for m, x in enumerate(refs[:-1]):
        refs[-1][m] = x[...]


def back_kernel(volume, mine, other, optic, rf, rt, cf, ct, volume_next, residual, frame):
    planes, rows, width = volume.shape
    half = rows // 2
    core = lax.axis_index("depth") % 2
    even = lax.axis_index("tile") % 2 == 0
    first, second = paired()
    strips = ((1, True), (jnp.where(even, 0, 2), second), (jnp.where(even, 2, 0), first))
    for m, (strip, valid) in enumerate(strips):
        at = strip * rows + core * half
        frame[pl.ds(pl.multiple_of(at, half), half)] = jnp.where(valid, mine[m], 0.0)
        at = strip * rows + (1 - core) * half
        frame[pl.ds(pl.multiple_of(at, half), half)] = jnp.where(valid, other[m], 0.0)
    residual[...] = frame[rows : 2 * rows]
    r = times_table(frame[...], cf[0], cf[1])
    r = row_spectrum(rf[0], rf[1], r)
    mixed = []
    for i in range(planes):
        h = [optic[i, j] for j in range(4)]
        g = (
            h[0] * r[0] + h[1] * r[1],
            h[0] * r[1] - h[1] * r[0],
            h[2] * r[2] + h[3] * r[3],
            h[2] * r[3] - h[3] * r[2],
        )
        mixed.append(table_times(rt[0, :rows], rt[1, :rows], folded(g)))
    gradient = times_table(jnp.concatenate(mixed, axis=0), ct[0], ct[1])
    shifted = volume[...] - step_size * gradient.reshape(planes, rows, width)
    volume_next[...] = jnp.maximum(shifted - threshold, 0.0) + jnp.minimum(
        shifted + threshold, 0.0
    )


def swap(x, axis, mask):
    return lax.ppermute(x, axis, [(i, i ^ mask) for i in range(lax.axis_size(axis))])


def pairing(depths, tiles, start):
    partner = {}
    for t in range(tiles):
        other = t + 1 if (t - start) % 2 == 0 else t - 1
        for d in range(depths):
            inside = 0 <= other < tiles
            partner[d * tiles + t] = d * tiles + other if inside else (d ^ 1) * tiles + t
    return sorted(partner.items())


def local(kernel, name, outs, *args):
    return pl.pallas_call(
        kernel,
        out_shape=[pltpu.VMEM(x, jnp.float32) for x in outs],
        in_specs=[VMEM] * len(args),
        out_specs=[VMEM] * len(outs),
        compiler_params=SMALL,
        name=name,
    )(*args)


def in_hbm(x):
    return pltpu.with_memory_space_constraint(x, pltpu.HBM)


def per_device(volume, point_spread, measured):
    planes, rows, width = volume.shape
    half_width = (point_spread.shape[1] - 1) // 2
    n = lax.axis_size("depth")
    tiles = lax.axis_size("tile")
    chips = n // 2
    f32, bf16 = jnp.float32, jnp.bfloat16
    rf, cf, shift = (jnp.asarray(x) for x in tables(rows, width, half_width))
    u, v = rf.shape[1], cf.shape[2]
    piece = (rows // 2, width)
    three = (3,) + piece
    kp = -(-(rows + half_width + 1) // 128) * 128
    spread = jnp.transpose(point_spread, (1, 0, 2))
    operands = (volume, spread, rf, cf, shift, measured)
    keep, send, optic, rf, rt, cf, ct = pl.pallas_call(
        project_kernel,
        out_shape=[
            pltpu.VMEM(three, f32),
            pltpu.VMEM(three, f32),
            pltpu.VMEM((planes, 4, u // 2, v // 2), f32),
            pltpu.VMEM(rf.shape, bf16),
            pltpu.VMEM((2, rf.shape[2], u), bf16),
            pltpu.VMEM(cf.shape, bf16),
            pltpu.VMEM((2, v, width), bf16),
        ],
        in_specs=[HBM] * 6,
        out_specs=[VMEM] * 7,
        scratch_shapes=[
            pltpu.VMEM(volume.shape, f32),
            pltpu.VMEM(spread.shape, f32),
            pltpu.VMEM(shift.shape, f32),
            pltpu.VMEM(measured.shape, f32),
            pltpu.VMEM((planes, kp, kp), f32),
            pltpu.SemaphoreType.DMA((7,)),
        ],
        compiler_params=PARAMS,
        name="project",
    )(*[in_hbm(x) for x in operands])
    received = swap(send, "depth", 1)
    pairs = [pairing(n, tiles, start) for start in (0, 1)]
    own, *sends = local(split_kernel, "split", [piece] * 3, keep, received)
    beside = [lax.ppermute(x, ("depth", "tile"), p) for x, p in zip(sends, pairs)]
    (part,) = local(tile_sum_kernel, "sum_tiles", [piece], own, *beside)
    others = [swap(part, "depth", 2 * m) for m in range(1, chips)]
    (whole,) = local(sum_kernel, "sum_chips", [piece], part, *others)
    beside = [lax.ppermute(whole, ("depth", "tile"), p) for p in pairs[::-1]]
    (gathered,) = local(stack_kernel, "stack", [three], whole, *beside)
    other = swap(gathered, "depth", 1)
    volume_next, residual = pl.pallas_call(
        back_kernel,
        out_shape=[
            jax.ShapeDtypeStruct(volume.shape, f32),
            jax.ShapeDtypeStruct(measured.shape, f32),
        ],
        in_specs=[VMEM] * 8,
        out_specs=[VMEM] * 2,
        scratch_shapes=[pltpu.VMEM((3 * rows, width), f32)],
        compiler_params=PARAMS,
        name="back",
    )(volume, gathered, other, optic, rf, rt, cf, ct)
    return volume_next, residual


def solution(mesh):
    placed = (P("depth", "tile", None), P("depth", None, None), P("tile", None))
    return jax.shard_map(
        per_device,
        mesh=mesh,
        in_specs=placed,
        out_specs=(P("depth", "tile", None), P("tile", None)),
        check_vma=False,
    )
```

time: 34.3 us -> 32 us (0.933)
  starting transfers between devices: 11.7 us -> 9.92 us
    ppermute x2, starting transfers between devices: 4.57 us -> 2.77 us  [per_device(): beside = [lax.ppermute(whole, ('depth', 'tile'), p) for p in pairs[::-1]]]
where the time goes in v3:
time: 32 us; the launch traced here: 31.9 us
  waiting for transfers between devices  12.7 us (40%)
  starting transfers between devices  9.92 us (31%)
  Pallas kernels  8.57 us (27%)
  between operations  0.68 us (2%)
    ppermute x5, waiting for transfers between devices, swap(): lax.ppermute(x, axis, [(i, i ^ mask) for i in range(lax.axis_size(axis))])  7.02 us
    pallas_call x1, Pallas kernels, per_device(): pl.pallas_call(project_kernel, out_shape=[pltpu.VMEM(three, f32), pltpu.V...  5.11 us
    ppermute x5, starting transfers between devices, swap(): lax.ppermute(x, axis, [(i, i ^ mask) for i in range(lax.axis_size(axis))])  4.14 us
    pallas_call x1, Pallas kernels, per_device(): pl.pallas_call(back_kernel, out_shape=[jax.ShapeDtypeStruct(volume.shape,...  3.37 us
    ppermute x2, waiting for transfers between devices, per_device(): lax.ppermute(x, ('depth', 'tile'), p)  3.1 us
    ppermute x2, starting transfers between devices, per_device(): lax.ppermute(x, ('depth', 'tile'), p)  3.01 us
    ppermute x2, starting transfers between devices, per_device(): beside = [lax.ppermute(whole, ('depth', 'tile'), p) for p in pairs[::-1]]  2.77 us
    ppermute x2, waiting for transfers between devices, per_device(): beside = [lax.ppermute(whole, ('depth', 'tile'), p) for p in pairs[::-1]]  2.6 us
  transfers between devices with their start and end apart: 9, of which 7 were waited for; matrix products, arithmetic and copies ran while one was open for 0% of the time, Pallas kernels for 0%

profile of v3, /device:TPU:0, one launch (start us, length us, event | category | flops | bytes accessed | tf_op | source)
XLA Modules:
  0.0 31.9 jit_solution(9485310752499960768)
XLA Ops:
  0.6 5.1 %project.1 = (f32[3,64,384]{2,1,0:T(8,128)S(1)}, f32[3,64,384]{2,1,0:T(8,128)S(1)}, f32[2,4,192,256]{3,2,1,0:T(8,128)S(1)}, bf16[2,384,384]{2,1,0:T(8,128)(2,1)S...) custom-call(f32[2,128,384]{2,1,0:T(8,128)} %volume.1, ...), custom_call_target="tpu_custom_call" | custom-call | tf_op jit(solution)/shard_map/project/pallas_call | solution.py:274
  5.7 0.0 copy-start
  5.8 0.5 %collective-permute-start = (f32[3,64,384]{2,1,0:T(8,128)S(1)}, f32[3,64,384]{2,1,0:T(8,128)S(1)}, u32[]{:S(2)}, u32[]{:S(2)}) collective-permute-start(f32[3,64,384]{2,1,0:T(8,128)S(1)} %get-tuple-element.13), channel_id=1, source_target_pairs={{0,4},{4,0},{8,12},{12,8},{16,20},{20,16},{24,28},{28,24},{1,5},{5... | collective-permute-start | bytes 884744 | tf_op jit(solution)/shard_map/ppermute | solution.py:232
  6.3 1.2 %collective-permute-done.received = f32[3,64,384]{2,1,0:T(8,128)S(1)} collective-permute-done((f32[3,64,384]{2,1,0:T(8,128)S(1)}, f32[3,64,384]{2,1,0:T(8,128)S(1)}, u32[]{:S(2)}, u32[]{:S(2)}) %collective-permute-start) | collective-permute-done | bytes 294944 | tf_op jit(solution)/shard_map/ppermute | solution.py:232
  7.5 3.0 %collective-permute-start.1 = (f32[64,384]{1,0:T(8,128)S(1)}, f32[64,384]{1,0:T(8,128)S(1)}, u32[]{:S(2)}, u32[]{:S(2)}) collective-permute-start(f32[64,384]{1,0:T(8,128)S(1)} %get-tuple-element.15), channel_id=1, source_target_pairs={{0,1},{1,0},{2,3},{3,2},{4,5},{5,4},{6,7},{7,6},{8,9},{9,8},{10,11... | collective-permute-start | bytes 294920 | tf_op jit(solution)/shard_map/ppermute | solution.py:301
  10.5 0.0 collective-permute-start.2
  10.5 3.1 %collective-permute-done.1.a = f32[64,384]{1,0:T(8,128)S(1)} collective-permute-done((f32[64,384]{1,0:T(8,128)S(1)}, f32[64,384]{1,0:T(8,128)S(1)}, u32[]{:S(2)}, u32[]{:S(2)}) %collective-permute-start.1) | collective-permute-done | bytes 98336 | tf_op jit(solution)/shard_map/ppermute | solution.py:301
  13.6 0.0 collective-permute-done.2.b
  13.6 2.7 %collective-permute-start.5 = (f32[64,384]{1,0:T(8,128)S(1)}, f32[64,384]{1,0:T(8,128)S(1)}, u32[]{:S(2)}, u32[]{:S(2)}) collective-permute-start(f32[64,384]{1,0:T(8,128)S(1)} %sum_tiles.1.refs_0_), channel_id=1, source_target_pairs={{0,24},{4,28},{8,16},{12,20},{16,8},{20,12},{24,0},{28,4},{1,25},{... | collective-permute-start | bytes 294920 | tf_op jit(solution)/shard_map/ppermute | solution.py:232
  16.3 0.5 %collective-permute-start.4 = (f32[64,384]{1,0:T(8,128)S(1)}, f32[64,384]{1,0:T(8,128)S(1)}, u32[]{:S(2)}, u32[]{:S(2)}) collective-permute-start(f32[64,384]{1,0:T(8,128)S(1)} %sum_tiles.1.refs_0_), channel_id=1, source_target_pairs={{0,16},{4,20},{8,24},{12,28},{16,0},{20,4},{24,8},{28,12},{1,17},{... | collective-permute-start | bytes 294920 | tf_op jit(solution)/shard_map/ppermute | solution.py:232
  16.8 0.4 %collective-permute-start.3 = (f32[64,384]{1,0:T(8,128)S(1)}, f32[64,384]{1,0:T(8,128)S(1)}, u32[]{:S(2)}, u32[]{:S(2)}) collective-permute-start(f32[64,384]{1,0:T(8,128)S(1)} %sum_tiles.1.refs_0_), channel_id=1, source_target_pairs={{0,8},{4,12},{8,0},{12,4},{16,24},{20,28},{24,16},{28,20},{1,9},{5... | collective-permute-start | bytes 294920 | tf_op jit(solution)/shard_map/ppermute | solution.py:232
  17.2 2.2 %collective-permute-done.5.refs_3_ = f32[64,384]{1,0:T(8,128)S(1)} collective-permute-done((f32[64,384]{1,0:T(8,128)S(1)}, f32[64,384]{1,0:T(8,128)S(1)}, u32[]{:S(2)}, u32[]{:S(2)}) %collective-permute-start.5) | collective-permute-done | bytes 98336 | tf_op jit(solution)/shard_map/ppermute | solution.py:232
  19.4 1.7 %collective-permute-done.4.refs_2_ = f32[64,384]{1,0:T(8,128)S(1)} collective-permute-done((f32[64,384]{1,0:T(8,128)S(1)}, f32[64,384]{1,0:T(8,128)S(1)}, u32[]{:S(2)}, u32[]{:S(2)}) %collective-permute-start.4) | collective-permute-done | bytes 98336 | tf_op jit(solution)/shard_map/ppermute | solution.py:232
  21.1 0.3 %collective-permute-done.3.refs_1_ = f32[64,384]{1,0:T(8,128)S(1)} collective-permute-done((f32[64,384]{1,0:T(8,128)S(1)}, f32[64,384]{1,0:T(8,128)S(1)}, u32[]{:S(2)}, u32[]{:S(2)}) %collective-permute-start.3) | collective-permute-done | bytes 98336 | tf_op jit(solution)/shard_map/ppermute | solution.py:232
  21.5 2.8 %collective-permute-start.7 = (f32[64,384]{1,0:T(8,128)S(1)}, f32[64,384]{1,0:T(8,128)S(1)}, u32[]{:S(2)}, u32[]{:S(2)}) collective-permute-start(f32[64,384]{1,0:T(8,128)S(1)} %sum_chips.1.refs_0_), channel_id=1, source_target_pairs={{0,1},{1,0},{2,3},{3,2},{4,5},{5,4},{6,7},{7,6},{8,9},{9,8},{10,11... | collective-permute-start | bytes 294920 | tf_op jit(solution)/shard_map/ppermute | solution.py:305
  24.2 0.0 collective-permute-start.6
  24.2 2.6 %collective-permute-done.7.refs_2_ = f32[64,384]{1,0:T(8,128)S(1)} collective-permute-done((f32[64,384]{1,0:T(8,128)S(1)}, f32[64,384]{1,0:T(8,128)S(1)}, u32[]{:S(2)}, u32[]{:S(2)}) %collective-permute-start.7) | collective-permute-done | bytes 98336 | tf_op jit(solution)/shard_map/ppermute | solution.py:305
  26.8 0.0 collective-permute-done.6.refs_1_
  26.9 0.1 collective-permute-start.8
  26.9 1.6 %collective-permute-done.8.other = f32[3,64,384]{2,1,0:T(8,128)S(1)} collective-permute-done((f32[3,64,384]{2,1,0:T(8,128)S(1)}, f32[3,64,384]{2,1,0:T(8,128)S(1)}, u32[]{:S(2)}, u32[]{:S(2)}) %collective-permute-start.8) | collective-permute-done | bytes 294944 | tf_op jit(solution)/shard_map/ppermute | solution.py:232
  28.5 0.0 copy-done
  28.5 3.4 %back.1 = (f32[2,128,384]{2,1,0:T(8,128)}, f32[128,384]{1,0:T(8,128)}) custom-call(f32[2,128,384]{2,1,0:T(8,128)S(1)} %copy-done, f32[3,64,384]{2,1,0:T(8,128)S(1)} %stack.1.mine, f32[3,64,384]{2,1,0:T(8,128)S(1)} %collective-permute-done.8.other, f32[2,4,192,256]{3,2,1,0:T(8,128)S(1)} %get-tuple-element.17.optic, ...), custom_call_target="tpu_custom_call" | custom-call | tf_op jit(solution)/shard_map/back/pallas_call | solution.py:308
  (4 shorter events, 0.1 us)
Async XLA Ops:
  5.7 22.8 %copy-start = (f32[2,128,384]{2,1,0:T(8,128)S(1)}, f32[2,128,384]{2,1,0:T(8,128)}, u32[]{:S(2)}) copy-start(f32[2,128,384]{2,1,0:T(8,128)} %volume.1) | copy-start | bytes 1179652
  5.8 1.7 %collective-permute-start = (f32[3,64,384]{2,1,0:T(8,128)S(1)}, f32[3,64,384]{2,1,0:T(8,128)S(1)}, u32[]{:S(2)}, u32[]{:S(2)}) collective-permute-start(f32[3,64,384]{2,1,0:T(8,128)S(1)} %get-tuple-element.13), channel_id=1, source_target_pairs={{0,4},{4,0},{8,12},{12,8},{16,20},{20,16},{24,28},{28,24},{1,5},{5... | collective-permute-start | bytes 884744 | tf_op jit(solution)/shard_map/ppermute | solution.py:232
  7.5 6.1 %collective-permute-start.1 = (f32[64,384]{1,0:T(8,128)S(1)}, f32[64,384]{1,0:T(8,128)S(1)}, u32[]{:S(2)}, u32[]{:S(2)}) collective-permute-start(f32[64,384]{1,0:T(8,128)S(1)} %get-tuple-element.15), channel_id=1, source_target_pairs={{0,1},{1,0},{2,3},{3,2},{4,5},{5,4},{6,7},{7,6},{8,9},{9,8},{10,11... | collective-permute-start | bytes 294920 | tf_op jit(solution)/shard_map/ppermute | solution.py:301
  10.5 3.1 %collective-permute-start.2 = (f32[64,384]{1,0:T(8,128)S(1)}, f32[64,384]{1,0:T(8,128)S(1)}, u32[]{:S(2)}, u32[]{:S(2)}) collective-permute-start(f32[64,384]{1,0:T(8,128)S(1)} %get-tuple-element.16), channel_id=1, source_target_pairs={{0,4},{1,2},{2,1},{3,7},{4,0},{5,6},{6,5},{7,3},{8,12},{9,10},{10,... | collective-permute-start | bytes 294920 | tf_op jit(solution)/shard_map/ppermute | solution.py:301
  13.6 5.7 %collective-permute-start.5 = (f32[64,384]{1,0:T(8,128)S(1)}, f32[64,384]{1,0:T(8,128)S(1)}, u32[]{:S(2)}, u32[]{:S(2)}) collective-permute-start(f32[64,384]{1,0:T(8,128)S(1)} %sum_tiles.1.refs_0_), channel_id=1, source_target_pairs={{0,24},{4,28},{8,16},{12,20},{16,8},{20,12},{24,0},{28,4},{1,25},{... | collective-permute-start | bytes 294920 | tf_op jit(solution)/shard_map/ppermute | solution.py:232
  16.3 4.8 %collective-permute-start.4 = (f32[64,384]{1,0:T(8,128)S(1)}, f32[64,384]{1,0:T(8,128)S(1)}, u32[]{:S(2)}, u32[]{:S(2)}) collective-permute-start(f32[64,384]{1,0:T(8,128)S(1)} %sum_tiles.1.refs_0_), channel_id=1, source_target_pairs={{0,16},{4,20},{8,24},{12,28},{16,0},{20,4},{24,8},{28,12},{1,17},{... | collective-permute-start | bytes 294920 | tf_op jit(solution)/shard_map/ppermute | solution.py:232
  16.8 4.6 %collective-permute-start.3 = (f32[64,384]{1,0:T(8,128)S(1)}, f32[64,384]{1,0:T(8,128)S(1)}, u32[]{:S(2)}, u32[]{:S(2)}) collective-permute-start(f32[64,384]{1,0:T(8,128)S(1)} %sum_tiles.1.refs_0_), channel_id=1, source_target_pairs={{0,8},{4,12},{8,0},{12,4},{16,24},{20,28},{24,16},{28,20},{1,9},{5... | collective-permute-start | bytes 294920 | tf_op jit(solution)/shard_map/ppermute | solution.py:232
  21.5 5.4 %collective-permute-start.7 = (f32[64,384]{1,0:T(8,128)S(1)}, f32[64,384]{1,0:T(8,128)S(1)}, u32[]{:S(2)}, u32[]{:S(2)}) collective-permute-start(f32[64,384]{1,0:T(8,128)S(1)} %sum_chips.1.refs_0_), channel_id=1, source_target_pairs={{0,1},{1,0},{2,3},{3,2},{4,5},{5,4},{6,7},{7,6},{8,9},{9,8},{10,11... | collective-permute-start | bytes 294920 | tf_op jit(solution)/shard_map/ppermute | solution.py:305
  24.2 2.6 %collective-permute-start.6 = (f32[64,384]{1,0:T(8,128)S(1)}, f32[64,384]{1,0:T(8,128)S(1)}, u32[]{:S(2)}, u32[]{:S(2)}) collective-permute-start(f32[64,384]{1,0:T(8,128)S(1)} %sum_chips.1.refs_0_), channel_id=1, source_target_pairs={{0,4},{1,2},{2,1},{3,7},{4,0},{5,6},{6,5},{7,3},{8,12},{9,10},{10,... | collective-permute-start | bytes 294920 | tf_op jit(solution)/shard_map/ppermute | solution.py:305
  26.9 1.6 %collective-permute-start.8 = (f32[3,64,384]{2,1,0:T(8,128)S(1)}, f32[3,64,384]{2,1,0:T(8,128)S(1)}, u32[]{:S(2)}, u32[]{:S(2)}) collective-permute-start(f32[3,64,384]{2,1,0:T(8,128)S(1)} %stack.1.mine), channel_id=1, source_target_pairs={{0,4},{4,0},{8,12},{12,8},{16,20},{20,16},{24,28},{28,24},{1,5},{5... | collective-permute-start | bytes 884744 | tf_op jit(solution)/shard_map/ppermute | solution.py:232

commit v4 on v3

--- a/solution.py
+++ b/solution.py
@@ -60,11 +60,14 @@
     )
 
 
-def row_spectrum(high, low, x):
-    q = table_times(high, low, x)
+def row_terms(q):
     u, v = q.shape[0] // 2, q.shape[1] // 2
     cr, ci, sr, si = q[:u, :v], q[:u, v:], q[u:, :v], q[u:, v:]
     return cr + si, ci - sr, cr - si, ci + sr
+
+
+def row_spectrum(high, low, x):
+    return row_terms(table_times(high, low, x))
 
 
 def folded(spectrum):
@@ -81,8 +84,9 @@
     cf_h,
     shift_h,
     measured_h,
-    keep,
+    spectrum,
     send,
+    measured,
     optic,
     rf,
     rt,
@@ -91,7 +95,6 @@
     volume,
     point_spread,
     shift,
-    measured,
     pad,
     arrived,
 ):
@@ -111,8 +114,6 @@
         moves[name].start()
     planes, rows, width = volume.shape
     k = point_spread.shape[0]
-    d, t = lax.axis_index("depth"), lax.axis_index("tile")
-    tiles = lax.axis_size("tile")
     above = rows - (k - 1) // 2
     pad[...] = jnp.zeros_like(pad)
     moves["spread"].wait()
@@ -146,17 +147,42 @@
             h[2] * f[3] + h[3] * f[2],
         )
         total = term if total is None else [a + b for a, b in zip(total, term)]
-    frame = times_table(table_times(rt[0], rt[1], folded(total)), ct[0], ct[1])
+    spectrum[0], spectrum[1] = split(folded(total))
+    image = image_rows(spectrum, rt, ct, 1)
     moves["measured"].wait()
-    strips = (
-        frame[:rows] * jnp.where(t == 0, 0.0, 1.0),
-        frame[rows : 2 * rows] - measured[...] * jnp.where(d == 0, 1.0, 0.0),
-        frame[2 * rows :] * jnp.where(t == tiles - 1, 0.0, 1.0),
-    )
+    finish(image, measured, send, 1)
+
+
+def image_rows(spectrum, rt, ct, other):
+    rows = rt.shape[1] // 3
     half = rows // 2
-    for j, strip in enumerate(strips):
-        keep[j] = jnp.where(d % 2 == 0, strip[:half], strip[half:])
-        send[j] = jnp.where(d % 2 == 0, strip[half:], strip[:half])
+    start = ((lax.axis_index("depth") + other) % 2) * half
+    table = [
+        jnp.concatenate(
+            [rt[i, pl.ds(pl.multiple_of(s * rows + start, half), half)] for s in range(3)], axis=0
+        )
+        for i in range(2)
+    ]
+    mixed = jnp.dot(
+        jnp.concatenate([table[0], table[0], table[1]], axis=1),
+        jnp.concatenate([spectrum[0], spectrum[1], spectrum[0]], axis=0),
+        preferred_element_type=jnp.float32,
+    )
+    return times_table(mixed, ct[0], ct[1])
+
+
+def finish(image, measured, out, other):
+    half = out.shape[1]
+    d, t = lax.axis_index("depth"), lax.axis_index("tile")
+    tiles = lax.axis_size("tile")
+    seen = jnp.where((d + other) % 2 == 0, measured[:half], measured[half:])
+    out[0] = image[:half] * jnp.where(t == 0, 0.0, 1.0)
+    out[1] = image[half : 2 * half] - seen * jnp.where(d == 0, 1.0, 0.0)
+    out[2] = image[2 * half :] * jnp.where(t == tiles - 1, 0.0, 1.0)
+
+
+def keep_kernel(spectrum, rt, ct, measured, keep):
+    finish(image_rows(spectrum, rt, ct, 0), measured, keep, 0)
 
 
 def split_kernel(keep, received, own, first, second):
@@ -196,21 +222,40 @@
         refs[-1][m] = x[...]
 
 
-def back_kernel(volume, mine, other, optic, rf, rt, cf, ct, volume_next, residual, frame):
+def by_core(x):
+    half = x.shape[-1] // 6
+    even = lax.axis_index("depth") % 2 == 0
+    first, second = (
+        jnp.concatenate(
+            [x[..., (2 * s + j) * half : (2 * s + j + 1) * half] for s in range(3)], axis=-1
+        )
+        for j in (0, 1)
+    )
+    return jnp.where(even, first, second), jnp.where(even, second, first)
+
+
+def row_part(strips, table, cf):
+    even = lax.axis_index("tile") % 2 == 0
+    first, second = paired()
+    b, a = jnp.where(second, strips[1], 0.0), jnp.where(first, strips[2], 0.0)
+    x = jnp.concatenate([jnp.where(even, b, a), strips[0], jnp.where(even, a, b)], axis=0)
+    return table_times(table[0], table[1], times_table(x, cf[0], cf[1]))
+
+
+def near_kernel(mine, rf, cf, partial, other_table):
+    tables = [by_core(rf[i]) for i in range(2)]
+    partial[...] = row_part(mine, [x for x, _ in tables], cf)
+    for i in range(2):
+        other_table[i] = tables[i][1]
+
+
+def back_kernel(volume, mine, other, table, partial, optic, rt, cf, ct, volume_next, residual):
     planes, rows, width = volume.shape
     half = rows // 2
-    core = lax.axis_index("depth") % 2
-    even = lax.axis_index("tile") % 2 == 0
-    first, second = paired()
-    strips = ((1, True), (jnp.where(even, 0, 2), second), (jnp.where(even, 2, 0), first))
-    for m, (strip, valid) in enumerate(strips):
-        at = strip * rows + core * half
-        frame[pl.ds(pl.multiple_of(at, half), half)] = jnp.where(valid, mine[m], 0.0)
-        at = strip * rows + (1 - core) * half
-        frame[pl.ds(pl.multiple_of(at, half), half)] = jnp.where(valid, other[m], 0.0)
-    residual[...] = frame[rows : 2 * rows]
-    r = times_table(frame[...], cf[0], cf[1])
-    r = row_spectrum(rf[0], rf[1], r)
+    even = lax.axis_index("depth") % 2 == 0
+    residual[:half] = jnp.where(even, mine[0], other[0])
+    residual[half:] = jnp.where(even, other[0], mine[0])
+    r = row_terms(partial[...] + row_part(other, table, cf))
     mixed = []
     for i in range(planes):
         h = [optic[i, j] for j in range(4)]
@@ -253,6 +298,10 @@
     )(*args)
 
 
+def cost(flops):
+    return pl.CostEstimate(flops=flops, bytes_accessed=0, transcendentals=0)
+
+
 def in_hbm(x):
     return pltpu.with_memory_space_constraint(x, pltpu.HBM)
 
@@ -271,11 +320,12 @@
     kp = -(-(rows + half_width + 1) // 128) * 128
     spread = jnp.transpose(point_spread, (1, 0, 2))
     operands = (volume, spread, rf, cf, shift, measured)
-    keep, send, optic, rf, rt, cf, ct = pl.pallas_call(
+    spectrum, send, seen, optic, rf, rt, cf, ct = pl.pallas_call(
         project_kernel,
         out_shape=[
+            pltpu.VMEM((2, u, v), bf16),
             pltpu.VMEM(three, f32),
-            pltpu.VMEM(three, f32),
+            pltpu.VMEM(measured.shape, f32),
             pltpu.VMEM((planes, 4, u // 2, v // 2), f32),
             pltpu.VMEM(rf.shape, bf16),
             pltpu.VMEM((2, rf.shape[2], u), bf16),
@@ -283,12 +333,11 @@
             pltpu.VMEM((2, v, width), bf16),
         ],
         in_specs=[HBM] * 6,
-        out_specs=[VMEM] * 7,
+        out_specs=[VMEM] * 8,
         scratch_shapes=[
             pltpu.VMEM(volume.shape, f32),
             pltpu.VMEM(spread.shape, f32),
             pltpu.VMEM(shift.shape, f32),
-            pltpu.VMEM(measured.shape, f32),
             pltpu.VMEM((planes, kp, kp), f32),
             pltpu.SemaphoreType.DMA((7,)),
         ],
@@ -296,6 +345,15 @@
         name="project",
     )(*[in_hbm(x) for x in operands])
     received = swap(send, "depth", 1)
+    (keep,) = pl.pallas_call(
+        keep_kernel,
+        out_shape=[pltpu.VMEM(three, f32)],
+        in_specs=[VMEM] * 4,
+        out_specs=[VMEM],
+        compiler_params=PARAMS,
+        cost_estimate=cost(9 * rows * v * (width + u)),
+        name="keep",
+    )(spectrum, rt, ct, seen)
     pairs = [pairing(n, tiles, start) for start in (0, 1)]
     own, *sends = local(split_kernel, "split", [piece] * 3, keep, received)
     beside = [lax.ppermute(x, ("depth", "tile"), p) for x, p in zip(sends, pairs)]
@@ -305,18 +363,26 @@
     beside = [lax.ppermute(whole, ("depth", "tile"), p) for p in pairs[::-1]]
     (gathered,) = local(stack_kernel, "stack", [three], whole, *beside)
     other = swap(gathered, "depth", 1)
+    partial, table = pl.pallas_call(
+        near_kernel,
+        out_shape=[pltpu.VMEM((u, v), f32), pltpu.VMEM((2, u, 3 * rows // 2), bf16)],
+        in_specs=[VMEM] * 3,
+        out_specs=[VMEM] * 2,
+        compiler_params=PARAMS,
+        cost_estimate=cost(2 * rows * v * 3 * (width + u)),
+        name="near",
+    )(gathered, rf, cf)
     volume_next, residual = pl.pallas_call(
         back_kernel,
         out_shape=[
             jax.ShapeDtypeStruct(volume.shape, f32),
             jax.ShapeDtypeStruct(measured.shape, f32),
         ],
-        in_specs=[VMEM] * 8,
+        in_specs=[VMEM] * 9,
         out_specs=[VMEM] * 2,
-        scratch_shapes=[pltpu.VMEM((3 * rows, width), f32)],
         compiler_params=PARAMS,
         name="back",
-    )(volume, gathered, other, optic, rf, rt, cf, ct)
+    )(volume, gathered, other, table, partial, optic, rt, cf, ct)
     return volume_next, residual
 
 

time: 32 us -> 31.2 us (0.975)
  waiting for transfers between devices: 12.7 us -> 11 us
  Pallas kernels: 8.57 us -> 9.53 us
    ppermute x5, waiting for transfers between devices: 7.02 us -> 5.27 us  [swap(): lax.ppermute(x, axis, [(i, i ^ mask) for i in range(lax.axis_size(axis))])]
    pallas_call x1 -> x3, Pallas kernels: 5.11 us -> 6.4 us  [the longest x1 4.67 us: per_device(): pl.pallas_call(project_kernel, out_shape=[pltpu.VMEM((2, u, v), bf16), pl...]
    pallas_call x1, Pallas kernels: 3.37 us -> 3.02 us  [per_device(): pl.pallas_call(back_kernel, out_shape=[jax.ShapeDtypeStruct(volume.shape,...]
  transfers between devices with their start and end apart: 9 -> 9, of which waited for: 7 -> 7; matrix products, arithmetic and copies ran while one was open for 0% -> 0% of each run, Pallas kernels for 0% -> 6%
where the time goes in v4:
time: 31.2 us; the launch traced here: 31.1 us
  waiting for transfers between devices  11 us (35%)
  starting transfers between devices  9.92 us (32%)
  Pallas kernels  9.53 us (31%)
  between operations  0.69 us (2%)
    ppermute x5, waiting for transfers between devices, swap(): lax.ppermute(x, axis, [(i, i ^ mask) for i in range(lax.axis_size(axis))])  5.27 us
    pallas_call x1, Pallas kernels, per_device(): pl.pallas_call(project_kernel, out_shape=[pltpu.VMEM((2, u, v), bf16), pl...  4.67 us
    ppermute x5, starting transfers between devices, swap(): lax.ppermute(x, axis, [(i, i ^ mask) for i in range(lax.axis_size(axis))])  4.14 us
    ppermute x2, waiting for transfers between devices, per_device(): lax.ppermute(x, ('depth', 'tile'), p)  3.1 us
    pallas_call x1, Pallas kernels, per_device(): pl.pallas_call(back_kernel, out_shape=[jax.ShapeDtypeStruct(volume.shape,...  3.02 us
    ppermute x2, starting transfers between devices, per_device(): lax.ppermute(x, ('depth', 'tile'), p)  3.02 us
    ppermute x2, starting transfers between devices, per_device(): beside = [lax.ppermute(whole, ('depth', 'tile'), p) for p in pairs[::-1]]  2.76 us
    ppermute x2, waiting for transfers between devices, per_device(): beside = [lax.ppermute(whole, ('depth', 'tile'), p) for p in pairs[::-1]]  2.6 us
  transfers between devices with their start and end apart: 9, of which 7 were waited for; matrix products, arithmetic and copies ran while one was open for 0% of the time, Pallas kernels for 6%

profile of v4, /device:TPU:0, one launch (start us, length us, event | category | flops | bytes accessed | tf_op | source)
XLA Modules:
  0.0 31.1 jit_solution(5556110141568360402)
XLA Ops:
  0.6 4.7 %project.1 = (bf16[2,384,512]{2,1,0:T(8,128)(2,1)S(1)}, f32[3,64,384]{2,1,0:T(8,128)S(1)}, f32[128,384]{1,0:T(8,128)S(1)}, f32[2,4,192,256]{3,2,1,0:T(8,128)S(1)...) custom-call(f32[2,128,384]{2,1,0:T(8,128)} %volume.1, ...), custom_call_target="tpu_custom_call" | custom-call | tf_op jit(solution)/shard_map/project/pallas_call | solution.py:323
  5.3 0.5 %collective-permute-start = (f32[3,64,384]{2,1,0:T(8,128)S(1)}, f32[3,64,384]{2,1,0:T(8,128)S(1)}, u32[]{:S(2)}, u32[]{:S(2)}) collective-permute-start(f32[3,64,384]{2,1,0:T(8,128)S(1)} %get-tuple-element.19), channel_id=1, source_target_pairs={{0,4},{4,0},{8,12},{12,8},{16,20},{20,16},{24,28},{28,24},{1,5},{5... | collective-permute-start | bytes 884744 | tf_op jit(solution)/shard_map/ppermute | solution.py:277
  5.8 0.8 %keep.1 = f32[3,64,384]{2,1,0:T(8,128)S(1)} custom-call(bf16[2,384,512]{2,1,0:T(8,128)(2,1)S(1)} %get-tuple-element.15.spectrum, bf16[2,384,384]{2,1,0:T(8,128)(2,1)S(1)} %get-tuple-element.16.rt, bf16[2,512,384]{2,1,0:T(8,128)(2,1)S(1)} %get-tuple-element.17.ct, f32[128,384]{1,0:T(8,128)S(1)} %get-tuple-element.18.measured), custom_call_target="tpu_custom_call" | custom-call | flops 452984832 | tf_op jit(solution)/shard_map/keep/pallas_call | solution.py:348
  6.7 0.4 %collective-permute-done.received = f32[3,64,384]{2,1,0:T(8,128)S(1)} collective-permute-done((f32[3,64,384]{2,1,0:T(8,128)S(1)}, f32[3,64,384]{2,1,0:T(8,128)S(1)}, u32[]{:S(2)}, u32[]{:S(2)}) %collective-permute-start) | collective-permute-done | bytes 294944 | tf_op jit(solution)/shard_map/ppermute | solution.py:277
  7.1 3.0 %collective-permute-start.1 = (f32[64,384]{1,0:T(8,128)S(1)}, f32[64,384]{1,0:T(8,128)S(1)}, u32[]{:S(2)}, u32[]{:S(2)}) collective-permute-start(f32[64,384]{1,0:T(8,128)S(1)} %get-tuple-element.21), channel_id=1, source_target_pairs={{0,1},{1,0},{2,3},{3,2},{4,5},{5,4},{6,7},{7,6},{8,9},{9,8},{10,11... | collective-permute-start | bytes 294920 | tf_op jit(solution)/shard_map/ppermute | solution.py:359
  10.1 0.0 collective-permute-start.2
  10.1 3.1 %collective-permute-done.1.a = f32[64,384]{1,0:T(8,128)S(1)} collective-permute-done((f32[64,384]{1,0:T(8,128)S(1)}, f32[64,384]{1,0:T(8,128)S(1)}, u32[]{:S(2)}, u32[]{:S(2)}) %collective-permute-start.1) | collective-permute-done | bytes 98336 | tf_op jit(solution)/shard_map/ppermute | solution.py:359
  13.2 0.0 collective-permute-done.2.b
  13.2 0.0 copy-start
  13.2 2.7 %collective-permute-start.5 = (f32[64,384]{1,0:T(8,128)S(1)}, f32[64,384]{1,0:T(8,128)S(1)}, u32[]{:S(2)}, u32[]{:S(2)}) collective-permute-start(f32[64,384]{1,0:T(8,128)S(1)} %sum_tiles.1.refs_0_), channel_id=1, source_target_pairs={{0,24},{4,28},{8,16},{12,20},{16,8},{20,12},{24,0},{28,4},{1,25},{... | collective-permute-start | bytes 294920 | tf_op jit(solution)/shard_map/ppermute | solution.py:277
  15.9 0.5 %collective-permute-start.4 = (f32[64,384]{1,0:T(8,128)S(1)}, f32[64,384]{1,0:T(8,128)S(1)}, u32[]{:S(2)}, u32[]{:S(2)}) collective-permute-start(f32[64,384]{1,0:T(8,128)S(1)} %sum_tiles.1.refs_0_), channel_id=1, source_target_pairs={{0,16},{4,20},{8,24},{12,28},{16,0},{20,4},{24,8},{28,12},{1,17},{... | collective-permute-start | bytes 294920 | tf_op jit(solution)/shard_map/ppermute | solution.py:277
  16.4 0.4 %collective-permute-start.3 = (f32[64,384]{1,0:T(8,128)S(1)}, f32[64,384]{1,0:T(8,128)S(1)}, u32[]{:S(2)}, u32[]{:S(2)}) collective-permute-start(f32[64,384]{1,0:T(8,128)S(1)} %sum_tiles.1.refs_0_), channel_id=1, source_target_pairs={{0,8},{4,12},{8,0},{12,4},{16,24},{20,28},{24,16},{28,20},{1,9},{5... | collective-permute-start | bytes 294920 | tf_op jit(solution)/shard_map/ppermute | solution.py:277
  16.8 2.2 %collective-permute-done.5.refs_3_ = f32[64,384]{1,0:T(8,128)S(1)} collective-permute-done((f32[64,384]{1,0:T(8,128)S(1)}, f32[64,384]{1,0:T(8,128)S(1)}, u32[]{:S(2)}, u32[]{:S(2)}) %collective-permute-start.5) | collective-permute-done | bytes 98336 | tf_op jit(solution)/shard_map/ppermute | solution.py:277
  18.9 1.7 %collective-permute-done.4.refs_2_ = f32[64,384]{1,0:T(8,128)S(1)} collective-permute-done((f32[64,384]{1,0:T(8,128)S(1)}, f32[64,384]{1,0:T(8,128)S(1)}, u32[]{:S(2)}, u32[]{:S(2)}) %collective-permute-start.4) | collective-permute-done | bytes 98336 | tf_op jit(solution)/shard_map/ppermute | solution.py:277
  20.7 0.3 %collective-permute-done.3.refs_1_ = f32[64,384]{1,0:T(8,128)S(1)} collective-permute-done((f32[64,384]{1,0:T(8,128)S(1)}, f32[64,384]{1,0:T(8,128)S(1)}, u32[]{:S(2)}, u32[]{:S(2)}) %collective-permute-start.3) | collective-permute-done | bytes 98336 | tf_op jit(solution)/shard_map/ppermute | solution.py:277
  21.0 2.8 %collective-permute-start.7 = (f32[64,384]{1,0:T(8,128)S(1)}, f32[64,384]{1,0:T(8,128)S(1)}, u32[]{:S(2)}, u32[]{:S(2)}) collective-permute-start(f32[64,384]{1,0:T(8,128)S(1)} %sum_chips.1.refs_0_), channel_id=1, source_target_pairs={{0,1},{1,0},{2,3},{3,2},{4,5},{5,4},{6,7},{7,6},{8,9},{9,8},{10,11... | collective-permute-start | bytes 294920 | tf_op jit(solution)/shard_map/ppermute | solution.py:363
  23.8 0.0 collective-permute-start.6
  23.8 2.6 %collective-permute-done.7.refs_2_ = f32[64,384]{1,0:T(8,128)S(1)} collective-permute-done((f32[64,384]{1,0:T(8,128)S(1)}, f32[64,384]{1,0:T(8,128)S(1)}, u32[]{:S(2)}, u32[]{:S(2)}) %collective-permute-start.7) | collective-permute-done | bytes 98336 | tf_op jit(solution)/shard_map/ppermute | solution.py:363
  26.4 0.0 collective-permute-done.6.refs_1_
  26.4 0.1 collective-permute-start.8
  26.5 0.9 %near.1 = (f32[384,512]{1,0:T(8,128)S(1)}, bf16[2,384,192]{2,1,0:T(8,128)(2,1)S(1)}) custom-call(f32[3,64,384]{2,1,0:T(8,128)S(1)} %stack.1.mine, bf16[2,384,384]{2,1,0:T(8,128)(2,1)S(1)} %get-tuple-element.23.rf, bf16[2,384,512]{2,1,0:T(8,128)(2,1)S(1)} %get-tuple-element.24.cf), custom_call_target="tpu_custom_call" | custom-call | flops 301989888 | tf_op jit(solution)/shard_map/near/pallas_call | solution.py:366
  27.4 0.7 %collective-permute-done.8.other = f32[3,64,384]{2,1,0:T(8,128)S(1)} collective-permute-done((f32[3,64,384]{2,1,0:T(8,128)S(1)}, f32[3,64,384]{2,1,0:T(8,128)S(1)}, u32[]{:S(2)}, u32[]{:S(2)}) %collective-permute-start.8) | collective-permute-done | bytes 294944 | tf_op jit(solution)/shard_map/ppermute | solution.py:277
  28.1 0.0 copy-done
  28.1 3.0 %back.1 = (f32[2,128,384]{2,1,0:T(8,128)}, f32[128,384]{1,0:T(8,128)}) custom-call(f32[2,128,384]{2,1,0:T(8,128)S(1)} %copy-done, f32[3,64,384]{2,1,0:T(8,128)S(1)} %stack.1.mine, f32[3,64,384]{2,1,0:T(8,128)S(1)} %collective-permute-done.8.other, bf16[2,384,192]{2,1,0:T(8,128)(2,1)S(1)} %get-tuple-element.25.table, ...), custom_call_target="tpu_custom_call" | custom-call | tf_op jit(solution)/shard_map/back/pallas_call | solution.py:375
  (4 shorter events, 0.1 us)
Async XLA Ops:
  5.3 1.7 %collective-permute-start = (f32[3,64,384]{2,1,0:T(8,128)S(1)}, f32[3,64,384]{2,1,0:T(8,128)S(1)}, u32[]{:S(2)}, u32[]{:S(2)}) collective-permute-start(f32[3,64,384]{2,1,0:T(8,128)S(1)} %get-tuple-element.19), channel_id=1, source_target_pairs={{0,4},{4,0},{8,12},{12,8},{16,20},{20,16},{24,28},{28,24},{1,5},{5... | collective-permute-start | bytes 884744 | tf_op jit(solution)/shard_map/ppermute | solution.py:277
  7.1 6.1 %collective-permute-start.1 = (f32[64,384]{1,0:T(8,128)S(1)}, f32[64,384]{1,0:T(8,128)S(1)}, u32[]{:S(2)}, u32[]{:S(2)}) collective-permute-start(f32[64,384]{1,0:T(8,128)S(1)} %get-tuple-element.21), channel_id=1, source_target_pairs={{0,1},{1,0},{2,3},{3,2},{4,5},{5,4},{6,7},{7,6},{8,9},{9,8},{10,11... | collective-permute-start | bytes 294920 | tf_op jit(solution)/shard_map/ppermute | solution.py:359
  10.1 3.1 %collective-permute-start.2 = (f32[64,384]{1,0:T(8,128)S(1)}, f32[64,384]{1,0:T(8,128)S(1)}, u32[]{:S(2)}, u32[]{:S(2)}) collective-permute-start(f32[64,384]{1,0:T(8,128)S(1)} %get-tuple-element.22), channel_id=1, source_target_pairs={{0,4},{1,2},{2,1},{3,7},{4,0},{5,6},{6,5},{7,3},{8,12},{9,10},{10,... | collective-permute-start | bytes 294920 | tf_op jit(solution)/shard_map/ppermute | solution.py:359
  13.2 14.9 %copy-start = (f32[2,128,384]{2,1,0:T(8,128)S(1)}, f32[2,128,384]{2,1,0:T(8,128)}, u32[]{:S(2)}) copy-start(f32[2,128,384]{2,1,0:T(8,128)} %volume.1) | copy-start | bytes 1179652
  13.2 5.7 %collective-permute-start.5 = (f32[64,384]{1,0:T(8,128)S(1)}, f32[64,384]{1,0:T(8,128)S(1)}, u32[]{:S(2)}, u32[]{:S(2)}) collective-permute-start(f32[64,384]{1,0:T(8,128)S(1)} %sum_tiles.1.refs_0_), channel_id=1, source_target_pairs={{0,24},{4,28},{8,16},{12,20},{16,8},{20,12},{24,0},{28,4},{1,25},{... | collective-permute-start | bytes 294920 | tf_op jit(solution)/shard_map/ppermute | solution.py:277
  15.9 4.8 %collective-permute-start.4 = (f32[64,384]{1,0:T(8,128)S(1)}, f32[64,384]{1,0:T(8,128)S(1)}, u32[]{:S(2)}, u32[]{:S(2)}) collective-permute-start(f32[64,384]{1,0:T(8,128)S(1)} %sum_tiles.1.refs_0_), channel_id=1, source_target_pairs={{0,16},{4,20},{8,24},{12,28},{16,0},{20,4},{24,8},{28,12},{1,17},{... | collective-permute-start | bytes 294920 | tf_op jit(solution)/shard_map/ppermute | solution.py:277
  16.4 4.6 %collective-permute-start.3 = (f32[64,384]{1,0:T(8,128)S(1)}, f32[64,384]{1,0:T(8,128)S(1)}, u32[]{:S(2)}, u32[]{:S(2)}) collective-permute-start(f32[64,384]{1,0:T(8,128)S(1)} %sum_tiles.1.refs_0_), channel_id=1, source_target_pairs={{0,8},{4,12},{8,0},{12,4},{16,24},{20,28},{24,16},{28,20},{1,9},{5... | collective-permute-start | bytes 294920 | tf_op jit(solution)/shard_map/ppermute | solution.py:277
  21.0 5.4 %collective-permute-start.7 = (f32[64,384]{1,0:T(8,128)S(1)}, f32[64,384]{1,0:T(8,128)S(1)}, u32[]{:S(2)}, u32[]{:S(2)}) collective-permute-start(f32[64,384]{1,0:T(8,128)S(1)} %sum_chips.1.refs_0_), channel_id=1, source_target_pairs={{0,1},{1,0},{2,3},{3,2},{4,5},{5,4},{6,7},{7,6},{8,9},{9,8},{10,11... | collective-permute-start | bytes 294920 | tf_op jit(solution)/shard_map/ppermute | solution.py:363
  23.8 2.6 %collective-permute-start.6 = (f32[64,384]{1,0:T(8,128)S(1)}, f32[64,384]{1,0:T(8,128)S(1)}, u32[]{:S(2)}, u32[]{:S(2)}) collective-permute-start(f32[64,384]{1,0:T(8,128)S(1)} %sum_chips.1.refs_0_), channel_id=1, source_target_pairs={{0,4},{1,2},{2,1},{3,7},{4,0},{5,6},{6,5},{7,3},{8,12},{9,10},{10,... | collective-permute-start | bytes 294920 | tf_op jit(solution)/shard_map/ppermute | solution.py:363
  26.4 1.6 %collective-permute-start.8 = (f32[3,64,384]{2,1,0:T(8,128)S(1)}, f32[3,64,384]{2,1,0:T(8,128)S(1)}, u32[]{:S(2)}, u32[]{:S(2)}) collective-permute-start(f32[3,64,384]{2,1,0:T(8,128)S(1)} %stack.1.mine), channel_id=1, source_target_pairs={{0,4},{4,0},{8,12},{12,8},{16,20},{20,16},{24,28},{28,24},{1,5},{5... | collective-permute-start | bytes 884744 | tf_op jit(solution)/shard_map/ppermute | solution.py:277

commit v5 on v4

--- a/solution.py
+++ b/solution.py
@@ -217,45 +217,54 @@
     refs[-1][...] = tree([x[...] for x in refs[:-1]])
 
 
-def stack_kernel(*refs):
-    for m, x in enumerate(refs[:-1]):
-        refs[-1][m] = x[...]
-
-
-def by_core(x):
-    half = x.shape[-1] // 6
-    even = lax.axis_index("depth") % 2 == 0
-    first, second = (
-        jnp.concatenate(
-            [x[..., (2 * s + j) * half : (2 * s + j + 1) * half] for s in range(3)], axis=-1
-        )
-        for j in (0, 1)
-    )
-    return jnp.where(even, first, second), jnp.where(even, second, first)
-
-
-def row_part(strips, table, cf):
+def stack_kernel(whole, whole_other, b, a, mine, halo):
+    for m, x in enumerate((whole, whole_other, b, a)):
+        mine[m] = x[...]
+    halo[0] = b[...]
+    halo[1] = a[...]
+
+
+def beside_first(b, a):
     even = lax.axis_index("tile") % 2 == 0
     first, second = paired()
-    b, a = jnp.where(second, strips[1], 0.0), jnp.where(first, strips[2], 0.0)
-    x = jnp.concatenate([jnp.where(even, b, a), strips[0], jnp.where(even, a, b)], axis=0)
-    return table_times(table[0], table[1], times_table(x, cf[0], cf[1]))
+    b, a = jnp.where(second, b, 0.0), jnp.where(first, a, 0.0)
+    return jnp.concatenate([jnp.where(even, b, a), jnp.where(even, a, b)], axis=0)
+
+
+def own_strip(whole, whole_other):
+    even = lax.axis_index("depth") % 2 == 0
+    return jnp.concatenate(
+        [jnp.where(even, whole, whole_other), jnp.where(even, whole_other, whole)], axis=0
+    )
+
+
+def by_core(x):
+    rows = x.shape[-1] // 3
+    half = rows // 2
+    even = lax.axis_index("depth") % 2 == 0
+    above, below = x[..., :rows], x[..., 2 * rows :]
+    first = jnp.concatenate([above[..., :half], below[..., :half]], axis=-1)
+    second = jnp.concatenate([above[..., half:], below[..., half:]], axis=-1)
+    return jnp.where(even, first, second), jnp.where(even, second, first)
 
 
 def near_kernel(mine, rf, cf, partial, other_table):
+    rows = rf.shape[2] // 3
     tables = [by_core(rf[i]) for i in range(2)]
-    partial[...] = row_part(mine, [x for x, _ in tables], cf)
+    table = [
+        jnp.concatenate([rf[i, :, rows : 2 * rows], tables[i][0]], axis=1) for i in range(2)
+    ]
+    x = jnp.concatenate([own_strip(mine[0], mine[1]), beside_first(mine[2], mine[3])], axis=0)
+    partial[...] = table_times(table[0], table[1], times_table(x, cf[0], cf[1]))
     for i in range(2):
         other_table[i] = tables[i][1]
 
 
 def back_kernel(volume, mine, other, table, partial, optic, rt, cf, ct, volume_next, residual):
     planes, rows, width = volume.shape
-    half = rows // 2
-    even = lax.axis_index("depth") % 2 == 0
-    residual[:half] = jnp.where(even, mine[0], other[0])
-    residual[half:] = jnp.where(even, other[0], mine[0])
-    r = row_terms(partial[...] + row_part(other, table, cf))
+    residual[...] = own_strip(mine[0], mine[1])
+    x = times_table(beside_first(other[0], other[1]), cf[0], cf[1])
+    r = row_terms(partial[...] + table_times(table[0], table[1], x))
     mixed = []
     for i in range(planes):
         h = [optic[i, j] for j in range(4)]
@@ -361,11 +370,14 @@
     others = [swap(part, "depth", 2 * m) for m in range(1, chips)]
     (whole,) = local(sum_kernel, "sum_chips", [piece], part, *others)
     beside = [lax.ppermute(whole, ("depth", "tile"), p) for p in pairs[::-1]]
-    (gathered,) = local(stack_kernel, "stack", [three], whole, *beside)
-    other = swap(gathered, "depth", 1)
+    whole_other = swap(whole, "depth", 1)
+    gathered, halo = local(
+        stack_kernel, "stack", [(4,) + piece, (2,) + piece], whole, whole_other, *beside
+    )
+    other = swap(halo, "depth", 1)
     partial, table = pl.pallas_call(
         near_kernel,
-        out_shape=[pltpu.VMEM((u, v), f32), pltpu.VMEM((2, u, 3 * rows // 2), bf16)],
+        out_shape=[pltpu.VMEM((u, v), f32), pltpu.VMEM((2, u, rows), bf16)],
         in_specs=[VMEM] * 3,
         out_specs=[VMEM] * 2,
         compiler_params=PARAMS,

time: 31.2 us -> 31 us (level)
  waiting for transfers between devices: 11 us -> 10.3 us
  starting transfers between devices: 9.92 us -> 10.4 us
    ppermute x2, waiting for transfers between devices: 2.6 us -> 2.09 us  [per_device(): beside = [lax.ppermute(whole, ('depth', 'tile'), p) for p in pairs[::-1]]]
    ppermute x5 -> x6, starting transfers between devices: 4.14 us -> 4.65 us  [swap(): lax.ppermute(x, axis, [(i, i ^ mask) for i in range(lax.axis_size(axis))])]
    ppermute x5 -> x6, waiting for transfers between devices: 5.27 us -> 5.1 us  [swap(): lax.ppermute(x, axis, [(i, i ^ mask) for i in range(lax.axis_size(axis))])]
  transfers between devices with their start and end apart: 9 -> 10, of which waited for: 7 -> 7; matrix products, arithmetic and copies ran while one was open for 0% -> 0% of each run, Pallas kernels for 6% -> 6%
where the time goes in v5:
time: 31 us; the launch traced here: 30.8 us
  starting transfers between devices  10.4 us (34%)
  waiting for transfers between devices  10.3 us (33%)
  Pallas kernels  9.39 us (30%)
  between operations  0.69 us (2%)
    ppermute x6, waiting for transfers between devices, swap(): lax.ppermute(x, axis, [(i, i ^ mask) for i in range(lax.axis_size(axis))])  5.1 us
    pallas_call x1, Pallas kernels, per_device(): pl.pallas_call(project_kernel, out_shape=[pltpu.VMEM((2, u, v), bf16), pl...  4.67 us
    ppermute x6, starting transfers between devices, swap(): lax.ppermute(x, axis, [(i, i ^ mask) for i in range(lax.axis_size(axis))])  4.65 us
    ppermute x2, waiting for transfers between devices, per_device(): lax.ppermute(x, ('depth', 'tile'), p)  3.1 us
    ppermute x2, starting transfers between devices, per_device(): lax.ppermute(x, ('depth', 'tile'), p)  3.02 us
    pallas_call x1, Pallas kernels, per_device(): pl.pallas_call(back_kernel, out_shape=[jax.ShapeDtypeStruct(volume.shape,...  2.84 us
    ppermute x2, starting transfers between devices, per_device(): beside = [lax.ppermute(whole, ('depth', 'tile'), p) for p in pairs[::-1]]  2.77 us
    ppermute x2, waiting for transfers between devices, per_device(): beside = [lax.ppermute(whole, ('depth', 'tile'), p) for p in pairs[::-1]]  2.09 us
  transfers between devices with their start and end apart: 10, of which 7 were waited for; matrix products, arithmetic and copies ran while one was open for 0% of the time, Pallas kernels for 6%

profile of v5, /device:TPU:0, one launch (start us, length us, event | category | flops | bytes accessed | tf_op | source)
XLA Modules:
  0.0 30.8 jit_solution(3521064936520033971)
XLA Ops:
  0.6 4.7 %project.1 = (bf16[2,384,512]{2,1,0:T(8,128)(2,1)S(1)}, f32[3,64,384]{2,1,0:T(8,128)S(1)}, f32[128,384]{1,0:T(8,128)S(1)}, f32[2,4,192,256]{3,2,1,0:T(8,128)S(1)...) custom-call(f32[2,128,384]{2,1,0:T(8,128)} %volume.1, ...), custom_call_target="tpu_custom_call" | custom-call | tf_op jit(solution)/shard_map/project/pallas_call | solution.py:332
  5.3 0.5 %collective-permute-start = (f32[3,64,384]{2,1,0:T(8,128)S(1)}, f32[3,64,384]{2,1,0:T(8,128)S(1)}, u32[]{:S(2)}, u32[]{:S(2)}) collective-permute-start(f32[3,64,384]{2,1,0:T(8,128)S(1)} %get-tuple-element.21), channel_id=1, source_target_pairs={{0,4},{4,0},{8,12},{12,8},{16,20},{20,16},{24,28},{28,24},{1,5},{5... | collective-permute-start | bytes 884744 | tf_op jit(solution)/shard_map/ppermute | solution.py:286
  5.8 0.8 %keep.1 = f32[3,64,384]{2,1,0:T(8,128)S(1)} custom-call(bf16[2,384,512]{2,1,0:T(8,128)(2,1)S(1)} %get-tuple-element.17.spectrum, bf16[2,384,384]{2,1,0:T(8,128)(2,1)S(1)} %get-tuple-element.18.rt, bf16[2,512,384]{2,1,0:T(8,128)(2,1)S(1)} %get-tuple-element.19.ct, f32[128,384]{1,0:T(8,128)S(1)} %get-tuple-element.20.measured), custom_call_target="tpu_custom_call" | custom-call | flops 452984832 | tf_op jit(solution)/shard_map/keep/pallas_call | solution.py:357
  6.7 0.4 %collective-permute-done.received = f32[3,64,384]{2,1,0:T(8,128)S(1)} collective-permute-done((f32[3,64,384]{2,1,0:T(8,128)S(1)}, f32[3,64,384]{2,1,0:T(8,128)S(1)}, u32[]{:S(2)}, u32[]{:S(2)}) %collective-permute-start) | collective-permute-done | bytes 294944 | tf_op jit(solution)/shard_map/ppermute | solution.py:286
  7.1 0.0 copy-start
  7.1 3.0 %collective-permute-start.1 = (f32[64,384]{1,0:T(8,128)S(1)}, f32[64,384]{1,0:T(8,128)S(1)}, u32[]{:S(2)}, u32[]{:S(2)}) collective-permute-start(f32[64,384]{1,0:T(8,128)S(1)} %get-tuple-element.23), channel_id=1, source_target_pairs={{0,1},{1,0},{2,3},{3,2},{4,5},{5,4},{6,7},{7,6},{8,9},{9,8},{10,11... | collective-permute-start | bytes 294920 | tf_op jit(solution)/shard_map/ppermute | solution.py:368
  10.1 0.0 collective-permute-start.2
  10.1 3.1 %collective-permute-done.1.a = f32[64,384]{1,0:T(8,128)S(1)} collective-permute-done((f32[64,384]{1,0:T(8,128)S(1)}, f32[64,384]{1,0:T(8,128)S(1)}, u32[]{:S(2)}, u32[]{:S(2)}) %collective-permute-start.1) | collective-permute-done | bytes 98336 | tf_op jit(solution)/shard_map/ppermute | solution.py:368
  13.2 0.0 collective-permute-done.2.b
  13.2 2.7 %collective-permute-start.5 = (f32[64,384]{1,0:T(8,128)S(1)}, f32[64,384]{1,0:T(8,128)S(1)}, u32[]{:S(2)}, u32[]{:S(2)}) collective-permute-start(f32[64,384]{1,0:T(8,128)S(1)} %sum_tiles.1.refs_0_), channel_id=1, source_target_pairs={{0,24},{4,28},{8,16},{12,20},{16,8},{20,12},{24,0},{28,4},{1,25},{... | collective-permute-start | bytes 294920 | tf_op jit(solution)/shard_map/ppermute | solution.py:286
  15.9 0.5 %collective-permute-start.4 = (f32[64,384]{1,0:T(8,128)S(1)}, f32[64,384]{1,0:T(8,128)S(1)}, u32[]{:S(2)}, u32[]{:S(2)}) collective-permute-start(f32[64,384]{1,0:T(8,128)S(1)} %sum_tiles.1.refs_0_), channel_id=1, source_target_pairs={{0,16},{4,20},{8,24},{12,28},{16,0},{20,4},{24,8},{28,12},{1,17},{... | collective-permute-start | bytes 294920 | tf_op jit(solution)/shard_map/ppermute | solution.py:286
  16.4 0.4 %collective-permute-start.3 = (f32[64,384]{1,0:T(8,128)S(1)}, f32[64,384]{1,0:T(8,128)S(1)}, u32[]{:S(2)}, u32[]{:S(2)}) collective-permute-start(f32[64,384]{1,0:T(8,128)S(1)} %sum_tiles.1.refs_0_), channel_id=1, source_target_pairs={{0,8},{4,12},{8,0},{12,4},{16,24},{20,28},{24,16},{28,20},{1,9},{5... | collective-permute-start | bytes 294920 | tf_op jit(solution)/shard_map/ppermute | solution.py:286
  16.8 2.2 %collective-permute-done.5.refs_3_ = f32[64,384]{1,0:T(8,128)S(1)} collective-permute-done((f32[64,384]{1,0:T(8,128)S(1)}, f32[64,384]{1,0:T(8,128)S(1)}, u32[]{:S(2)}, u32[]{:S(2)}) %collective-permute-start.5) | collective-permute-done | bytes 98336 | tf_op jit(solution)/shard_map/ppermute | solution.py:286
  18.9 1.7 %collective-permute-done.4.refs_2_ = f32[64,384]{1,0:T(8,128)S(1)} collective-permute-done((f32[64,384]{1,0:T(8,128)S(1)}, f32[64,384]{1,0:T(8,128)S(1)}, u32[]{:S(2)}, u32[]{:S(2)}) %collective-permute-start.4) | collective-permute-done | bytes 98336 | tf_op jit(solution)/shard_map/ppermute | solution.py:286
  20.7 0.3 %collective-permute-done.3.refs_1_ = f32[64,384]{1,0:T(8,128)S(1)} collective-permute-done((f32[64,384]{1,0:T(8,128)S(1)}, f32[64,384]{1,0:T(8,128)S(1)}, u32[]{:S(2)}, u32[]{:S(2)}) %collective-permute-start.3) | collective-permute-done | bytes 98336 | tf_op jit(solution)/shard_map/ppermute | solution.py:286
  21.0 2.8 %collective-permute-start.8 = (f32[64,384]{1,0:T(8,128)S(1)}, f32[64,384]{1,0:T(8,128)S(1)}, u32[]{:S(2)}, u32[]{:S(2)}) collective-permute-start(f32[64,384]{1,0:T(8,128)S(1)} %sum_chips.1.whole), channel_id=1, source_target_pairs={{0,1},{1,0},{2,3},{3,2},{4,5},{5,4},{6,7},{7,6},{8,9},{9,8},{10,11... | collective-permute-start | bytes 294920 | tf_op jit(solution)/shard_map/ppermute | solution.py:372
  23.8 0.0 collective-permute-start.7
  23.8 0.5 %collective-permute-start.6 = (f32[64,384]{1,0:T(8,128)S(1)}, f32[64,384]{1,0:T(8,128)S(1)}, u32[]{:S(2)}, u32[]{:S(2)}) collective-permute-start(f32[64,384]{1,0:T(8,128)S(1)} %sum_chips.1.whole), channel_id=1, source_target_pairs={{0,4},{4,0},{8,12},{12,8},{16,20},{20,16},{24,28},{28,24},{1,5},{5... | collective-permute-start | bytes 294920 | tf_op jit(solution)/shard_map/ppermute | solution.py:286
  24.3 2.1 %collective-permute-done.8.a = f32[64,384]{1,0:T(8,128)S(1)} collective-permute-done((f32[64,384]{1,0:T(8,128)S(1)}, f32[64,384]{1,0:T(8,128)S(1)}, u32[]{:S(2)}, u32[]{:S(2)}) %collective-permute-start.8) | collective-permute-done | bytes 98336 | tf_op jit(solution)/shard_map/ppermute | solution.py:372
  26.4 0.0 collective-permute-done.7.b
  26.4 0.0 collective-permute-done.6.whole_other
  26.5 0.1 collective-permute-start.9
  26.5 0.9 %near.1 = (f32[384,512]{1,0:T(8,128)S(1)}, bf16[2,384,128]{2,1,0:T(8,128)(2,1)S(1)}) custom-call(f32[4,64,384]{2,1,0:T(8,128)S(1)} %get-tuple-element.25.mine, bf16[2,384,384]{2,1,0:T(8,128)(2,1)S(1)} %get-tuple-element.27.rf, bf16[2,384,512]{2,1,0:T(8,128)(2,1)S(1)} %get-tuple-element.28.cf), custom_call_target="tpu_custom_call" | custom-call | flops 301989888 | tf_op jit(solution)/shard_map/near/pallas_call | solution.py:378
  27.5 0.5 %collective-permute-done.9.other = f32[2,64,384]{2,1,0:T(8,128)S(1)} collective-permute-done((f32[2,64,384]{2,1,0:T(8,128)S(1)}, f32[2,64,384]{2,1,0:T(8,128)S(1)}, u32[]{:S(2)}, u32[]{:S(2)}) %collective-permute-start.9) | collective-permute-done | bytes 196640 | tf_op jit(solution)/shard_map/ppermute | solution.py:286
  28.0 0.0 copy-done
  28.0 2.8 %back.1 = (f32[2,128,384]{2,1,0:T(8,128)}, f32[128,384]{1,0:T(8,128)}) custom-call(f32[2,128,384]{2,1,0:T(8,128)S(1)} %copy-done, f32[4,64,384]{2,1,0:T(8,128)S(1)} %get-tuple-element.25.mine, f32[2,64,384]{2,1,0:T(8,128)S(1)} %collective-permute-done.9.other, bf16[2,384,128]{2,1,0:T(8,128)(2,1)S(1)} %get-tuple-element.29.table, ...), custom_call_target="tpu_custom_call" | custom-call | tf_op jit(solution)/shard_map/back/pallas_call | solution.py:387
  (4 shorter events, 0.1 us)
Async XLA Ops:
  5.3 1.7 %collective-permute-start = (f32[3,64,384]{2,1,0:T(8,128)S(1)}, f32[3,64,384]{2,1,0:T(8,128)S(1)}, u32[]{:S(2)}, u32[]{:S(2)}) collective-permute-start(f32[3,64,384]{2,1,0:T(8,128)S(1)} %get-tuple-element.21), channel_id=1, source_target_pairs={{0,4},{4,0},{8,12},{12,8},{16,20},{20,16},{24,28},{28,24},{1,5},{5... | collective-permute-start | bytes 884744 | tf_op jit(solution)/shard_map/ppermute | solution.py:286
  7.1 20.9 %copy-start = (f32[2,128,384]{2,1,0:T(8,128)S(1)}, f32[2,128,384]{2,1,0:T(8,128)}, u32[]{:S(2)}) copy-start(f32[2,128,384]{2,1,0:T(8,128)} %volume.1) | copy-start | bytes 1179652
  7.1 6.1 %collective-permute-start.1 = (f32[64,384]{1,0:T(8,128)S(1)}, f32[64,384]{1,0:T(8,128)S(1)}, u32[]{:S(2)}, u32[]{:S(2)}) collective-permute-start(f32[64,384]{1,0:T(8,128)S(1)} %get-tuple-element.23), channel_id=1, source_target_pairs={{0,1},{1,0},{2,3},{3,2},{4,5},{5,4},{6,7},{7,6},{8,9},{9,8},{10,11... | collective-permute-start | bytes 294920 | tf_op jit(solution)/shard_map/ppermute | solution.py:368
  10.1 3.1 %collective-permute-start.2 = (f32[64,384]{1,0:T(8,128)S(1)}, f32[64,384]{1,0:T(8,128)S(1)}, u32[]{:S(2)}, u32[]{:S(2)}) collective-permute-start(f32[64,384]{1,0:T(8,128)S(1)} %get-tuple-element.24), channel_id=1, source_target_pairs={{0,4},{1,2},{2,1},{3,7},{4,0},{5,6},{6,5},{7,3},{8,12},{9,10},{10,... | collective-permute-start | bytes 294920 | tf_op jit(solution)/shard_map/ppermute | solution.py:368
  13.2 5.7 %collective-permute-start.5 = (f32[64,384]{1,0:T(8,128)S(1)}, f32[64,384]{1,0:T(8,128)S(1)}, u32[]{:S(2)}, u32[]{:S(2)}) collective-permute-start(f32[64,384]{1,0:T(8,128)S(1)} %sum_tiles.1.refs_0_), channel_id=1, source_target_pairs={{0,24},{4,28},{8,16},{12,20},{16,8},{20,12},{24,0},{28,4},{1,25},{... | collective-permute-start | bytes 294920 | tf_op jit(solution)/shard_map/ppermute | solution.py:286
  15.9 4.8 %collective-permute-start.4 = (f32[64,384]{1,0:T(8,128)S(1)}, f32[64,384]{1,0:T(8,128)S(1)}, u32[]{:S(2)}, u32[]{:S(2)}) collective-permute-start(f32[64,384]{1,0:T(8,128)S(1)} %sum_tiles.1.refs_0_), channel_id=1, source_target_pairs={{0,16},{4,20},{8,24},{12,28},{16,0},{20,4},{24,8},{28,12},{1,17},{... | collective-permute-start | bytes 294920 | tf_op jit(solution)/shard_map/ppermute | solution.py:286
  16.4 4.6 %collective-permute-start.3 = (f32[64,384]{1,0:T(8,128)S(1)}, f32[64,384]{1,0:T(8,128)S(1)}, u32[]{:S(2)}, u32[]{:S(2)}) collective-permute-start(f32[64,384]{1,0:T(8,128)S(1)} %sum_tiles.1.refs_0_), channel_id=1, source_target_pairs={{0,8},{4,12},{8,0},{12,4},{16,24},{20,28},{24,16},{28,20},{1,9},{5... | collective-permute-start | bytes 294920 | tf_op jit(solution)/shard_map/ppermute | solution.py:286
  21.0 5.4 %collective-permute-start.8 = (f32[64,384]{1,0:T(8,128)S(1)}, f32[64,384]{1,0:T(8,128)S(1)}, u32[]{:S(2)}, u32[]{:S(2)}) collective-permute-start(f32[64,384]{1,0:T(8,128)S(1)} %sum_chips.1.whole), channel_id=1, source_target_pairs={{0,1},{1,0},{2,3},{3,2},{4,5},{5,4},{6,7},{7,6},{8,9},{9,8},{10,11... | collective-permute-start | bytes 294920 | tf_op jit(solution)/shard_map/ppermute | solution.py:372
  23.8 2.6 %collective-permute-start.7 = (f32[64,384]{1,0:T(8,128)S(1)}, f32[64,384]{1,0:T(8,128)S(1)}, u32[]{:S(2)}, u32[]{:S(2)}) collective-permute-start(f32[64,384]{1,0:T(8,128)S(1)} %sum_chips.1.whole), channel_id=1, source_target_pairs={{0,4},{1,2},{2,1},{3,7},{4,0},{5,6},{6,5},{7,3},{8,12},{9,10},{10,... | collective-permute-start | bytes 294920 | tf_op jit(solution)/shard_map/ppermute | solution.py:372
  23.8 2.6 %collective-permute-start.6 = (f32[64,384]{1,0:T(8,128)S(1)}, f32[64,384]{1,0:T(8,128)S(1)}, u32[]{:S(2)}, u32[]{:S(2)}) collective-permute-start(f32[64,384]{1,0:T(8,128)S(1)} %sum_chips.1.whole), channel_id=1, source_target_pairs={{0,4},{4,0},{8,12},{12,8},{16,20},{20,16},{24,28},{28,24},{1,5},{5... | collective-permute-start | bytes 294920 | tf_op jit(solution)/shard_map/ppermute | solution.py:286
  26.5 1.5 %collective-permute-start.9 = (f32[2,64,384]{2,1,0:T(8,128)S(1)}, f32[2,64,384]{2,1,0:T(8,128)S(1)}, u32[]{:S(2)}, u32[]{:S(2)}) collective-permute-start(f32[2,64,384]{2,1,0:T(8,128)S(1)} %get-tuple-element.26), channel_id=1, source_target_pairs={{0,4},{4,0},{8,12},{12,8},{16,20},{20,16},{24,28},{28,24},{1,5},{5... | collective-permute-start | bytes 589832 | tf_op jit(solution)/shard_map/ppermute | solution.py:286

commit v6 on v5

--- a/solution.py
+++ b/solution.py
@@ -148,19 +148,23 @@
         )
         total = term if total is None else [a + b for a, b in zip(total, term)]
     spectrum[0], spectrum[1] = split(folded(total))
-    image = image_rows(spectrum, rt, ct, 1)
+    up, down = image_rows(spectrum, rt, ct, ((0, 1), (2, 1)))
+    send[0], send[1] = seen_part(up, 0), seen_part(down, -1)
     moves["measured"].wait()
-    finish(image, measured, send, 1)
-
-
-def image_rows(spectrum, rt, ct, other):
+
+
+def seen_part(strip, edge):
+    outside = edge % lax.axis_size("tile")
+    return strip * jnp.where(lax.axis_index("tile") == outside, 0.0, 1.0)
+
+
+def image_rows(spectrum, rt, ct, picks):
     rows = rt.shape[1] // 3
     half = rows // 2
-    start = ((lax.axis_index("depth") + other) % 2) * half
+    core = lax.axis_index("depth") % 2
+    starts = [s * rows + (core + other) % 2 * half for s, other in picks]
     table = [
-        jnp.concatenate(
-            [rt[i, pl.ds(pl.multiple_of(s * rows + start, half), half)] for s in range(3)], axis=0
-        )
+        jnp.concatenate([rt[i, pl.ds(pl.multiple_of(x, half), half)] for x in starts], axis=0)
         for i in range(2)
     ]
     mixed = jnp.dot(
@@ -168,27 +172,24 @@
         jnp.concatenate([spectrum[0], spectrum[1], spectrum[0]], axis=0),
         preferred_element_type=jnp.float32,
     )
-    return times_table(mixed, ct[0], ct[1])
-
-
-def finish(image, measured, out, other):
-    half = out.shape[1]
-    d, t = lax.axis_index("depth"), lax.axis_index("tile")
-    tiles = lax.axis_size("tile")
-    seen = jnp.where((d + other) % 2 == 0, measured[:half], measured[half:])
-    out[0] = image[:half] * jnp.where(t == 0, 0.0, 1.0)
-    out[1] = image[half : 2 * half] - seen * jnp.where(d == 0, 1.0, 0.0)
-    out[2] = image[2 * half :] * jnp.where(t == tiles - 1, 0.0, 1.0)
-
-
-def keep_kernel(spectrum, rt, ct, measured, keep):
-    finish(image_rows(spectrum, rt, ct, 0), measured, keep, 0)
-
-
-def split_kernel(keep, received, own, first, second):
+    image = times_table(mixed, ct[0], ct[1])
+    return [image[j * half : (j + 1) * half] for j in range(len(picks))]
+
+
+def keep_kernel(spectrum, rt, ct, measured, keep, own, own_send):
+    half = own.shape[0]
+    d = lax.axis_index("depth")
+    up, down, mine, other = image_rows(spectrum, rt, ct, ((0, 0), (2, 0), (1, 0), (1, 1)))
+    keep[0], keep[1] = seen_part(up, 0), seen_part(down, -1)
+    once = jnp.where(d == 0, 1.0, 0.0)
+    first, second = measured[:half] * once, measured[half:] * once
+    own[...] = mine - jnp.where(d % 2 == 0, first, second)
+    own_send[...] = other - jnp.where(d % 2 == 0, second, first)
+
+
+def split_kernel(keep, received, first, second):
     even = lax.axis_index("tile") % 2 == 0
-    up, down = keep[0] + received[0], keep[2] + received[2]
-    own[...] = keep[1] + received[1]
+    up, down = keep[0] + received[0], keep[1] + received[1]
     first[...] = jnp.where(even, down, up)
     second[...] = jnp.where(even, up, down)
 
@@ -208,9 +209,9 @@
     return first < n, jnp.logical_and(second >= 0, second < n)
 
 
-def tile_sum_kernel(own, a, b, out):
+def tile_sum_kernel(own, a, b, own_received, out):
     first, second = paired()
-    out[...] = own[...] + jnp.where(first, a[...], 0.0) + jnp.where(second, b[...], 0.0)
+    out[...] = own[...] + own_received[...] + jnp.where(first, a[...], 0.0) + jnp.where(second, b[...], 0.0)
 
 
 def sum_kernel(*refs):
@@ -325,7 +326,7 @@
     rf, cf, shift = (jnp.asarray(x) for x in tables(rows, width, half_width))
     u, v = rf.shape[1], cf.shape[2]
     piece = (rows // 2, width)
-    three = (3,) + piece
+    two = (2,) + piece
     kp = -(-(rows + half_width + 1) // 128) * 128
     spread = jnp.transpose(point_spread, (1, 0, 2))
     operands = (volume, spread, rf, cf, shift, measured)
@@ -333,7 +334,7 @@
         project_kernel,
         out_shape=[
             pltpu.VMEM((2, u, v), bf16),
-            pltpu.VMEM(three, f32),
+            pltpu.VMEM(two, f32),
             pltpu.VMEM(measured.shape, f32),
             pltpu.VMEM((planes, 4, u // 2, v // 2), f32),
             pltpu.VMEM(rf.shape, bf16),
@@ -354,25 +355,26 @@
         name="project",
     )(*[in_hbm(x) for x in operands])
     received = swap(send, "depth", 1)
-    (keep,) = pl.pallas_call(
+    keep, own, own_send = pl.pallas_call(
         keep_kernel,
-        out_shape=[pltpu.VMEM(three, f32)],
+        out_shape=[pltpu.VMEM(two, f32), pltpu.VMEM(piece, f32), pltpu.VMEM(piece, f32)],
         in_specs=[VMEM] * 4,
-        out_specs=[VMEM],
+        out_specs=[VMEM] * 3,
         compiler_params=PARAMS,
         cost_estimate=cost(9 * rows * v * (width + u)),
         name="keep",
     )(spectrum, rt, ct, seen)
     pairs = [pairing(n, tiles, start) for start in (0, 1)]
-    own, *sends = local(split_kernel, "split", [piece] * 3, keep, received)
+    sends = local(split_kernel, "split", [piece] * 2, keep, received)
+    own_send, *sends = lax.optimization_barrier((own_send, *sends))
     beside = [lax.ppermute(x, ("depth", "tile"), p) for x, p in zip(sends, pairs)]
-    (part,) = local(tile_sum_kernel, "sum_tiles", [piece], own, *beside)
+    (part,) = local(tile_sum_kernel, "sum_tiles", [piece], own, *beside, swap(own_send, "depth", 1))
     others = [swap(part, "depth", 2 * m) for m in range(1, chips)]
     (whole,) = local(sum_kernel, "sum_chips", [piece], part, *others)
     beside = [lax.ppermute(whole, ("depth", "tile"), p) for p in pairs[::-1]]
     whole_other = swap(whole, "depth", 1)
     gathered, halo = local(
-        stack_kernel, "stack", [(4,) + piece, (2,) + piece], whole, whole_other, *beside
+        stack_kernel, "stack", [(4,) + piece, two], whole, whole_other, *beside
     )
     other = swap(halo, "depth", 1)
     partial, table = pl.pallas_call(

time: 31 us -> 30.6 us (0.987)
  waiting for transfers between devices: 10.3 us -> 9.47 us
  starting transfers between devices: 10.4 us -> 10.9 us
    ppermute x6 -> x7, starting transfers between devices: 4.65 us -> 5.17 us  [swap(): lax.ppermute(x, axis, [(i, i ^ mask) for i in range(lax.axis_size(axis))])]
    ppermute x2, waiting for transfers between devices: 3.1 us -> 2.59 us  [per_device(): lax.ppermute(x, ('depth', 'tile'), p)]
    ppermute x6 -> x7, waiting for transfers between devices: 5.1 us -> 4.8 us  [swap(): lax.ppermute(x, axis, [(i, i ^ mask) for i in range(lax.axis_size(axis))])]
  transfers between devices with their start and end apart: 10 -> 11, of which waited for: 7 -> 7; matrix products, arithmetic and copies ran while one was open for 0% -> 0% of each run, Pallas kernels for 6% -> 6%
where the time goes in v6:
time: 30.6 us; the launch traced here: 30.5 us
  starting transfers between devices  10.9 us (36%)
  waiting for transfers between devices  9.47 us (31%)
  Pallas kernels  9.37 us (31%)
  between operations  0.69 us (2%)
    ppermute x7, starting transfers between devices, swap(): lax.ppermute(x, axis, [(i, i ^ mask) for i in range(lax.axis_size(axis))])  5.17 us
    ppermute x7, waiting for transfers between devices, swap(): lax.ppermute(x, axis, [(i, i ^ mask) for i in range(lax.axis_size(axis))])  4.8 us
    pallas_call x1, Pallas kernels, per_device(): pl.pallas_call(project_kernel, out_shape=[pltpu.VMEM((2, u, v), bf16), pl...  4.48 us
    ppermute x2, starting transfers between devices, per_device(): lax.ppermute(x, ('depth', 'tile'), p)  3.01 us
    pallas_call x1, Pallas kernels, per_device(): pl.pallas_call(back_kernel, out_shape=[jax.ShapeDtypeStruct(volume.shape,...  2.83 us
    ppermute x2, starting transfers between devices, per_device(): beside = [lax.ppermute(whole, ('depth', 'tile'), p) for p in pairs[::-1]]  2.77 us
    ppermute x2, waiting for transfers between devices, per_device(): lax.ppermute(x, ('depth', 'tile'), p)  2.59 us
    ppermute x2, waiting for transfers between devices, per_device(): beside = [lax.ppermute(whole, ('depth', 'tile'), p) for p in pairs[::-1]]  2.09 us
  transfers between devices with their start and end apart: 11, of which 7 were waited for; matrix products, arithmetic and copies ran while one was open for 0% of the time, Pallas kernels for 6%

profile of v6, /device:TPU:0, one launch (start us, length us, event | category | flops | bytes accessed | tf_op | source)
XLA Modules:
  0.0 30.5 jit_solution(6073974440740932518)
XLA Ops:
  0.6 4.5 %project.1 = (bf16[2,384,512]{2,1,0:T(8,128)(2,1)S(1)}, f32[2,64,384]{2,1,0:T(8,128)S(1)}, f32[128,384]{1,0:T(8,128)S(1)}, f32[2,4,192,256]{3,2,1,0:T(8,128)S(1)...) custom-call(f32[2,128,384]{2,1,0:T(8,128)} %volume.1, ...), custom_call_target="tpu_custom_call" | custom-call | tf_op jit(solution)/shard_map/project/pallas_call | solution.py:333
  5.1 0.5 %collective-permute-start = (f32[2,64,384]{2,1,0:T(8,128)S(1)}, f32[2,64,384]{2,1,0:T(8,128)S(1)}, u32[]{:S(2)}, u32[]{:S(2)}) collective-permute-start(f32[2,64,384]{2,1,0:T(8,128)S(1)} %get-tuple-element.29), channel_id=1, source_target_pairs={{0,4},{4,0},{8,12},{12,8},{16,20},{20,16},{24,28},{28,24},{1,5},{5... | collective-permute-start | bytes 589832 | tf_op jit(solution)/shard_map/ppermute | solution.py:287
  5.6 1.0 %keep.1 = (f32[2,64,384]{2,1,0:T(8,128)S(1)}, f32[64,384]{1,0:T(8,128)S(1)}, f32[64,384]{1,0:T(8,128)S(1)}) custom-call(bf16[2,384,512]{2,1,0:T(8,128)(2,1)S(1)} %get-tuple-element.22.spectrum, bf16[2,384,384]{2,1,0:T(8,128)(2,1)S(1)} %get-tuple-element.23.rt, bf16[2,512,384]{2,1,0:T(8,128)(2,1)S(1)} %get-tuple-element.24.ct, ...), custom_call_target="tpu_custom_call" | custom-call | flops 452984832 | tf_op jit(solution)/shard_map/keep/pallas_call | solution.py:358
  6.6 0.1 collective-permute-done.received
  6.7 3.0 %collective-permute-start.1 = (f32[64,384]{1,0:T(8,128)S(1)}, f32[64,384]{1,0:T(8,128)S(1)}, u32[]{:S(2)}, u32[]{:S(2)}) collective-permute-start(f32[64,384]{1,0:T(8,128)S(1)} %get-tuple-element.32), channel_id=1, source_target_pairs={{0,1},{1,0},{2,3},{3,2},{4,5},{5,4},{6,7},{7,6},{8,9},{9,8},{10,11... | collective-permute-start | bytes 294920 | tf_op jit(solution)/shard_map/ppermute | solution.py:370
  9.8 0.0 collective-permute-start.2
  9.8 0.5 %collective-permute-start.3 = (f32[64,384]{1,0:T(8,128)S(1)}, f32[64,384]{1,0:T(8,128)S(1)}, u32[]{:S(2)}, u32[]{:S(2)}) collective-permute-start(f32[64,384]{1,0:T(8,128)S(1)} %get-tuple-element.34), channel_id=1, source_target_pairs={{0,4},{4,0},{8,12},{12,8},{16,20},{20,16},{24,28},{28,24},{1,5},{5... | collective-permute-start | bytes 294920 | tf_op jit(solution)/shard_map/ppermute | solution.py:287
  10.3 2.6 %collective-permute-done.1.a = f32[64,384]{1,0:T(8,128)S(1)} collective-permute-done((f32[64,384]{1,0:T(8,128)S(1)}, f32[64,384]{1,0:T(8,128)S(1)}, u32[]{:S(2)}, u32[]{:S(2)}) %collective-permute-start.1) | collective-permute-done | bytes 98336 | tf_op jit(solution)/shard_map/ppermute | solution.py:370
  12.9 0.0 collective-permute-done.2.b
  12.9 0.0 collective-permute-done.3.own_received
  12.9 0.0 copy-start
  12.9 2.7 %collective-permute-start.6 = (f32[64,384]{1,0:T(8,128)S(1)}, f32[64,384]{1,0:T(8,128)S(1)}, u32[]{:S(2)}, u32[]{:S(2)}) collective-permute-start(f32[64,384]{1,0:T(8,128)S(1)} %sum_tiles.1.refs_0_), channel_id=1, source_target_pairs={{0,24},{4,28},{8,16},{12,20},{16,8},{20,12},{24,0},{28,4},{1,25},{... | collective-permute-start | bytes 294920 | tf_op jit(solution)/shard_map/ppermute | solution.py:287
  15.6 0.5 %collective-permute-start.5 = (f32[64,384]{1,0:T(8,128)S(1)}, f32[64,384]{1,0:T(8,128)S(1)}, u32[]{:S(2)}, u32[]{:S(2)}) collective-permute-start(f32[64,384]{1,0:T(8,128)S(1)} %sum_tiles.1.refs_0_), channel_id=1, source_target_pairs={{0,16},{4,20},{8,24},{12,28},{16,0},{20,4},{24,8},{28,12},{1,17},{... | collective-permute-start | bytes 294920 | tf_op jit(solution)/shard_map/ppermute | solution.py:287
  16.1 0.4 %collective-permute-start.4 = (f32[64,384]{1,0:T(8,128)S(1)}, f32[64,384]{1,0:T(8,128)S(1)}, u32[]{:S(2)}, u32[]{:S(2)}) collective-permute-start(f32[64,384]{1,0:T(8,128)S(1)} %sum_tiles.1.refs_0_), channel_id=1, source_target_pairs={{0,8},{4,12},{8,0},{12,4},{16,24},{20,28},{24,16},{28,20},{1,9},{5... | collective-permute-start | bytes 294920 | tf_op jit(solution)/shard_map/ppermute | solution.py:287
  16.5 2.2 %collective-permute-done.6.refs_3_ = f32[64,384]{1,0:T(8,128)S(1)} collective-permute-done((f32[64,384]{1,0:T(8,128)S(1)}, f32[64,384]{1,0:T(8,128)S(1)}, u32[]{:S(2)}, u32[]{:S(2)}) %collective-permute-start.6) | collective-permute-done | bytes 98336 | tf_op jit(solution)/shard_map/ppermute | solution.py:287
  18.6 1.7 %collective-permute-done.5.refs_2_ = f32[64,384]{1,0:T(8,128)S(1)} collective-permute-done((f32[64,384]{1,0:T(8,128)S(1)}, f32[64,384]{1,0:T(8,128)S(1)}, u32[]{:S(2)}, u32[]{:S(2)}) %collective-permute-start.5) | collective-permute-done | bytes 98336 | tf_op jit(solution)/shard_map/ppermute | solution.py:287
  20.4 0.3 %collective-permute-done.4.refs_1_ = f32[64,384]{1,0:T(8,128)S(1)} collective-permute-done((f32[64,384]{1,0:T(8,128)S(1)}, f32[64,384]{1,0:T(8,128)S(1)}, u32[]{:S(2)}, u32[]{:S(2)}) %collective-permute-start.4) | collective-permute-done | bytes 98336 | tf_op jit(solution)/shard_map/ppermute | solution.py:287
  20.7 2.8 %collective-permute-start.9 = (f32[64,384]{1,0:T(8,128)S(1)}, f32[64,384]{1,0:T(8,128)S(1)}, u32[]{:S(2)}, u32[]{:S(2)}) collective-permute-start(f32[64,384]{1,0:T(8,128)S(1)} %sum_chips.1.whole), channel_id=1, source_target_pairs={{0,1},{1,0},{2,3},{3,2},{4,5},{5,4},{6,7},{7,6},{8,9},{9,8},{10,11... | collective-permute-start | bytes 294920 | tf_op jit(solution)/shard_map/ppermute | solution.py:374
  23.5 0.0 collective-permute-start.8
  23.5 0.5 %collective-permute-start.7 = (f32[64,384]{1,0:T(8,128)S(1)}, f32[64,384]{1,0:T(8,128)S(1)}, u32[]{:S(2)}, u32[]{:S(2)}) collective-permute-start(f32[64,384]{1,0:T(8,128)S(1)} %sum_chips.1.whole), channel_id=1, source_target_pairs={{0,4},{4,0},{8,12},{12,8},{16,20},{20,16},{24,28},{28,24},{1,5},{5... | collective-permute-start | bytes 294920 | tf_op jit(solution)/shard_map/ppermute | solution.py:287
  24.0 2.1 %collective-permute-done.9.a = f32[64,384]{1,0:T(8,128)S(1)} collective-permute-done((f32[64,384]{1,0:T(8,128)S(1)}, f32[64,384]{1,0:T(8,128)S(1)}, u32[]{:S(2)}, u32[]{:S(2)}) %collective-permute-start.9) | collective-permute-done | bytes 98336 | tf_op jit(solution)/shard_map/ppermute | solution.py:374
  26.1 0.0 collective-permute-done.8.b
  26.1 0.0 collective-permute-done.7.whole_other
  26.1 0.1 collective-permute-start.10
  26.2 0.9 %near.1 = (f32[384,512]{1,0:T(8,128)S(1)}, bf16[2,384,128]{2,1,0:T(8,128)(2,1)S(1)}) custom-call(f32[4,64,384]{2,1,0:T(8,128)S(1)} %get-tuple-element.35.mine, bf16[2,384,384]{2,1,0:T(8,128)(2,1)S(1)} %get-tuple-element.37.rf, bf16[2,384,512]{2,1,0:T(8,128)(2,1)S(1)} %get-tuple-element.38.cf), custom_call_target="tpu_custom_call" | custom-call | flops 301989888 | tf_op jit(solution)/shard_map/near/pallas_call | solution.py:380
  27.2 0.5 %collective-permute-done.10.other = f32[2,64,384]{2,1,0:T(8,128)S(1)} collective-permute-done((f32[2,64,384]{2,1,0:T(8,128)S(1)}, f32[2,64,384]{2,1,0:T(8,128)S(1)}, u32[]{:S(2)}, u32[]{:S(2)}) %collective-permute-start.10) | collective-permute-done | bytes 196640 | tf_op jit(solution)/shard_map/ppermute | solution.py:287
  27.7 0.0 copy-done
  27.7 2.8 %back.1 = (f32[2,128,384]{2,1,0:T(8,128)}, f32[128,384]{1,0:T(8,128)}) custom-call(f32[2,128,384]{2,1,0:T(8,128)S(1)} %copy-done, f32[4,64,384]{2,1,0:T(8,128)S(1)} %get-tuple-element.35.mine, f32[2,64,384]{2,1,0:T(8,128)S(1)} %collective-permute-done.10.other, bf16[2,384,128]{2,1,0:T(8,128)(2,1)S(1)} %get-tuple-element.39.table, ...), custom_call_target="tpu_custom_call" | custom-call | tf_op jit(solution)/shard_map/back/pallas_call | solution.py:389
  (4 shorter events, 0.1 us)
Async XLA Ops:
  5.1 1.6 %collective-permute-start = (f32[2,64,384]{2,1,0:T(8,128)S(1)}, f32[2,64,384]{2,1,0:T(8,128)S(1)}, u32[]{:S(2)}, u32[]{:S(2)}) collective-permute-start(f32[2,64,384]{2,1,0:T(8,128)S(1)} %get-tuple-element.29), channel_id=1, source_target_pairs={{0,4},{4,0},{8,12},{12,8},{16,20},{20,16},{24,28},{28,24},{1,5},{5... | collective-permute-start | bytes 589832 | tf_op jit(solution)/shard_map/ppermute | solution.py:287
  6.7 6.1 %collective-permute-start.1 = (f32[64,384]{1,0:T(8,128)S(1)}, f32[64,384]{1,0:T(8,128)S(1)}, u32[]{:S(2)}, u32[]{:S(2)}) collective-permute-start(f32[64,384]{1,0:T(8,128)S(1)} %get-tuple-element.32), channel_id=1, source_target_pairs={{0,1},{1,0},{2,3},{3,2},{4,5},{5,4},{6,7},{7,6},{8,9},{9,8},{10,11... | collective-permute-start | bytes 294920 | tf_op jit(solution)/shard_map/ppermute | solution.py:370
  9.8 3.1 %collective-permute-start.2 = (f32[64,384]{1,0:T(8,128)S(1)}, f32[64,384]{1,0:T(8,128)S(1)}, u32[]{:S(2)}, u32[]{:S(2)}) collective-permute-start(f32[64,384]{1,0:T(8,128)S(1)} %get-tuple-element.33), channel_id=1, source_target_pairs={{0,4},{1,2},{2,1},{3,7},{4,0},{5,6},{6,5},{7,3},{8,12},{9,10},{10,... | collective-permute-start | bytes 294920 | tf_op jit(solution)/shard_map/ppermute | solution.py:370
  9.8 3.1 %collective-permute-start.3 = (f32[64,384]{1,0:T(8,128)S(1)}, f32[64,384]{1,0:T(8,128)S(1)}, u32[]{:S(2)}, u32[]{:S(2)}) collective-permute-start(f32[64,384]{1,0:T(8,128)S(1)} %get-tuple-element.34), channel_id=1, source_target_pairs={{0,4},{4,0},{8,12},{12,8},{16,20},{20,16},{24,28},{28,24},{1,5},{5... | collective-permute-start | bytes 294920 | tf_op jit(solution)/shard_map/ppermute | solution.py:287
  12.9 14.8 %copy-start = (f32[2,128,384]{2,1,0:T(8,128)S(1)}, f32[2,128,384]{2,1,0:T(8,128)}, u32[]{:S(2)}) copy-start(f32[2,128,384]{2,1,0:T(8,128)} %volume.1) | copy-start | bytes 1179652
  12.9 5.7 %collective-permute-start.6 = (f32[64,384]{1,0:T(8,128)S(1)}, f32[64,384]{1,0:T(8,128)S(1)}, u32[]{:S(2)}, u32[]{:S(2)}) collective-permute-start(f32[64,384]{1,0:T(8,128)S(1)} %sum_tiles.1.refs_0_), channel_id=1, source_target_pairs={{0,24},{4,28},{8,16},{12,20},{16,8},{20,12},{24,0},{28,4},{1,25},{... | collective-permute-start | bytes 294920 | tf_op jit(solution)/shard_map/ppermute | solution.py:287
  15.6 4.8 %collective-permute-start.5 = (f32[64,384]{1,0:T(8,128)S(1)}, f32[64,384]{1,0:T(8,128)S(1)}, u32[]{:S(2)}, u32[]{:S(2)}) collective-permute-start(f32[64,384]{1,0:T(8,128)S(1)} %sum_tiles.1.refs_0_), channel_id=1, source_target_pairs={{0,16},{4,20},{8,24},{12,28},{16,0},{20,4},{24,8},{28,12},{1,17},{... | collective-permute-start | bytes 294920 | tf_op jit(solution)/shard_map/ppermute | solution.py:287
  16.1 4.6 %collective-permute-start.4 = (f32[64,384]{1,0:T(8,128)S(1)}, f32[64,384]{1,0:T(8,128)S(1)}, u32[]{:S(2)}, u32[]{:S(2)}) collective-permute-start(f32[64,384]{1,0:T(8,128)S(1)} %sum_tiles.1.refs_0_), channel_id=1, source_target_pairs={{0,8},{4,12},{8,0},{12,4},{16,24},{20,28},{24,16},{28,20},{1,9},{5... | collective-permute-start | bytes 294920 | tf_op jit(solution)/shard_map/ppermute | solution.py:287
  20.7 5.4 %collective-permute-start.9 = (f32[64,384]{1,0:T(8,128)S(1)}, f32[64,384]{1,0:T(8,128)S(1)}, u32[]{:S(2)}, u32[]{:S(2)}) collective-permute-start(f32[64,384]{1,0:T(8,128)S(1)} %sum_chips.1.whole), channel_id=1, source_target_pairs={{0,1},{1,0},{2,3},{3,2},{4,5},{5,4},{6,7},{7,6},{8,9},{9,8},{10,11... | collective-permute-start | bytes 294920 | tf_op jit(solution)/shard_map/ppermute | solution.py:374
  23.5 2.6 %collective-permute-start.8 = (f32[64,384]{1,0:T(8,128)S(1)}, f32[64,384]{1,0:T(8,128)S(1)}, u32[]{:S(2)}, u32[]{:S(2)}) collective-permute-start(f32[64,384]{1,0:T(8,128)S(1)} %sum_chips.1.whole), channel_id=1, source_target_pairs={{0,4},{1,2},{2,1},{3,7},{4,0},{5,6},{6,5},{7,3},{8,12},{9,10},{10,... | collective-permute-start | bytes 294920 | tf_op jit(solution)/shard_map/ppermute | solution.py:374
  23.5 2.6 %collective-permute-start.7 = (f32[64,384]{1,0:T(8,128)S(1)}, f32[64,384]{1,0:T(8,128)S(1)}, u32[]{:S(2)}, u32[]{:S(2)}) collective-permute-start(f32[64,384]{1,0:T(8,128)S(1)} %sum_chips.1.whole), channel_id=1, source_target_pairs={{0,4},{4,0},{8,12},{12,8},{16,20},{20,16},{24,28},{28,24},{1,5},{5... | collective-permute-start | bytes 294920 | tf_op jit(solution)/shard_map/ppermute | solution.py:287
  26.1 1.5 %collective-permute-start.10 = (f32[2,64,384]{2,1,0:T(8,128)S(1)}, f32[2,64,384]{2,1,0:T(8,128)S(1)}, u32[]{:S(2)}, u32[]{:S(2)}) collective-permute-start(f32[2,64,384]{2,1,0:T(8,128)S(1)} %get-tuple-element.36), channel_id=1, source_target_pairs={{0,4},{4,0},{8,12},{12,8},{16,20},{20,16},{24,28},{28,24},{1,5},{5... | collective-permute-start | bytes 589832 | tf_op jit(solution)/shard_map/ppermute | solution.py:287
